TPU v7x, 128 devices: a whole 4x4x4 slice. The times are simulated.
128 devices in a mesh: dp: 2 (over core), ctx: 64 (over x, z, y).
Axes of the slice: x: 4, y: 4, z: 4, core: 2. Of those that a mesh axis runs over, the one named last changes fastest.
Arguments:
- text_values: bfloat16 [32768, 4096], P(('dp', 'ctx')), parts along dimension 0, may hold values from -6 to 6
- text_gate: bfloat16 [32768, 4096], P(('dp', 'ctx')), parts along dimension 0, may hold values from -6 to 6
- text_proj: bfloat16 [32768, 1024], P(('dp', 'ctx')), parts along dimension 0, may hold values from -6 to 6
- text_step: bfloat16 [32768, 64], P(('dp', 'ctx')), parts along dimension 0
- tile_values: bfloat16 [8192, 4096], P(('dp', 'ctx')), parts along dimension 0, may hold values from -6 to 6
- tile_gate: bfloat16 [8192, 4096], P(('dp', 'ctx')), parts along dimension 0, may hold values from -6 to 6
- tile_proj: bfloat16 [8192, 1024], P(('dp', 'ctx')), parts along dimension 0, may hold values from -6 to 6
- tile_step: bfloat16 [8192, 64], P(('dp', 'ctx')), parts along dimension 0
- tile_position: int32 [8192], P('dp'), parts along dimension 0, may hold values from 0 to 16383, as said below
- tile_count: int32 [128], P('dp'), parts along dimension 0, may hold values from 32 to 64
- conv_weight: float32 [4, 5120], replicated, may hold values from -3 to 3
- conv_bias: float32 [5120], replicated, may hold values from -3 to 3
- step_bias: float32 [64], replicated, may hold values from -0.5 to 0.5
- decay_log: float32 [64], replicated
- skip_gain: float32 [64], replicated, may hold values from 0.5 to 1.5
- norm_gain: float32 [4096], replicated, may hold values from 0.5 to 1.5
Outputs:
- mixer_out: bfloat16 [32768, 4096], P(('dp', 'ctx')), parts along dimension 0
There are 2 independent parts, one for each index of `dp`. A program takes and returns all parts, laid end to end along the dimension named above; an argument that names none is the same for every part. Nothing has to cross between parts.
Inputs may be any that keep to these rules, and one draw needn't show every extreme that they name: `tile_position`: positions of the tile rows are distinct over all rows. The 64 rows of one encoder device go in order, 2 at a time, to 32 different devices, so at most 2 rows of one encoder device land on one device's 256 positions; the rows that land on one device fill one run of consecutive positions, ordered by source device.
All inputs are finite; a program needn't handle non-finite values.
Results may differ from a plain program's by a relative error of at most 0.0095.
Values may be sent and summed in bfloat16 or wider, within the bound.
No kernel may reach another device: no remote copies, remote signals or barrier semaphores. Data moves between devices by JAX's collectives and lax.ppermute only.
A program may use at most 320 MiB of HBM per device.

v0:
```python
import jax
import jax.numpy as jnp
from jax import lax
from jax.sharding import PartitionSpec as P

H = 64
P_SIZE = 64
N = 64
G = 8
SPAN = 128
KCONV = 4
CAP = 2
E = 4096


highest = lax.Precision.HIGHEST


def passed_along(value, axis, steps):
    count = lax.axis_size(axis)
    leading, last = (max(0, -steps), min(count, count - steps))
    return lax.ppermute(value, axis, [(source, source + steps) for source in range(leading, last)])


def entering(part, axis, combine, identity):
    place = lax.axis_index(axis)
    gathered = jax.tree.map(lambda a: lax.all_gather(a, axis), part)
    state = jax.tree.map(lambda a, e: jnp.zeros_like(a) + jnp.asarray(e, a.dtype), part, identity)

    def one(hop, state):
        return combine(
            state, jax.tree.map(lambda a: lax.dynamic_index_in_dim(a, hop, 0, False), gathered)
        )

    return lax.fori_loop(0, place, one, state)


def causal_conv(row_data, lead_rows, weights, bias_row):
    extended = jnp.concatenate([lead_rows, row_data], axis=0).astype(jnp.float32)
    length = row_data.shape[0]
    running_sum = jnp.zeros((length, row_data.shape[1]), jnp.float32) + bias_row[None, :]
    for offset in range(KCONV):
        running_sum = running_sum + weights[offset][None, :] * extended[offset : offset + length]
    return jax.nn.silu(running_sum).astype(jnp.bfloat16)


def gated_norm(mixed, gate_rows, gain_row):
    gated = mixed * jax.nn.silu(gate_rows.astype(jnp.float32))
    length = gated.shape[0]
    grouped = gated.reshape(length, G, E // G)
    scale = lax.rsqrt(jnp.mean(grouped * grouped, axis=-1, keepdims=True) + 1e-05)
    return ((grouped * scale).reshape(length, E) * gain_row[None, :]).astype(jnp.bfloat16)


def combine_states(earlier, later_pair):
    earlier_decay, earlier_state = earlier
    later_decay, later_state = later_pair
    return (earlier_decay * later_decay, later_decay[:, None, None] * earlier_state + later_state)


def shards(
    text_values,
    text_gate,
    text_proj,
    text_step,
    tile_values,
    tile_gate,
    tile_proj,
    tile_step,
    tile_position,
    tile_count,
    conv_weight,
    conv_bias,
    step_bias,
    decay_log,
    skip_gain,
    norm_gain,
):
    tok_dev = text_values.shape[0]
    tile_dev = tile_values.shape[0]
    devices = lax.axis_size("ctx")
    device = lax.axis_index("ctx")
    slot_count = devices * CAP
    position_grid = tile_position.reshape(devices, tile_dev)
    row_ids = jnp.arange(tile_dev, dtype=jnp.int32)
    real_rows = row_ids[None, :] < tile_count[:, None]
    target_dev = position_grid // tok_dev
    target_row = position_grid % tok_dev
    earlier_same = (target_dev[:, :, None] == target_dev[:, None, :]) & (
        row_ids[None, None, :] < row_ids[None, :, None]
    )
    rank_in = jnp.sum(earlier_same.astype(jnp.int32), axis=2)
    own_slots = lax.dynamic_index_in_dim(target_dev * CAP + rank_in, device, 0, keepdims=False)
    own_real = lax.dynamic_index_in_dim(real_rows, device, 0, keepdims=False)
    send_map = ((jnp.arange(slot_count)[:, None] == own_slots[None, :]) & own_real[None, :]).astype(
        jnp.bfloat16
    )

    def pack_rows(row_data):
        return jnp.dot(send_map, row_data, preferred_element_type=jnp.float32).astype(jnp.bfloat16)

    arrived = (
        lax.all_to_all(pack_rows(tile_values), "ctx", split_axis=0, concat_axis=0, tiled=True),
        lax.all_to_all(pack_rows(tile_gate), "ctx", split_axis=0, concat_axis=0, tiled=True),
        lax.all_to_all(pack_rows(tile_proj), "ctx", split_axis=0, concat_axis=0, tiled=True),
        lax.all_to_all(pack_rows(tile_step), "ctx", split_axis=0, concat_axis=0, tiled=True),
    )
    landing = real_rows & (target_dev == device)
    incoming_slot = jnp.arange(devices, dtype=jnp.int32)[:, None] * CAP + rank_in
    row_match = (jnp.arange(tok_dev)[:, None] == target_row.reshape(1, -1)) & landing.reshape(1, -1)
    slot_match = incoming_slot.reshape(-1, 1) == jnp.arange(slot_count)[None, :]
    placement = jnp.dot(
        row_match.astype(jnp.bfloat16),
        slot_match.astype(jnp.bfloat16),
        preferred_element_type=jnp.float32,
    ).astype(jnp.bfloat16)
    from_tile = jnp.any(row_match, axis=1)[:, None]

    def place_rows(received, text_rows):
        placed = jnp.dot(placement, received, preferred_element_type=jnp.float32).astype(
            jnp.bfloat16
        )
        return jnp.where(from_tile, placed, text_rows)

    values_in = place_rows(arrived[0], text_values)
    gate_in = place_rows(arrived[1], text_gate)
    proj_in = place_rows(arrived[2], text_proj)
    step_in = place_rows(arrived[3], text_step)
    rim_values, rim_proj = passed_along(
        (values_in[tok_dev - KCONV + 1 :], proj_in[tok_dev - KCONV + 1 :]), "ctx", 1
    )
    values_conv = causal_conv(values_in, rim_values, conv_weight[:, :E], conv_bias[:E])
    proj_conv = causal_conv(proj_in, rim_proj, conv_weight[:, E:], conv_bias[E:])
    step_size = jax.nn.softplus(step_in.astype(jnp.float32) + step_bias[None, :])
    log_decay = step_size * (-jnp.exp(decay_log))[None, :]
    blocks = tok_dev // SPAN
    values_f = values_conv.reshape(blocks, SPAN, H, P_SIZE).astype(jnp.float32)
    input_bf = proj_conv[:, : G * N].reshape(blocks, SPAN, G, N)
    output_bf = proj_conv[:, G * N :].reshape(blocks, SPAN, G, N)
    input_groups = input_bf.astype(jnp.float32)
    output_groups = output_bf.astype(jnp.float32)
    cum_decay = jnp.cumsum(log_decay.reshape(blocks, SPAN, H), axis=1)
    weighted = values_f * step_size.reshape(blocks, SPAN, H)[:, :, :, None]
    input_heads = jnp.repeat(input_groups, H // G, axis=2)
    output_heads = jnp.repeat(output_groups, H // G, axis=2)
    causal = jnp.arange(SPAN)[:, None] >= jnp.arange(SPAN)[None, :]
    group_scores = jnp.einsum(
        "cign,cjgn->cgij", output_bf, input_bf, preferred_element_type=jnp.float32
    )
    scores = jnp.repeat(group_scores, H // G, axis=1)
    cum_heads = jnp.swapaxes(cum_decay, 1, 2)
    differ = cum_heads[:, :, :, None] - cum_heads[:, :, None, :]
    kernel = jnp.where(causal[None, None], jnp.exp(jnp.where(causal[None, None], differ, 0.0)), 0.0)
    diagonal = jnp.einsum("chij,cjhp->cihp", kernel * scores, weighted, precision=highest)
    tail_weight = jnp.exp(cum_decay[:, -1:, :] - cum_decay)
    states = jnp.einsum(
        "cjhn,cjhp->chnp", input_heads * tail_weight[:, :, :, None], weighted, precision=highest
    )
    decays = jnp.exp(cum_decay[:, -1, :])

    def accumulate(running, current):
        return (combine_states(running, current), running)

    start_pair = (jnp.ones((H,), jnp.float32), jnp.zeros((H, N, P_SIZE), jnp.float32))
    totals, entries = lax.scan(accumulate, start_pair, (decays, states))
    identity = (jnp.ones((H,), jnp.float32), jnp.zeros((H, N, P_SIZE), jnp.float32))
    scanned = entering(totals, "ctx", combine_states, identity)
    carried = scanned[1]
    entry_state = entries[1] + entries[0][:, :, None, None] * carried[None]
    offdiag = (
        jnp.einsum("cihn,chnp->cihp", output_heads, entry_state, precision=highest)
        * jnp.exp(cum_decay)[:, :, :, None]
    )
    mixed = diagonal + offdiag + skip_gain[None, None, :, None] * values_f
    return gated_norm(mixed.reshape(tok_dev, E), gate_in, norm_gain)


def solution(mesh):
    placed = (
        P(("dp", "ctx"), None),
        P(("dp", "ctx"), None),
        P(("dp", "ctx"), None),
        P(("dp", "ctx"), None),
        P(("dp", "ctx"), None),
        P(("dp", "ctx"), None),
        P(("dp", "ctx"), None),
        P(("dp", "ctx"), None),
        P("dp"),
        P("dp"),
        P(),
        P(),
        P(),
        P(),
        P(),
        P(),
    )
    return jax.shard_map(
        shards, mesh=mesh, in_specs=placed, out_specs=P(("dp", "ctx"), None), check_vma=False
    )
```

profile of v0, /device:TPU:126, one launch (start us, length us, event | category | flops | bytes accessed | tf_op | source)
XLA Modules:
  0.0 843.5 jit_solution(268119496220451089)
XLA Ops:
  11.7 10.0 %all-to-all-start.1 = ((bf16[64,2,64]{2,1,0:T(2,128)(2,1)}), bf16[64,2,64]{2,1,0:T(2,128)(2,1)S(1)}, u32[]{:S(2)}, u32[]{:S(2)}) async-start(bf16[64,2,64]{2,1,0:T(2,128)(2,1)} %bitcast.8), calls=%async_computation.1 | async-start | bytes 65536 | tf_op jit(solution)/shard_map/all_to_all | solution.py:106
  30.0 10.5 %all-to-all-start.2 = ((bf16[64,2,1024]{2,1,0:T(2,128)(2,1)}), bf16[64,2,1024]{2,1,0:T(2,128)(2,1)S(1)}, u32[]{:S(2)}, u32[]{:S(2)}) async-start(bf16[64,2,1024]{2,1,0:T(2,128)(2,1)} %all_to_all.38), calls=%async_computation.2 | async-start | bytes 524288 | tf_op jit(solution)/shard_map/all_to_all | solution.py:105
  41.4 2.5 all_to_all.32
  45.8 10.5 %all-to-all-start = ((bf16[64,2,4096]{2,1,0:T(2,128)(2,1)}), bf16[64,2,4096]{2,1,0:T(2,128)(2,1)}, u32[]{:S(2)}, u32[]{:S(2)}) async-start(bf16[64,2,4096]{2,1,0:T(2,128)(2,1)} %all_to_all.32), calls=%async_computation | async-start | bytes 2097152 | tf_op jit(solution)/shard_map/all_to_all | solution.py:103
  62.3 3.2 collective-permute-done.1
  67.9 2.2 all_to_all.34
  70.1 2.6 fusion.9
  76.6 4.2 collective-permute-done
  80.8 2.2 maximum_convert_fusion
  83.0 4.8 fusion.43
  87.8 5.7 copy.108
  93.5 5.8 reshape.224
  99.3 4.4 broadcast_multiply_fusion
  104.6 8.4 fusion.24
  113.0 9.3 %while.30 = (s32[]{:T(128)}, f32[64]{0:T(128)}, f32[64,64,64]{2,1,0:T(8,128)S(1)}, f32[2,64]{1,0:T(2,128)}, f32[2,64,64,64]{3,2,1,0:T(8,128)}, /*index=5*/f32[2,...) while((s32[]{:T(128)}, f32[64]{0:T(128)}, f32[64,64,64]{2,1,0:T(8,128)S(1)}, ...), condition=%wide.region_4.5_spmd.clone, body=%wide.region_3.4_spmd.clone.sunk | while | flops 1048707 | bytes 14682769 | solution.py:165
  125.6 24.2 %all-to-all-start.3 = ((bf16[64,2,4096]{2,1,0:T(2,128)(2,1)}), bf16[64,2,4096]{2,1,0:T(2,128)(2,1)S(1)}, u32[]{:S(2)}, u32[]{:S(2)}) async-start(bf16[64,2,4096]{2,1,0:T(2,128)(2,1)} %all_to_all.41), calls=%async_computation.3 | async-start | bytes 2097152 | tf_op jit(solution)/shard_map/all_to_all | solution.py:104
  152.6 20.4 %all-to-all-done.3 = bf16[64,2,4096]{2,1,0:T(2,128)(2,1)S(1)} async-done(((bf16[64,2,4096]{2,1,0:T(2,128)(2,1)}), bf16[64,2,4096]{2,1,0:T(2,128)(2,1)S(1)}, u32[]{:S(2)}, u32[]{:S(2)}) %all-to-all-start.3) | async-done | bytes 1048608 | tf_op jit(solution)/shard_map/all_to_all | solution.py:104
  175.0 347.1 %all-reduce = f32[4096]{0:T(1024)S(1)} all-reduce(f32[4096]{0:T(1024)S(1)} %dynamic-update-slice), channel_id=2, replica_groups=mesh['dp'=2,'ctx'=64] {'ctx'}, use_global_device_ids=true, to_apply=%add | all-reduce | flops 4096 | bytes 32768
  524.4 18.0 %fusion.3 = f32[2,64,64,128]{3,2,1,0:T(8,128)} fusion(f32[2,64,128,128]{3,2,1,0:T(8,128)S(1)} %bitcast.78, f32[2,64,128]{2,1,0:T(8,128)S(1)} %copy-done.10, pred[128,128]{1,0:T(8,128)(4,1)S(1)} %iota_compare_fusion.5, f32[2,128,64,64]{1,0,3,2:T(2,128)S(1)} %copy-done.6), kind=kOutput, calls=%fused_computation.9 | convolution fusion | flops 1619001344 | bytes 16859136 | tf_op jit(solution)/shard_map/chij,cjhp->cihp/dot_general | solution.py:154
  542.4 113.3 %all-gather.4.cloned.1.call-done = f32[4096,64,64]{2,1,0:T(8,128)} async-done(((f32[64,64,64]{2,1,0:T(8,128)}), f32[4096,64,64]{2,1,0:T(8,128)}) %all-gather.4.cloned.1.call-update) | async-done | bytes 67108880 | tf_op jit(solution)/shard_map/all_gather | solution.py:27
  655.9 127.6 %while.29 = (s32[]{:T(128)}, f32[64,64,64]{2,1,0:T(8,128)S(1)}, s32[]{:T(128)}, f32[64,64]{1,0:T(8,128)S(1)}, f32[64,64,64,64]{3,2,1,0:T(8,128)}, /*index=5*/s32[]{:T(128)}, s32[]{:T(128)}, s32[]{:T(128)}) while((s32[]{:T(128)}, f32[64,64,64]{2,1,0:T(8,128)S(1)}, s32[]{:T(128)}, f32[64,64]{1,0:T(8,128)S(1)}, f32[64,64,64,64]{3,2,1,0:T(8,128)}, ...), condition=%wide.region_6.7_spmd, body=%wide.region_5.6_spmd.sunk | while | flops 524293 | bytes 3146623 | solution.py:35
  658.0 2.0 bitcast_add_fusion.4
  662.0 2.0 bitcast_add_fusion.4
  666.1 2.0 bitcast_add_fusion.4
  670.1 2.0 bitcast_add_fusion.4
  674.2 2.0 bitcast_add_fusion.4
  678.2 2.0 bitcast_add_fusion.4
  680.3 2.0 bitcast_add_fusion.4
  684.3 2.0 bitcast_add_fusion.4
  688.4 2.0 bitcast_add_fusion.4
  692.4 2.0 bitcast_add_fusion.4
  696.5 2.0 bitcast_add_fusion.4
  700.5 2.0 bitcast_add_fusion.4
  704.6 2.0 bitcast_add_fusion.4
  708.6 2.0 bitcast_add_fusion.4
  712.7 2.0 bitcast_add_fusion.4
  716.7 2.0 bitcast_add_fusion.4
  718.7 2.0 bitcast_add_fusion.4
  722.8 2.0 bitcast_add_fusion.4
  726.9 2.0 bitcast_add_fusion.4
  785.7 11.8 %fusion.20 = f32[2,128,64,64]{1,3,2,0:T(8,128)} fusion(f32[2,64,64,128]{3,2,1,0:T(8,128)} %fusion.3, f32[2,128,64,64]{1,0,3,2:T(2,128)S(1)} %copy-done.4, f32[64]{0:T(128)S(1)} %copy-done.25, f32[2,128,64]{1,2,0:T(8,128)S(1)} %copy.123, f32[2,128,64,64]{1,3,2,0:T(8,128)S(1)} %bitcast.79, f32[2,64,64,64]{3,2,1,0:T(8,128)} %get-tuple-element.89, ...), kind=kOutput, calls=%fused_computation.37 | convolution fusion | flops 810549248 | bytes 19989248 | tf_op jit(solution)/shard_map/cihn,chnp->cihp/dot_general | solution.py:171
  797.5 9.2 %copy.131 = f32[2,128,64,64]{3,2,1,0:T(8,128)} copy(f32[2,128,64,64]{1,3,2,0:T(8,128)} %fusion.20) | data formatting | bytes 8388608 | tf_op jit(solution)/shard_map/reshape | solution.py:175
  806.7 8.2 reshape.232
  815.0 6.5 fusion.86
  821.4 5.8 copy.133
  827.2 2.5 reduce_sum.19
  830.3 3.9 copy.134
  834.2 2.1 multiply_convert_fusion
  (253 shorter events, 138.5 us)
Async XLA Ops:
  6.5 18.6 %copy-start = (bf16[64,4096]{1,0:T(8,128)(2,1)S(1)}, bf16[64,4096]{1,0:T(8,128)(2,1)}, u32[]{:S(2)}) copy-start(bf16[64,4096]{1,0:T(8,128)(2,1)} %param.24) | copy-start | bytes 1572868
  10.1 31.3 %copy-start.19 = (s32[64]{0:T(128)}, s32[64]{0:T(128)S(1)}, u32[]{:S(2)}) copy-start(s32[64]{0:T(128)S(1)} %fusion.79) | copy-start | bytes 772
  10.1 31.3 %copy-start.23 = (pred[64]{0:T(512)(128)(4,1)}, pred[64]{0:T(512)(128)(4,1)S(1)}, u32[]{:S(2)}) copy-start(pred[64]{0:T(512)(128)(4,1)S(1)} %dynamic-slice_bitcast_fusion.1) | copy-start | bytes 196
  11.7 18.2 %all-to-all-start.1 = ((bf16[64,2,64]{2,1,0:T(2,128)(2,1)}), bf16[64,2,64]{2,1,0:T(2,128)(2,1)S(1)}, u32[]{:S(2)}, u32[]{:S(2)}) async-start(bf16[64,2,64]{2,1,0:T(2,128)(2,1)} %bitcast.8), calls=%async_computation.1 | async-start | bytes 65536 | tf_op jit(solution)/shard_map/all_to_all | solution.py:106
  30.0 26.4 %copy-start.26 = (bf16[256,64]{0,1:T(8,128)(2,1)S(1)}, bf16[256,64]{0,1:T(8,128)(2,1)}, u32[]{:S(2)}) copy-start(bf16[256,64]{0,1:T(8,128)(2,1)} %param.23) | copy-start | bytes 98308
  30.0 26.4 %copy-start.27 = (f32[64]{0:T(128)S(1)}, f32[64]{0:T(128)}, u32[]{:S(2)}) copy-start(f32[64]{0:T(128)} %param.32) | copy-start | bytes 772
  30.0 15.9 %all-to-all-start.2 = ((bf16[64,2,1024]{2,1,0:T(2,128)(2,1)}), bf16[64,2,1024]{2,1,0:T(2,128)(2,1)S(1)}, u32[]{:S(2)}, u32[]{:S(2)}) async-start(bf16[64,2,1024]{2,1,0:T(2,128)(2,1)} %all_to_all.38), calls=%async_computation.2 | async-start | bytes 524288 | tf_op jit(solution)/shard_map/all_to_all | solution.py:105
  41.3 28.8 %copy-start.21 = (pred[256]{0:T(512)(128)(4,1)}, pred[256]{0:T(512)(128)(4,1)S(1)}, u32[]{:S(2)}) copy-start(pred[256]{0:T(512)(128)(4,1)S(1)} %fusion.32) | copy-start | bytes 772
  45.2 24.9 %copy-start.13 = (bf16[256,128]{1,0:T(8,128)(2,1)}, bf16[256,128]{1,0:T(8,128)(2,1)S(1)}, u32[]{:S(2)}) copy-start(bf16[256,128]{1,0:T(8,128)(2,1)S(1)} %fusion.45) | copy-start | bytes 196612
  45.3 20.4 %slice-start.1 = ((f32[5120]{0:T(1024)}), f32[1024]{0:T(1024)S(1)}, s32[]{:S(2)}) async-start(f32[5120]{0:T(1024)} %param.31), calls=%async_computation.6 | async-start | bytes 8192 | tf_op jit(solution)/shard_map/slice | solution.py:133
  45.8 22.0 %all-to-all-start = ((bf16[64,2,4096]{2,1,0:T(2,128)(2,1)}), bf16[64,2,4096]{2,1,0:T(2,128)(2,1)}, u32[]{:S(2)}, u32[]{:S(2)}) async-start(bf16[64,2,4096]{2,1,0:T(2,128)(2,1)} %all_to_all.32), calls=%async_computation | async-start | bytes 2097152 | tf_op jit(solution)/shard_map/all_to_all | solution.py:103
  56.3 599.3 %all-gather.4.cloned.1.call-start = ((), (), s32[]{:S(2)}) async-start(), calls=%async_computation.4 | async-start | bytes 136314880 | tf_op jit(solution)/shard_map/all_gather | solution.py:27
  58.4 7.2 collective-permute-start.1
  72.7 1.3 copy-start.7
  74.7 6.1 collective-permute-start
  76.3 6.7 slice-start
  93.5 5.8 copy-start.16
  103.7 9.3 %copy-start.5 = (f32[2,128,64,64]{1,0,3,2:T(2,128)}, f32[2,128,64,64]{1,0,3,2:T(2,128)S(1)}, u32[]{:S(2)}) copy-start(f32[2,128,64,64]{1,0,3,2:T(2,128)S(1)} %broadcast_multiply_fusion) | copy-start | bytes 12582916
  103.7 0.9 copy-start.15
  104.6 8.4 copy-start.18
  104.6 19.0 %copy-start.12 = (bf16[64,4096]{1,0:T(8,128)(2,1)S(1)}, bf16[64,4096]{1,0:T(8,128)(2,1)}, u32[]{:S(2)}) copy-start(bf16[64,4096]{1,0:T(8,128)(2,1)} %param.25) | copy-start | bytes 1572868
  113.0 10.6 %copy-start.20 = (s32[64]{0:T(128)S(1)}, s32[64]{0:T(128)}, u32[]{:S(2)}) copy-start(s32[64]{0:T(128)} %copy-done.19) | copy-start | bytes 772
  113.0 10.6 %copy-start.24 = (pred[64]{0:T(512)(128)(4,1)S(1)}, pred[64]{0:T(512)(128)(4,1)}, u32[]{:S(2)}) copy-start(pred[64]{0:T(512)(128)(4,1)} %copy-done.23) | copy-start | bytes 196
  113.0 2.9 copy-start.3
  117.7 2.9 copy-start.3
  122.3 1.3 copy-start.2
  122.3 27.5 %copy-start.28 = (u32[128]{0:T(128)S(1)}, u32[128]{0:T(128)}, u32[]{:S(2)}) copy-start(u32[128]{0:T(128)} %constant.103) | copy-start | bytes 1540
  122.3 29.6 %copy-start.11 = (f32[2,128,64]{2,1,0:T(8,128)S(1)}, f32[2,128,64]{2,1,0:T(8,128)}, u32[]{:S(2)}) copy-start(f32[2,128,64]{2,1,0:T(8,128)} %get-tuple-element.148) | copy-start | bytes 196612
  125.6 47.3 %all-to-all-start.3 = ((bf16[64,2,4096]{2,1,0:T(2,128)(2,1)}), bf16[64,2,4096]{2,1,0:T(2,128)(2,1)S(1)}, u32[]{:S(2)}, u32[]{:S(2)}) async-start(bf16[64,2,4096]{2,1,0:T(2,128)(2,1)} %all_to_all.41), calls=%async_computation.3 | async-start | bytes 2097152 | tf_op jit(solution)/shard_map/all_to_all | solution.py:104
  522.2 2.2 copy-start.6
  522.2 2.2 copy-start.10
  783.5 2.2 copy-start.4
  783.6 2.2 copy-start.25
  806.7 8.2 copy-start.9
  806.7 8.2 copy-start.14
  806.7 8.3 copy-start.22
  830.3 3.9 copy-start.8
  830.3 3.9 copy-start.17
  834.2 2.1 copy-start.1
Sparse Core Ops, SparseCore 0:
  123.8 531.8 all-gather.3
where the time goes:
time: 854 us; the launch traced here: 844 us
  blocking collectives  347 us (41%)
  other arithmetic  154 us (18%)
  waiting for transfers between devices  143 us (17%)
  local copies, waits for them, and re-layouts  69.8 us (8%)
  starting transfers between devices  58 us (7%)
  matrix products  54.2 us (6%)
  between operations  15.1 us (2%)
    unnamed x1, blocking collectives  347 us
    add x65, other arithmetic, combine_states(): later_decay[:, None, None] * earlier_state + later_state  125 us
    all_gather x1, waiting for transfers between devices, entering(): gathered = jax.tree.map(lambda a: lax.all_gather(a, axis), part)  113 us
    all_to_all x1, starting transfers between devices, shards(): lax.all_to_all(pack_rows(tile_gate), 'ctx', split_axis=0, concat_axis=0,...  24.2 us
    all_to_all x1, waiting for transfers between devices, shards(): lax.all_to_all(pack_rows(tile_gate), 'ctx', split_axis=0, concat_axis=0,...  20.4 us
    dot_general x1, matrix products, shards(): jnp.einsum('chij,cjhp->cihp', kernel * scores, weighted, precision=highest)  18 us
    reshape x2, local copies, waits for them, and re-layouts, shards(): return gated_norm(mixed.reshape(tok_dev, E), gate_in, norm_gain)  17.4 us
  transfers between devices with their start and end apart: 7, of which 6 were waited for; matrix products, arithmetic and copies ran while one was open for 4% of the time, Pallas kernels for 0%

commit v1 on v0

v1 whole, which is shorter than its diff:
```python
import functools

import jax
import jax.numpy as jnp
from jax import lax
from jax.experimental import pallas as pl
from jax.experimental.pallas import tpu as pltpu
from jax.sharding import PartitionSpec as P

H = 64
P_SIZE = 64
N = 64
G = 8
SPAN = 128
KCONV = 4
E = 4096
TOK = 256
TILE = 64
DEVS = 64
GW = E // G
PW = 2 * G * N
EDGE = 16
LANES = 128
QUART = 4
V_AT, G_AT, P_AT, S_AT = 0, 1024, 2048, 2304
CHUNK = 2432
STATE_W = GW + LANES

f32 = jnp.float32
bf16 = jnp.bfloat16
MIB = 1024 * 1024
VMEM_MIB = 32


def cost(flops, size, trans=0):
    return pl.CostEstimate(flops=flops, bytes_accessed=size, transcendentals=trans)


def whole(shape):
    return pl.BlockSpec(shape, lambda *_: (0,) * len(shape))


def group_cols(g):
    return pl.ds(pl.multiple_of(g * GW, GW), GW)


def iota(shape, dim):
    return lax.broadcasted_iota(jnp.int32, shape, dim)


def dot(a, b):
    return jnp.dot(a, b, preferred_element_type=f32)


def dot_rows(a, b):
    return lax.dot_general(a, b, (((0,), (0,)), ((), ())), preferred_element_type=f32)


def dot_cols(a, b):
    return lax.dot_general(a, b, (((1,), (1,)), ((), ())), preferred_element_type=f32)


def dot_whole(a, b):
    high = b.astype(bf16)
    low = (b - high.astype(f32)).astype(bf16)
    return dot(jnp.concatenate([a, a], axis=1), jnp.concatenate([high, low], axis=0))


def silu(x):
    half = 0.5 * x
    return half + half * jnp.tanh(half)


def split2(x):
    high = x.astype(bf16)
    low = (x - high.astype(f32)).astype(bf16)
    return jnp.where(iota(x.shape, 1) < H, high.astype(f32), low.astype(f32)).astype(bf16)


def expander(group):
    head = iota((LANES, GW), 0) & (H - 1)
    col = group * (H // G) + (iota((LANES, GW), 1) >> 6)
    return jnp.where(head == col, 1.0, 0.0).astype(bf16)


def pack_kernel(
    dev_ref, pos_ref, step_ref, val_hbm, gate_hbm, proj_hbm, out_hbm,
    val_ref, gate_ref, proj_ref, out_ref, in_sem, out_sem,
):
    loads = [
        pltpu.make_async_copy(src, dst, in_sem.at[i])
        for i, (src, dst) in enumerate(((val_hbm, val_ref), (gate_hbm, gate_ref), (proj_hbm, proj_ref)))
    ]
    for load in loads:
        load.start()
    dev = dev_ref[0]
    row = pos_ref[pl.ds(dev // 2, 1), :]
    other = pltpu.roll(row, 64, 1)
    lane = iota((1, LANES), 1)
    own = jnp.where((lane >> 6) == lax.rem(dev, 2), row, other)
    key = (own >> 8) * 8 + (lane & 1) * QUART + (lane >> 6)
    keys = jnp.concatenate([key, key + 2], axis=1)
    pick = jnp.where(iota((DEVS * 8, 2 * LANES), 0) == keys, 1.0, 0.0).astype(bf16)
    step = step_ref[...]
    out_ref[:, S_AT:] = dot(pick[:, :TILE], jnp.concatenate([step, step], axis=1)).astype(bf16)
    stores = []
    for i, (ref, at, width, part) in enumerate(
        ((val_ref, V_AT, 1024, 512), (gate_ref, G_AT, 1024, 512), (proj_ref, P_AT, 256, 256))
    ):
        loads[i].wait()
        for low in range(0, width, part):
            rows = [ref[:, b * width + low : b * width + low + part] for b in range(QUART)]
            out_ref[:, at + low : at + low + part] = dot(pick, jnp.concatenate(rows, axis=0)).astype(bf16)
            end = at + low + part if i < 2 else CHUNK
            cols = slice(at + low, end)
            store = pltpu.make_async_copy(out_ref.at[:, cols], out_hbm.at[:, cols], out_sem.at[len(stores)])
            store.start()
            stores.append(store)
    for store in stores:
        store.wait()


def rim_kernel(slot_ref, recv_ref, val_ref, proj_ref, out_ref):
    count = KCONV - 1
    slots = [slot_ref[i] for i in range(count)]
    starts = [jnp.maximum(k, 0) * QUART for k in slots]
    rows = [recv_ref[pl.ds(pl.multiple_of((k >> 4) * 16, 16), 16), :] for k in starts]
    rows = jnp.concatenate(rows, axis=0)
    row, col = iota((EDGE, 16 * count), 0), iota((EDGE, 16 * count), 1)
    at = jnp.full((EDGE, 16 * count), -16, jnp.int32)
    taken = jnp.full((EDGE, 1), -1, jnp.int32)
    for i, k in enumerate(starts):
        at = jnp.where(row == EDGE - count + i, 16 * i + (k & 15), at)
        taken = jnp.where(iota((EDGE, 1), 0) == EDGE - count + i, slots[i], taken)
    for b in range(QUART):
        place = jnp.where(col == at + b, 1.0, 0.0).astype(bf16)
        tile = dot(place, rows[:, V_AT:G_AT])
        cols = slice(b * 1024, (b + 1) * 1024)
        out_ref[:, cols] = jnp.where(taken >= 0, tile, val_ref[:, cols].astype(f32)).astype(bf16)
        tile = dot(place, rows[:, P_AT:S_AT])
        cols = slice(b * 256, (b + 1) * 256)
        out_ref[:, E + b * 256 : E + (b + 1) * 256] = jnp.where(
            taken >= 0, tile, proj_ref[:, cols].astype(f32)
        ).astype(bf16)


def placement(at_ref):
    return jnp.where(iota((TOK, LANES), 0) == at_ref[...], 1.0, 0.0).astype(bf16)


def spread_out(recv, wide_ref):
    for k in range(recv.shape[1] // LANES):
        wide_ref[k] = recv[:, k * LANES : (k + 1) * LANES].astype(f32)


def quarter_rows(wide_ref, b, count):
    rows = [wide_ref[k, pl.ds(b, 2 * DEVS, stride=QUART), :] for k in range(count)]
    return jnp.concatenate(rows, axis=1).astype(bf16)


def conv_chunk(x, before, weights, bias):
    ext = jnp.concatenate([before, x], axis=0)
    total = bias + weights[KCONV - 1 : KCONV, :] * x
    for back in range(1, KCONV):
        total = total + weights[KCONV - 1 - back : KCONV - back, :] * pltpu.roll(ext, back, 0)[8:]
    return silu(total).astype(bf16)


CHUNK_ROWS = 64


def conv_columns(tile_ref, text_ref, taken_ref, cols, weights, bias, use):
    before = jnp.zeros((8, LANES), f32)
    for low in range(0, TOK, CHUNK_ROWS):
        rows = slice(low, low + CHUNK_ROWS)
        x = jnp.where(taken_ref[rows, :] > 0, tile_ref[rows, cols], text_ref[rows, cols].astype(f32))
        use(rows, x, conv_chunk(x, before, weights, bias))
        before = x[CHUNK_ROWS - 8 :]


def softplus(v):
    return jnp.maximum(v, 0.0) + jnp.log1p(jnp.exp(-jnp.abs(v)))


def three(x):
    a = x.astype(bf16)
    left = x - a.astype(f32)
    b = left.astype(bf16)
    return a, b, (left - b.astype(f32)).astype(bf16)


def order(i):
    return lax.rem(i, G // 2) * 2 + i // (G // 2)


def place_kernel(
    recv_hbm, val_hbm, proj_hbm, at_ref, step_ref, w_ref, b_ref, sbias_ref, dlog_ref,
    conv_hbm, in_hbm, out_hbm, state_ref, cum_ref, size_ref, total_ref, hv_ref, hp_ref, we_ref,
    recv_ref, val_ref, proj_ref, conv_ref, in_ref, out_ref, place_scr, taken_scr, wide_scr, tail_scr,
    tile_scr, weight_scr, part_scr, recv_sem, val_sem, proj_sem, conv_sem, bc_sem,
):
    def load(i):
        cols = group_cols(order(i))
        return pltpu.make_async_copy(val_hbm.at[:, cols], val_ref.at[:, cols], val_sem.at[i])

    def store(i):
        cols = group_cols(order(i))
        return pltpu.make_async_copy(conv_ref.at[:, cols], conv_hbm.at[:, cols], conv_sem.at[i])

    def arrived(i, low, high):
        return pltpu.make_async_copy(recv_hbm.at[:, low:high], recv_ref.at[:, low:high], recv_sem.at[i])

    load_proj = pltpu.make_async_copy(proj_hbm, proj_ref, proj_sem)
    pieces = [arrived(0, P_AT, CHUNK), arrived(1, 0, GW), arrived(2, GW, 2 * GW)]
    store_bc = [
        pltpu.make_async_copy(src, dst, bc_sem.at[i])
        for i, (src, dst) in enumerate(((in_ref, in_hbm), (out_ref, out_hbm)))
    ]
    pieces[0].start()
    load_proj.start()
    pieces[1].start()
    for i in range(G // 2):
        load(i).start()
    pieces[2].start()
    for i in range(G // 2, G):
        load(i).start()

    def first():
        place_scr[...] = placement(at_ref)
        taken_scr[...] = dot(place_scr[...], jnp.ones((LANES, LANES), bf16))
        pieces[0].wait()
        spread_out(recv_ref[:, P_AT:], wide_scr)
        load_proj.wait()
        for b in range(QUART):
            tile_scr[0, :, :256] = dot(place_scr[...], quarter_rows(wide_scr, b, 2))
            for half in range(2):
                pair = b * 2 + half
                cols = slice(pair * LANES, (pair + 1) * LANES)

                def use(rows, x, y, pair=pair, cols=cols):
                    if rows.start == 0:
                        hp_ref[:, cols] = x[:EDGE].astype(bf16)
                    if pair < G // 2:
                        in_ref[pair, rows, :] = y
                    else:
                        out_ref[pair - G // 2, rows, :] = y

                at = slice(E + pair * LANES, E + (pair + 1) * LANES)
                conv_columns(
                    tile_scr.at[0, :, half * LANES : (half + 1) * LANES], proj_ref.at[:, cols], taken_scr,
                    slice(None), w_ref[:, at], b_ref[:, at], use,
                )
        for copy in store_bc:
            copy.start()
        steps = wide_scr[2, pl.ds(0, 2 * DEVS, stride=QUART), :].astype(bf16)
        tile = dot(place_scr[...], steps)
        step = step_ref[...].astype(f32)
        step = jnp.where(taken_scr[...] > 0, tile, jnp.concatenate([step, step], axis=1))
        sbias, dlog = sbias_ref[...], dlog_ref[...]
        size = softplus(step + jnp.concatenate([sbias, sbias], axis=1))
        logs = -jnp.exp(jnp.concatenate([dlog, dlog], axis=1)) * size
        size_ref[...] = size
        lower = jnp.where(iota((SPAN, SPAN), 0) >= iota((SPAN, SPAN), 1), 1.0, 0.0).astype(bf16)
        cums = []
        for k in range(TOK // SPAN):
            parts = three(logs[k * SPAN : (k + 1) * SPAN])
            cums.append(dot(lower, parts[0]) + (dot(lower, parts[1]) + dot(lower, parts[2])))
        last = [c[SPAN - 1 : SPAN, :] for c in cums]
        for k, c in enumerate(cums):
            rows = slice(k * SPAN, (k + 1) * SPAN)
            cum_ref[rows, :] = c
            left = last[k] - c
            if k == 0:
                left = left + last[1]
            tail_scr[rows, :] = split2(jnp.exp(left) * size[rows])
        total_ref[...] = jnp.broadcast_to(jnp.exp(last[0] + last[1]), total_ref.shape)

    first()
    for odd in range(2):
        pieces[1 + odd].wait()
        spread_out(recv_ref[:, odd * GW : (odd + 1) * GW], wide_scr)

        @pl.loop(0, G // 4)
        def _(two, odd=odd):
            for slot in range(2):
                pair = 2 * two + slot
                g = 2 * pair + odd
                i = odd * (G // 2) + pair
                tile_scr[slot] = dot(place_scr[...], quarter_rows(wide_scr, pair, GW // LANES))
                weight_scr[slot] = dot(tail_scr[...], expander(g))
                we_ref[:, group_cols(g)] = weight_scr[slot, :EDGE, :]
                load(i).wait()
                for k in range(GW // LANES):
                    cols = pl.ds(pl.multiple_of(g * GW + k * LANES, LANES), LANES)
                    part = slice(k * LANES, (k + 1) * LANES)

                    def use(rows, x, y, cols=cols, part=part, slot=slot):
                        if rows.start == 0:
                            hv_ref[:, cols] = x[:EDGE].astype(bf16)
                        conv_ref[rows, cols] = y
                        weight = weight_scr[slot, rows, part]
                        part_scr[slot, rows, part] = (y.astype(f32) * weight).astype(bf16)

                    conv_columns(
                        tile_scr.at[slot, :, part], val_ref.at[:, cols], taken_scr, slice(None),
                        w_ref[:, cols], b_ref[:, cols], use,
                    )
                store(i).start()
            for slot in range(2):
                pair = 2 * two + slot
                rows = pl.ds(pl.multiple_of((2 * pair + odd) * N, N), N)
                b_g = in_ref[pair, EDGE:, odd * N : (odd + 1) * N]
                state_ref[rows, :] = dot_rows(b_g, part_scr[slot, EDGE:, :])

    for copy in store_bc:
        copy.wait()
    for i in range(G):
        store(i).wait()


def power8(s):
    s2 = s * s
    s4 = s2 * s2
    s8 = s4 * s4
    return jnp.where(s < 0, -s8, s8).astype(bf16)


def root8(code):
    code = code.astype(f32)
    size = jnp.exp(0.125 * jnp.log(jnp.abs(code)))
    return jnp.where(code < 0, -size, size)


FLOOR = 1e-30


def edge_kernel(
    rim_ref, hv_ref, hp_ref, w_ref, b_ref, we_ref, total_ref, state_ref,
    send_ref, conv_ref, proj_ref,
    full_scr,
):
    def conv(x_ref, at, columns):
        before = rim_ref[EDGE - 8 :, columns].astype(f32)
        return conv_chunk(x_ref[:, at].astype(f32), before, w_ref[:, columns], b_ref[:, columns])

    p = [conv(hp_ref, slice(k * LANES, (k + 1) * LANES), slice(E + k * LANES, E + (k + 1) * LANES)) for k in range(PW // LANES)]
    p = jnp.concatenate(p, axis=1)
    proj_ref[...] = p
    top = jnp.zeros((8, LANES), f32)
    for g in range(G):
        b_g = p[:, g * N : (g + 1) * N]
        cols = slice(g * GW, (g + 1) * GW)
        y = conv(hv_ref, cols, cols)
        conv_ref[:, cols] = y
        rows = slice(g * N, (g + 1) * N)
        state = state_ref[rows, :] + dot_rows(b_g, (y.astype(f32) * we_ref[:, cols]).astype(bf16))
        full_scr[rows, :] = state
        sums = jnp.abs(state[:8])
        for k in range(8, N, 8):
            sums = sums + jnp.abs(state[k : k + 8])
        top = top + dot_cols(sums.astype(bf16), expander(g))
    top = jnp.maximum(jnp.sum(top, axis=0, keepdims=True) * 2.0**-14, FLOOR).astype(bf16).astype(f32)
    top = jnp.where(iota((8, LANES), 1) < H, top, 0.0)
    for g in range(G):
        back = 1.0 / dot(top.astype(bf16), expander(g))[:1]
        for low in range(g * N, (g + 1) * N, 32):
            send_ref[low : low + 32, :GW] = power8(full_scr[low : low + 32, :] * back)
    decay = split2(total_ref[...]).astype(f32)
    odd = (iota((8, LANES), 0) & 1) == 1
    side = jnp.where(odd, top, decay).astype(bf16)
    side = jnp.concatenate([side, side], axis=0)
    for low in range(0, G * N, 16):
        send_ref[low : low + 16, GW:] = side


def scan_kernel(dev_ref, recv_ref, after_ref, out_ref, bound_ref, side_scr):
    dev = dev_ref[0]
    side_scr[...] = dot(recv_ref[:, GW:], expander(dev // 8))

    def code(state, bound):
        return state * (1.0 / jnp.maximum(bound, FLOOR))

    def two(i, carry):
        rows = pl.ds(pl.multiple_of(i * 16, 16), 16)
        first, bound, own = carry
        state = root8(recv_ref[rows, :GW])
        side = side_scr[rows, :]
        second = side[:1] * first + state[:8] * side[1:2]
        second_bound = side[:1] * bound + side[1:2]
        out_ref[rows, :] = power8(jnp.concatenate([code(first, bound), code(second, second_bound)], axis=0))
        part = recv_ref[rows, GW:].astype(f32)
        part = part + pltpu.roll(part, H, 1)
        own = jnp.where(2 * i < dev, part[:1] * own + part[1:2], own)
        own = jnp.where(2 * i + 1 < dev, part[8:9] * own + part[9:10], own)
        return (
            side[8:9] * second + state[8:] * side[9:10],
            side[8:9] * second_bound + side[9:10],
            own,
        )

    zeros = (jnp.zeros((8, GW), f32), jnp.zeros((1, GW), f32), jnp.zeros((1, LANES), f32))
    own = lax.fori_loop(0, DEVS // 2, two, zeros, unroll=8)[2]
    bound_ref[...] = jnp.broadcast_to(own, bound_ref.shape)


def local_kernel(
    odd, recv_ref, at_ref, gate_ref, conv_ref, edge_ref, in_ref, out_ref, ein_ref, eout_ref,
    cum_ref, cumt_ref, size_ref, skip_ref, *rest,
):
    mix_out, scale_out, query_ref, place_scr, taken_scr, wide_scr, gate_scr, weighted_scr, first_scr, mix_ref, scale_ref = rest[-11:]
    i = pl.program_id(0)
    g = 2 * i + odd

    @pl.when(i == 0)
    def _():
        place_scr[...] = placement(at_ref)
        taken_scr[...] = dot(place_scr[...], jnp.ones((LANES, LANES), bf16))
        spread_out(recv_ref[...], wide_scr)

    def patched(edge, rest):
        return jnp.concatenate([edge, rest[EDGE:]], axis=0)

    half = slice(odd * N, (odd + 1) * N)
    b_g = patched(ein_ref[:, half], in_ref[0, :, half])
    c_g = patched(eout_ref[:, half], out_ref[0, :, half])
    query_ref[0] = c_g
    cum = cum_ref[...]
    spread = expander(g)
    skip = skip_ref[...]
    skip = jnp.broadcast_to(jnp.concatenate([skip, skip], axis=1), (8, LANES))
    skip = dot(split2(skip), spread)[:1]
    last = cum[SPAN - 1 : SPAN, :]
    upto = jnp.concatenate([cum[:SPAN], cum[SPAN:] + last], axis=0)
    scale_ref[...] = dot(split2(jnp.exp(upto)), spread)
    weighted_scr[...] = dot(split2(size_ref[...]), spread)
    gate_scr[...] = dot(place_scr[...], quarter_rows(wide_scr, i, GW // LANES))
    own = pltpu.roll(cum, lax.rem(LANES - g * (H // G), LANES), 1)
    for low in range(0, TOK, 32):
        rows = slice(low, low + 32)
        taken = taken_scr[rows, :] > 0
        for k in range(GW // LANES):
            cols = slice(k * LANES, (k + 1) * LANES)
            gate = silu(jnp.where(taken, gate_scr[rows, cols], gate_ref[rows, cols].astype(f32)))
            gate_scr[rows, cols] = gate
            scale_out[rows, cols] = (scale_ref[rows, cols] * gate).astype(bf16)
            x = conv_ref[rows, cols]
            if low == 0:
                x = patched(edge_ref[:, cols], x)
            x = x.astype(f32)
            weighted_scr[rows, cols] = weighted_scr[rows, cols] * x
            mix_ref[rows, cols] = skip[:, cols] * x
    tail = dot(split2(jnp.exp(last - cum[:SPAN])), spread)
    inner = dot(split2(jnp.exp(cum[SPAN:])), spread)
    state = dot_rows(b_g[:SPAN], (weighted_scr[:SPAN] * tail).astype(bf16))
    first_scr[...] = dot_whole(c_g[SPAN:], state) * inner
    causal = iota((SPAN, SPAN), 0) >= iota((SPAN, SPAN), 1)
    lane = iota((SPAN, LANES), 1)
    for k in range(TOK // SPAN):
        rows = slice(k * SPAN, (k + 1) * SPAN)
        scores = jnp.where(causal, dot_cols(c_g[rows], b_g[rows]), 0.0)
        for pair in range(H // G // 2):
            kernels = []
            for head in (2 * pair, 2 * pair + 1):
                apart = own[rows, head : head + 1] - cumt_ref[0, head : head + 1, rows]
                kernels.append((jnp.exp(jnp.minimum(apart, 0.0)) * scores).astype(bf16))
            cols = slice(pair * LANES, (pair + 1) * LANES)
            w = weighted_scr[rows, cols]
            low = jnp.where(lane < P_SIZE, w, 0.0).astype(bf16)
            high = jnp.where(lane < P_SIZE, 0.0, w).astype(bf16)
            mixed = dot(jnp.concatenate(kernels, axis=1), jnp.concatenate([low, high], axis=0))
            mixed = mixed + mix_ref[rows, cols]
            if k == 1:
                mixed = mixed + first_scr[:, cols]
            mix_out[rows, cols] = (mixed * gate_scr[rows, cols]).astype(bf16)


def final_kernel(
    bound_ref, entry_ref, gain_ref, qe_hbm, qo_hbm, me_hbm, se_hbm, mo_hbm, so_hbm, out_hbm,
    query_ref, mix_ref, scale_ref, out_ref, entry_scr, part_scr, square_scr, query_sem, mix_sem, scale_sem, out_sem,
):
    queries = [
        pltpu.make_async_copy(src, query_ref.at[i * G // 2 : (i + 1) * G // 2], query_sem.at[i])
        for i, src in enumerate((qe_hbm, qo_hbm))
    ]
    mixes, scales, stores = [], [], []
    for i in range(G):
        cols = slice(i % (G // 2) * GW, (i % (G // 2) + 1) * GW)
        mix, scale = (me_hbm, se_hbm) if i < G // 2 else (mo_hbm, so_hbm)
        mixes.append(pltpu.make_async_copy(mix.at[:, cols], mix_ref.at[i], mix_sem.at[i]))
        scales.append(pltpu.make_async_copy(scale.at[:, cols], scale_ref.at[i], scale_sem.at[i]))
        g = i % (G // 2) * 2 + i // (G // 2)
        cols = slice(g * GW, (g + 1) * GW)
        stores.append(pltpu.make_async_copy(out_ref.at[:, cols], out_hbm.at[:, cols], out_sem.at[i]))
    for load in (*queries, *(c for pair in zip(mixes, scales) for c in pair)):
        load.start()
    bound = split2(jnp.maximum(bound_ref[...], FLOOR))
    for g in range(G):
        rows = slice(g * N, (g + 1) * N)
        entry_scr[rows, :] = root8(entry_ref[rows, :]) * dot(bound, expander(g))[:1]
    for query in queries:
        query.wait()
    for i in range(G):
        g = i % (G // 2) * 2 + i // (G // 2)
        own = dot_whole(query_ref[i], entry_scr[g * N : (g + 1) * N, :])
        mixes[i].wait()
        scales[i].wait()
        for k in range(GW // LANES):
            cols = slice(k * LANES, (k + 1) * LANES)
            part = mix_ref[i, :, cols].astype(f32) + scale_ref[i, :, cols].astype(f32) * own[:, cols]
            part_scr[:, cols] = part
            square_scr[:, cols] = (part * part).astype(bf16)
        mean = dot(square_scr[...], jnp.ones((GW, LANES), bf16)) * (1.0 / GW)
        mean = lax.rsqrt(mean + 1e-05)
        for k in range(GW // LANES):
            cols = slice(k * LANES, (k + 1) * LANES)
            at = slice(g * GW + k * LANES, g * GW + (k + 1) * LANES)
            out_ref[:, at] = (part_scr[:, cols] * mean * gain_ref[:, at]).astype(bf16)
        stores[i].start()
    for store in stores:
        store.wait()


def call(kernel, outs, grid, in_specs, out_specs, scratch=(), est=None, name=None, vmem=VMEM_MIB, alias=None):
    return pl.pallas_call(
        kernel,
        out_shape=outs,
        grid_spec=pltpu.PrefetchScalarGridSpec(
            num_scalar_prefetch=0,
            grid=grid,
            in_specs=in_specs,
            out_specs=out_specs,
            scratch_shapes=scratch,
        ),
        compiler_params=pltpu.CompilerParams(vmem_limit_bytes=vmem * MIB),
        input_output_aliases=alias or {},
        cost_estimate=est,
        name=name,
    )


def struct(*shape, dtype=bf16):
    return pltpu.HBM(shape, dtype)


def near(*shape, dtype=bf16):
    return pltpu.VMEM(shape, dtype)


def far(a):
    return pltpu.with_memory_space_constraint(a, pltpu.HBM)


def kept(a):
    return pltpu.with_memory_space_constraint(a, pltpu.VMEM)


def exchange(rows):
    return lax.all_to_all(rows, "ctx", split_axis=0, concat_axis=0, tiled=True)


def twice(a):
    return jnp.concatenate([a, a], axis=-1)


def shards(
    text_values, text_gate, text_proj, text_step, tile_values, tile_gate, tile_proj, tile_step,
    tile_position, tile_count, conv_weight, conv_bias, step_bias, decay_log, skip_gain, norm_gain,
):
    device = lax.axis_index("ctx")
    scalar = pl.BlockSpec(memory_space=pltpu.SMEM)
    dev = device.reshape(1).astype(jnp.int32)

    hbm = pl.BlockSpec(memory_space=pl.ANY)
    sems = pltpu.SemaphoreType.DMA
    packed = call(
        pack_kernel,
        struct(DEVS * 8, CHUNK),
        (1,),
        [scalar, whole((32, LANES)), whole((TILE, H)), hbm, hbm, hbm],
        hbm,
        scratch=[pltpu.VMEM((TILE, E), bf16), pltpu.VMEM((TILE, E), bf16), pltpu.VMEM((TILE, PW), bf16),
                 pltpu.VMEM((DEVS * 8, CHUNK), bf16), sems((3,)), sems((5,))],
        est=cost(2 * 512 * 256 * CHUNK, 4_000_000),
        name="pack",
    )(dev, far(tile_position.reshape(32, LANES)), far(tile_step), far(tile_values), far(tile_gate), far(tile_proj))
    recv = kept(exchange(packed))

    position = tile_position.reshape(DEVS, TILE)
    ids = jnp.arange(TILE, dtype=jnp.int32)
    landing = ((position >> 8) == device) & (ids[None, :] < tile_count[:, None])
    local = jnp.where(landing, position & (TOK - 1), -1)
    at = jnp.max(local.reshape(DEVS, TILE // 2, 2), axis=1).reshape(1, 2 * DEVS)
    ends = jnp.arange(TOK - KCONV + 1, TOK)[:, None]
    rim_slot = jnp.max(jnp.where(at == ends, jnp.arange(2 * DEVS)[None, :], -1), axis=1)
    at = far(at)
    bias = conv_bias[None, :]

    recv_spec = whole((DEVS * 8, CHUNK))
    at_spec = whole((1, 2 * DEVS))
    rim = call(
        rim_kernel,
        struct(EDGE, E + PW),
        (1,),
        [scalar, recv_spec,
         pl.BlockSpec((EDGE, E), lambda i: (TOK // EDGE - 1, 0)),
         pl.BlockSpec((EDGE, PW), lambda i: (TOK // EDGE - 1, 0))],
        whole((EDGE, E + PW)),
        est=cost(2 * 16 * 48 * 5120, 3_000_000),
        name="rim",
    )(rim_slot, recv, far(text_values), far(text_proj))
    rim = lax.ppermute(rim, "ctx", [(i, i + 1) for i in range(DEVS - 1)])

    conv, inputs, outputs, state, cum, size, total, head_v, head_p, tail = call(
        place_kernel,
        (
            struct(TOK, E), struct(G // 2, TOK, LANES), struct(G // 2, TOK, LANES), near(G * N, GW, dtype=f32),
            struct(TOK, LANES, dtype=f32), struct(TOK, LANES, dtype=f32),
            near(8, LANES, dtype=f32),
            near(EDGE, E), near(EDGE, PW), near(EDGE, E, dtype=f32),
        ),
        (1,),
        [hbm, hbm, hbm, at_spec, whole((TOK, H)), whole((KCONV, E + PW)), whole((1, E + PW)),
         whole((1, H)), whole((1, H))],
        [hbm, hbm, hbm, whole((G * N, GW)), whole((TOK, LANES)), whole((TOK, LANES)),
         whole((8, LANES)), whole((EDGE, E)), whole((EDGE, PW)), whole((EDGE, E))],
        scratch=[pltpu.VMEM((DEVS * 8, CHUNK), bf16), pltpu.VMEM((TOK, E), bf16), pltpu.VMEM((TOK, PW), bf16),
                 pltpu.VMEM((TOK, E), bf16), pltpu.VMEM((G // 2, TOK, LANES), bf16), pltpu.VMEM((G // 2, TOK, LANES), bf16),
                 pltpu.VMEM((TOK, LANES), bf16), pltpu.VMEM((TOK, LANES), f32),
                 pltpu.VMEM((GW // LANES, DEVS * 8, LANES), f32), pltpu.VMEM((TOK, LANES), bf16),
                 pltpu.VMEM((2, TOK, GW), f32), pltpu.VMEM((2, TOK, GW), f32), pltpu.VMEM((2, TOK, GW), bf16),
                 sems((3,)), sems((G,)), sems(()), sems((G,)), sems((2,))],
        est=cost(2 * 256 * 512 * 5120, 10_000_000, 1_300_000),
        name="place",
    )(recv, far(text_values), far(text_proj), at, far(text_step), far(conv_weight), far(bias),
      far(step_bias[None, :]), far(decay_log[None, :]))

    send, edge, edge_p = call(
        edge_kernel,
        (struct(G * N, STATE_W), struct(EDGE, E), struct(EDGE, PW)),
        (1,),
        [whole((EDGE, E + PW)), whole((EDGE, E)), whole((EDGE, PW)), whole((KCONV, E + PW)),
         whole((1, E + PW)), whole((EDGE, E)), whole((8, LANES)), whole((G * N, GW))],
        [whole((G * N, STATE_W)), whole((EDGE, E)), whole((EDGE, PW))],
        scratch=[pltpu.VMEM((G * N, GW), f32)],
        est=cost(2 * 64 * 16 * 4096, 2_000_000, 100_000),
        name="edge",
    )(kept(rim), kept(head_v), kept(head_p), far(conv_weight), far(bias), kept(tail), kept(total), kept(state))
    states = kept(exchange(send))

    by_head = cum[:, :H].T.reshape(G, H // G, TOK)

    def rows_own(odd, more):
        per_pair = pl.BlockSpec((1, TOK, LANES), lambda i: (i, 0, 0))
        cols = pl.BlockSpec((TOK, GW), lambda i: (0, 2 * i + odd))
        own_cols = pl.BlockSpec((TOK, GW), lambda i: (0, i))
        anywhere = pl.BlockSpec(memory_space=pl.ANY)
        return call(
            functools.partial(local_kernel, odd),
            (struct(TOK, E // 2), struct(TOK, E // 2), struct(G // 2, TOK, N)),
            (G // 2,),
            [pl.BlockSpec((DEVS * 8, GW), lambda i: (0, G_AT // GW + odd)), at_spec, cols, cols,
             pl.BlockSpec((EDGE, GW), lambda i: (0, 2 * i + odd)), per_pair, per_pair,
             pl.BlockSpec((EDGE, LANES), lambda i: (0, i)), pl.BlockSpec((EDGE, LANES), lambda i: (0, G // 2 + i)),
             whole((TOK, LANES)), pl.BlockSpec((1, H // G, TOK), lambda i: (2 * i + odd, 0, 0)),
             whole((TOK, LANES)), whole((1, H))] + [anywhere] * len(more),
            [own_cols, own_cols, pl.BlockSpec((1, TOK, N), lambda i: (i, 0, 0))],
            scratch=[pltpu.VMEM((TOK, LANES), bf16), pltpu.VMEM((TOK, LANES), f32),
                     pltpu.VMEM((GW // LANES, DEVS * 8, LANES), f32), pltpu.VMEM((TOK, GW), f32), pltpu.VMEM((TOK, GW), f32), pltpu.VMEM((SPAN, GW), f32),
                     pltpu.VMEM((TOK, GW), f32), pltpu.VMEM((TOK, GW), f32)],
            est=cost(6_000_000_000, 8_000_000, 2_000_000),
            name=f"local{odd}",
        )(recv, at, far(text_gate), *map(far, (conv, edge, inputs, outputs, edge_p, edge_p, cum, by_head, size, skip_gain[None, :])), *more)

    even = rows_own(0, ())
    entries, bound = call(
        scan_kernel,
        (struct(G * N, GW), near(8, LANES, dtype=f32)),
        (1,),
        [scalar, whole((DEVS * 8, STATE_W)), pl.BlockSpec(memory_space=pl.ANY)],
        [whole((G * N, GW)), whole((8, LANES))],
        scratch=[pltpu.VMEM((G * N, GW), f32)],
        est=cost(2 * 512 * 512 * 128, 1_200_000),
        name="scan",
    )(dev, states, even[2])
    entry = kept(exchange(entries))
    odds = rows_own(1, (bound,))

    return call(
        final_kernel,
        struct(TOK, E),
        (1,),
        [whole((8, LANES)), whole((G * N, GW)), whole((1, E))] + [hbm] * 6,
        hbm,
        scratch=[pltpu.VMEM((G, TOK, N), bf16), pltpu.VMEM((G, TOK, GW), bf16), pltpu.VMEM((G, TOK, GW), bf16),
                 pltpu.VMEM((TOK, E), bf16), pltpu.VMEM((G * N, GW), f32), pltpu.VMEM((TOK, GW), f32),
                 pltpu.VMEM((TOK, GW), bf16), sems((2,)), sems((G,)), sems((G,)), sems((G,))],
        est=cost(2 * 256 * 64 * 4096, 11_000_000),
        name="final",
    )(kept(bound), entry, far(norm_gain[None, :]), *map(far, (even[2], odds[2], even[0], even[1], odds[0], odds[1])))


def solution(mesh):
    rows = P(("dp", "ctx"), None)
    specs = (rows,) * 8 + (P("dp"),) * 2 + (P(),) * 6
    return jax.shard_map(shards, mesh=mesh, in_specs=specs, out_specs=rows, check_vma=False)
```

time: 854 us -> 122 us (0.14)
  the two profiles are of different devices: /device:TPU:126 before, /device:TPU:0 now
where the time goes in v1:
time: 122 us; the launch traced here: 121 us
  Pallas kernels  44.9 us (37%)
  waiting for transfers between devices  34.3 us (28%)
  starting transfers between devices  30.1 us (25%)
  local copies, waits for them, and re-layouts  8.19 us (7%)
  other arithmetic  3.4 us (3%)
    all_to_all x3, waiting for transfers between devices, exchange(): return lax.all_to_all(rows, 'ctx', split_axis=0, concat_axis=0, tiled=True)  34.3 us
    all_to_all x3, starting transfers between devices, exchange(): return lax.all_to_all(rows, 'ctx', split_axis=0, concat_axis=0, tiled=True)  27.5 us
    pallas_call x2, Pallas kernels, rows_own(): call(functools.partial(local_kernel, odd), (struct(TOK, E // 2), struct(T...  15.5 us
    pallas_call x1, Pallas kernels, shards(): call(place_kernel, (struct(TOK, E), struct(G // 2, TOK, LANES), struct(G...  11.6 us
    pallas_call x1, Pallas kernels, shards(): call(final_kernel, struct(TOK, E), (1,), [whole((8, LANES)), whole((G * N...  6.9 us
    pallas_call x1, Pallas kernels, shards(): call(pack_kernel, struct(DEVS * 8, CHUNK), (1,), [scalar, whole((32, LANE...  3.88 us
    pallas_call x1, Pallas kernels, shards(): call(edge_kernel, (struct(G * N, STATE_W), struct(EDGE, E), struct(EDGE,...  3.18 us
    ppermute x1, starting transfers between devices, shards(): rim = lax.ppermute(rim, 'ctx', [(i, i + 1) for i in range(DEVS - 1)])  2.6 us
  transfers between devices with their start and end apart: 4, of which 3 were waited for; matrix products, arithmetic and copies ran while one was open for 9% of the time, Pallas kernels for 22%

profile of v1, /device:TPU:0, one launch (start us, length us, event | category | flops | bytes accessed | tf_op | source)
XLA Modules:
  0.0 121.2 jit_solution(12906130245705721047)
XLA Ops:
  0.0 3.9 %pack.1 = bf16[512,2432]{1,0:T(8,128)(2,1)} custom-call(s32[1]{0:T(128)} %bitcast.dev_ref, s32[32,128]{1,0:T(8,128)} %bitcast.25, bf16[64,64]{1,0:T(8,128)(2,1)} %step_ref.2, bf16[64,4096]{1,0:T(8,128)(2,1)} %val_hbm.2, bf16[64,4096]{1,0:T(8,128)(2,1)} %gate_hbm.1, bf16[64,1024]{1,0:T(8,128)(2,1)} %proj_hbm.2), custom_call_target="tpu_custom_call" | custom-call | flops 637534208 | bytes 4000000 | tf_op jit(solution)/shard_map/pack/pallas_call | solution.py:575
  3.9 0.0 copy-start.2
  3.9 11.5 %all-to-all-start = ((bf16[64,8,2432]{2,1,0:T(8,128)(2,1)}), bf16[64,8,2432]{2,1,0:T(8,128)(2,1)S(1)}, u32[]{:S(2)}, u32[]{:S(2)}) async-start(bf16[64,8,2432]{2,1,0:T(8,128)(2,1)} %bitcast.22), calls=%async_computation | async-start | bytes 4980736 | tf_op jit(solution)/shard_map/all_to_all | solution.py:558
  15.4 0.0 copy-done.2
  15.4 0.6 broadcast_and_fusion
  16.0 1.7 %and.18 = s32[64,32,2]{2,1,0:T(8,128)S(1)} reshape(s32[4096]{0:T(1024)} %broadcast_and_fusion) | data formatting | bytes 32768 | tf_op jit(solution)/shard_map/and | solution.py:591
  17.8 0.6 shift-right-arithmetic_compare_fusion
  18.4 2.5 %eq.27 = pred[64,32,2]{2,1,0:T(8,128)(4,1)} reshape(pred[4096]{0:T(1024)(128)(4,1)} %shift-right-arithmetic_compare_fusion) | data formatting | bytes 8192 | tf_op jit(solution)/shard_map/eq | solution.py:590
  20.9 2.0 %select_reduce_fusion = s32[64,2]{1,0:T(8,128)} fusion(s32[64,32,2]{2,1,0:T(8,128)S(1)} %and.18, pred[64,32,2]{2,1,0:T(8,128)(4,1)} %eq.27, s32[32,2]{1,0:T(8,128)S(1)} %multiply_add_fusion, s32[64]{0:T(128)} %param.25), kind=kLoop, calls=%fused_computation | loop fusion | flops 16256 | bytes 21504 | tf_op jit(solution)/shard_map/reduce_max | solution.py:592
  22.9 0.9 eq.28
  23.8 0.2 select_reduce_fusion.1.slot_ref
  24.0 25.1 %all-to-all-done = bf16[64,8,2432]{2,1,0:T(8,128)(2,1)S(1)} async-done(((bf16[64,8,2432]{2,1,0:T(8,128)(2,1)}), bf16[64,8,2432]{2,1,0:T(8,128)(2,1)S(1)}, u32[]{:S(2)}, u32[]{:S(2)}) %all-to-all-start) | async-done | bytes 2490400 | tf_op jit(solution)/shard_map/all_to_all | solution.py:558
  49.1 0.0 copy-start.1
  49.1 0.0 copy-start.4
  49.1 1.8 %rim.1 = bf16[16,5120]{1,0:T(8,128)(2,1)} custom-call(s32[3]{0:T(128)S(1)} %select_reduce_fusion.1.slot_ref, bf16[512,2432]{1,0:T(8,128)(2,1)S(1)} %bitcast.16, bf16[256,4096]{1,0:T(8,128)(2,1)} %val_hbm.3, bf16[256,1024]{1,0:T(8,128)(2,1)} %proj_hbm.3), custom_call_target="tpu_custom_call" | custom-call | flops 7864320 | bytes 3000000 | tf_op jit(solution)/shard_map/rim/pallas_call | solution.py:600
  50.9 2.6 %collective-permute-start = (bf16[16,5120]{1,0:T(8,128)(2,1)}, bf16[16,5120]{1,0:T(8,128)(2,1)S(1)}, u32[]{:S(2)}, u32[]{:S(2)}) collective-permute-start(bf16[16,5120]{1,0:T(8,128)(2,1)} %rim.1), channel_id=1, source_target_pairs={{0,1},{1,2},{2,3},{3,4},{4,5},{5,6},{6,7},{7,8},{8,9},{9,10},{10,1... | collective-permute-start | bytes 491528 | tf_op jit(solution)/shard_map/ppermute | solution.py:611
  53.5 0.0 copy-done.1
  53.5 0.7 reshape.49.at_ref
  54.2 0.0 copy-done.4
  54.2 0.7 copy.21.step_ref
  54.9 11.6 %place.1 = (bf16[256,4096]{1,0:T(8,128)(2,1)}, bf16[4,256,128]{2,1,0:T(8,128)(2,1)}, bf16[4,256,128]{2,1,0:T(8,128)(2,1)}, f32[512,512]{1,0:T(8,128)S(1)}, f32[2...) custom-call(bf16[512,2432]{1,0:T(8,128)(2,1)S(1)} %bitcast.17, ...), custom_call_target="tpu_custom_call" | custom-call | flops 1342177280 | bytes 10000000 | tf_op jit(solution)/shard_map/place/pallas_call | solution.py:613
  66.5 0.0 copy-start.3
  66.6 0.0 collective-permute-done.rim_ref
  66.6 3.2 %edge.1 = (bf16[512,640]{1,0:T(8,128)(2,1)}, bf16[16,4096]{1,0:T(8,128)(2,1)}, bf16[16,1024]{1,0:T(8,128)(2,1)}) custom-call(bf16[16,5120]{1,0:T(8,128)(2,1)S(1)} %collective-permute-done.rim_ref, bf16[16,4096]{1,0:T(8,128)(2,1)S(1)} %get-tuple-element.26.hv_ref, bf16[16,1024]{1,0:T(8,128)(2,1)S(1)} %get-tuple-element.27.hp_ref, f32[4,5120]{1,0:T(4,128)} %w_ref.3, ...), custom_call_target="tpu_custom_call" | custom-call | flops 8388608 | bytes 2000000 | tf_op jit(solution)/shard_map/edge/pallas_call | solution.py:637
  69.7 10.9 %all-to-all-start.1 = ((bf16[64,8,640]{2,1,0:T(8,128)(2,1)}), bf16[64,8,640]{2,1,0:T(8,128)(2,1)S(1)}, u32[]{:S(2)}, u32[]{:S(2)}) async-start(bf16[64,8,640]{2,1,0:T(8,128)(2,1)} %bitcast.23), calls=%async_computation.1 | async-start | bytes 1310720 | tf_op jit(solution)/shard_map/all_to_all | solution.py:558
  80.6 0.0 copy-done.3
  80.7 0.7 copy.22
  81.4 7.7 %local0.1 = (bf16[256,2048]{1,0:T(8,128)(2,1)}, bf16[256,2048]{1,0:T(8,128)(2,1)}, bf16[4,256,64]{2,1,0:T(8,128)(2,1)}) custom-call(bf16[512,2432]{1,0:T(8,128)(2,1)S(1)} %bitcast.18, s32[1,128]{1,0:T(1,128)} %reshape.49.at_ref, bf16[256,4096]{1,0:T(8,128)(2,1)} %gate_ref.3, bf16[256,4096]{1,0:T(8,128)(2,1)} %get-tuple-element.32.conv_ref, ...), custom_call_target="tpu_custom_call" | custom-call | flops 6000000000 | bytes 8000000 | tf_op jit(solution)/shard_map/local0/pallas_call | solution.py:657
  89.1 5.1 %all-to-all-done.1 = bf16[64,8,640]{2,1,0:T(8,128)(2,1)S(1)} async-done(((bf16[64,8,640]{2,1,0:T(8,128)(2,1)}), bf16[64,8,640]{2,1,0:T(8,128)(2,1)S(1)}, u32[]{:S(2)}, u32[]{:S(2)}) %all-to-all-start.1) | async-done | bytes 655392 | tf_op jit(solution)/shard_map/all_to_all | solution.py:558
  94.2 0.0 copy-start
  94.2 0.9 copy-done
  95.2 2.1 %scan.1 = (bf16[512,512]{1,0:T(8,128)(2,1)}, f32[8,128]{1,0:T(8,128)S(1)}) custom-call(s32[1]{0:T(128)} %bitcast.dev_ref, bf16[512,640]{1,0:T(8,128)(2,1)S(1)} %bitcast.20, bf16[4,256,64]{2,1,0:T(8,128)(2,1)S(1)} %copy-done), custom_call_target="tpu_custom_call" | custom-call | flops 67108864 | bytes 1200000 | tf_op jit(solution)/shard_map/scan/pallas_call | solution.py:675
  97.3 5.0 %all-to-all-start.2 = ((bf16[64,8,512]{2,1,0:T(8,128)(2,1)}), bf16[64,8,512]{2,1,0:T(8,128)(2,1)S(1)}, u32[]{:S(2)}, u32[]{:S(2)}) async-start(bf16[64,8,512]{2,1,0:T(8,128)(2,1)} %bitcast.24), calls=%async_computation.2 | async-start | bytes 1048576 | tf_op jit(solution)/shard_map/all_to_all | solution.py:558
  102.3 7.7 %local1.1 = (bf16[256,2048]{1,0:T(8,128)(2,1)}, bf16[256,2048]{1,0:T(8,128)(2,1)}, bf16[4,256,64]{2,1,0:T(8,128)(2,1)}) custom-call(bf16[512,2432]{1,0:T(8,128)(2,1)S(1)} %bitcast.19, s32[1,128]{1,0:T(1,128)} %reshape.49.at_ref, bf16[256,4096]{1,0:T(8,128)(2,1)} %gate_ref.3, bf16[256,4096]{1,0:T(8,128)(2,1)} %get-tuple-element.32.conv_ref, ...), custom_call_target="tpu_custom_call" | custom-call | flops 6000000000 | bytes 8000000 | tf_op jit(solution)/shard_map/local1/pallas_call | solution.py:657
  110.1 4.1 %all-to-all-done.2 = bf16[64,8,512]{2,1,0:T(8,128)(2,1)S(1)} async-done(((bf16[64,8,512]{2,1,0:T(8,128)(2,1)}), bf16[64,8,512]{2,1,0:T(8,128)(2,1)S(1)}, u32[]{:S(2)}, u32[]{:S(2)}) %all-to-all-start.2) | async-done | bytes 524320 | tf_op jit(solution)/shard_map/all_to_all | solution.py:558
  114.1 6.9 %final.1 = bf16[256,4096]{1,0:T(8,128)(2,1)} custom-call(f32[8,128]{1,0:T(8,128)S(1)} %get-tuple-element.40.rest_0_.bound_ref, bf16[512,512]{1,0:T(8,128)(2,1)S(1)} %bitcast.21, f32[1,4096]{1,0:T(1,128)} %bitcast.30, bf16[4,256,64]{2,1,0:T(8,128)(2,1)} %get-tuple-element.39.after_ref.qe_hbm, bf16[4,256,64]{2,1,0:T(8,128)(2,1)} %get-tuple-element.42.qo_hbm, ...), custom_call_target="tpu_custom_call" | custom-call | flops 134217728 | bytes 11000000 | tf_op jit(solution)/shard_map/final/pallas_call | solution.py:688
  (3 shorter events, 0.0 us)
Async XLA Ops:
  3.9 11.5 %copy-start.2 = (s32[4096]{0:T(1024)S(1)}, s32[4096]{0:T(1024)}, u32[]{:S(2)}) copy-start(s32[4096]{0:T(1024)} %param.24) | copy-start | bytes 49156
  3.9 45.2 %all-to-all-start = ((bf16[64,8,2432]{2,1,0:T(8,128)(2,1)}), bf16[64,8,2432]{2,1,0:T(8,128)(2,1)S(1)}, u32[]{:S(2)}, u32[]{:S(2)}) async-start(bf16[64,8,2432]{2,1,0:T(8,128)(2,1)} %bitcast.22), calls=%async_computation | async-start | bytes 4980736 | tf_op jit(solution)/shard_map/all_to_all | solution.py:558
  49.1 4.4 %copy-start.1 = (s32[64,2]{1,0:T(8,128)S(1)}, s32[64,2]{1,0:T(8,128)}, u32[]{:S(2)}) copy-start(s32[64,2]{1,0:T(8,128)} %select_reduce_fusion) | copy-start | bytes 1540
  49.1 5.1 %copy-start.4 = (bf16[256,64]{0,1:T(8,128)(2,1)S(1)}, bf16[256,64]{0,1:T(8,128)(2,1)}, u32[]{:S(2)}) copy-start(bf16[256,64]{0,1:T(8,128)(2,1)} %param.19) | copy-start | bytes 98308
  50.9 15.7 %collective-permute-start = (bf16[16,5120]{1,0:T(8,128)(2,1)}, bf16[16,5120]{1,0:T(8,128)(2,1)S(1)}, u32[]{:S(2)}, u32[]{:S(2)}) collective-permute-start(bf16[16,5120]{1,0:T(8,128)(2,1)} %rim.1), channel_id=1, source_target_pairs={{0,1},{1,2},{2,3},{3,4},{4,5},{5,6},{6,7},{7,8},{8,9},{9,10},{10,1... | collective-permute-start | bytes 491528 | tf_op jit(solution)/shard_map/ppermute | solution.py:611
  66.5 14.1 %copy-start.3 = (f32[256,128]{1,0:T(8,128)S(1)}, f32[256,128]{1,0:T(8,128)}, u32[]{:S(2)}) copy-start(f32[256,128]{1,0:T(8,128)} %get-tuple-element.37.cum_ref) | copy-start | bytes 393220
  69.7 24.5 %all-to-all-start.1 = ((bf16[64,8,640]{2,1,0:T(8,128)(2,1)}), bf16[64,8,640]{2,1,0:T(8,128)(2,1)S(1)}, u32[]{:S(2)}, u32[]{:S(2)}) async-start(bf16[64,8,640]{2,1,0:T(8,128)(2,1)} %bitcast.23), calls=%async_computation.1 | async-start | bytes 1310720 | tf_op jit(solution)/shard_map/all_to_all | solution.py:558
  94.2 1.0 copy-start
  97.3 16.9 %all-to-all-start.2 = ((bf16[64,8,512]{2,1,0:T(8,128)(2,1)}), bf16[64,8,512]{2,1,0:T(8,128)(2,1)S(1)}, u32[]{:S(2)}, u32[]{:S(2)}) async-start(bf16[64,8,512]{2,1,0:T(8,128)(2,1)} %bitcast.24), calls=%async_computation.2 | async-start | bytes 1048576 | tf_op jit(solution)/shard_map/all_to_all | solution.py:558

commit v2 on v1

--- a/solution.py
+++ b/solution.py
@@ -84,16 +84,16 @@
 
 
 def pack_kernel(
-    dev_ref, pos_ref, step_ref, val_hbm, gate_hbm, proj_hbm, out_hbm,
-    val_ref, gate_ref, proj_ref, out_ref, in_sem, out_sem,
+    pos_hbm, step_hbm, val_hbm, gate_hbm, proj_hbm, out_hbm,
+    pos_ref, step_ref, val_ref, gate_ref, proj_ref, out_ref, in_sem, out_sem,
 ):
-    loads = [
-        pltpu.make_async_copy(src, dst, in_sem.at[i])
-        for i, (src, dst) in enumerate(((val_hbm, val_ref), (gate_hbm, gate_ref), (proj_hbm, proj_ref)))
-    ]
-    for load in loads:
+    pairs = ((val_hbm, val_ref), (gate_hbm, gate_ref), (proj_hbm, proj_ref), (pos_hbm, pos_ref), (step_hbm, step_ref))
+    loads = [pltpu.make_async_copy(src, dst, in_sem.at[i]) for i, (src, dst) in enumerate(pairs)]
+    for load in (loads[3], loads[4], loads[0], loads[1], loads[2]):
         load.start()
-    dev = dev_ref[0]
+    dev = lax.axis_index("ctx")
+    loads[3].wait()
+    loads[4].wait()
     row = pos_ref[pl.ds(dev // 2, 1), :]
     other = pltpu.roll(row, 64, 1)
     lane = iota((1, LANES), 1)
@@ -120,7 +120,7 @@
         store.wait()
 
 
-def rim_kernel(slot_ref, recv_ref, val_ref, proj_ref, out_ref):
+def rim_kernel(slot_ref, recv_ref, val_ref, proj_ref, at_ref, step_ref, out_ref):
     count = KCONV - 1
     slots = [slot_ref[i] for i in range(count)]
     starts = [jnp.maximum(k, 0) * QUART for k in slots]
@@ -194,10 +194,11 @@
 
 
 def place_kernel(
-    recv_hbm, val_hbm, proj_hbm, at_ref, step_ref, w_ref, b_ref, sbias_ref, dlog_ref,
+    recv_hbm, val_hbm, proj_hbm, at_hbm, step_hbm, w_hbm, b_hbm, sbias_hbm, dlog_hbm,
     conv_hbm, in_hbm, out_hbm, state_ref, cum_ref, size_ref, total_ref, hv_ref, hp_ref, we_ref,
+    at_ref, step_ref, w_ref, b_ref, sbias_ref, dlog_ref,
     recv_ref, val_ref, proj_ref, conv_ref, in_ref, out_ref, place_scr, taken_scr, wide_scr, tail_scr,
-    tile_scr, weight_scr, part_scr, recv_sem, val_sem, proj_sem, conv_sem, bc_sem,
+    tile_scr, weight_scr, part_scr, small_sem, recv_sem, val_sem, proj_sem, conv_sem, bc_sem,
 ):
     def load(i):
         cols = group_cols(order(i))
@@ -216,8 +217,15 @@
         pltpu.make_async_copy(src, dst, bc_sem.at[i])
         for i, (src, dst) in enumerate(((in_ref, in_hbm), (out_ref, out_hbm)))
     ]
+    pairs = (
+        (at_hbm, at_ref), (w_hbm, w_ref), (b_hbm, b_ref), (step_hbm, step_ref), (sbias_hbm, sbias_ref), (dlog_hbm, dlog_ref),
+    )
+    small = [pltpu.make_async_copy(src, dst, small_sem.at[i]) for i, (src, dst) in enumerate(pairs)]
+    small[0].start()
     pieces[0].start()
     load_proj.start()
+    for load_small in small[1:]:
+        load_small.start()
     pieces[1].start()
     for i in range(G // 2):
         load(i).start()
@@ -226,8 +234,11 @@
         load(i).start()
 
     def first():
+        small[0].wait()
         place_scr[...] = placement(at_ref)
         taken_scr[...] = dot(place_scr[...], jnp.ones((LANES, LANES), bf16))
+        for load_small in small[1:]:
+            load_small.wait()
         pieces[0].wait()
         spread_out(recv_ref[:, P_AT:], wide_scr)
         load_proj.wait()
@@ -283,13 +294,13 @@
         @pl.loop(0, G // 4)
         def _(two, odd=odd):
             for slot in range(2):
+                load(odd * (G // 2) + 2 * two + slot).wait()
+            for slot in range(2):
                 pair = 2 * two + slot
                 g = 2 * pair + odd
-                i = odd * (G // 2) + pair
                 tile_scr[slot] = dot(place_scr[...], quarter_rows(wide_scr, pair, GW // LANES))
                 weight_scr[slot] = dot(tail_scr[...], expander(g))
                 we_ref[:, group_cols(g)] = weight_scr[slot, :EDGE, :]
-                load(i).wait()
                 for k in range(GW // LANES):
                     cols = pl.ds(pl.multiple_of(g * GW + k * LANES, LANES), LANES)
                     part = slice(k * LANES, (k + 1) * LANES)
@@ -305,12 +316,13 @@
                         tile_scr.at[slot, :, part], val_ref.at[:, cols], taken_scr, slice(None),
                         w_ref[:, cols], b_ref[:, cols], use,
                     )
-                store(i).start()
             for slot in range(2):
                 pair = 2 * two + slot
                 rows = pl.ds(pl.multiple_of((2 * pair + odd) * N, N), N)
                 b_g = in_ref[pair, EDGE:, odd * N : (odd + 1) * N]
                 state_ref[rows, :] = dot_rows(b_g, part_scr[slot, EDGE:, :])
+            for slot in range(2):
+                store(odd * (G // 2) + 2 * two + slot).start()
 
     for copy in store_bc:
         copy.wait()
@@ -407,7 +419,8 @@
     odd, recv_ref, at_ref, gate_ref, conv_ref, edge_ref, in_ref, out_ref, ein_ref, eout_ref,
     cum_ref, cumt_ref, size_ref, skip_ref, *rest,
 ):
-    mix_out, scale_out, query_ref, place_scr, taken_scr, wide_scr, gate_scr, weighted_scr, first_scr, mix_ref, scale_ref = rest[-11:]
+    mix_out, scale_out, query_ref, token_ref, place_scr, taken_scr, wide_scr, gate_scr, weighted_scr, first_scr, mix_ref, scale_ref = rest[-12:]
+    token_ref[...] = jnp.zeros_like(token_ref)
     i = pl.program_id(0)
     g = 2 * i + odd
 
@@ -475,9 +488,10 @@
 
 
 def final_kernel(
-    bound_ref, entry_ref, gain_ref, qe_hbm, qo_hbm, me_hbm, se_hbm, mo_hbm, so_hbm, out_hbm,
-    query_ref, mix_ref, scale_ref, out_ref, entry_scr, part_scr, square_scr, query_sem, mix_sem, scale_sem, out_sem,
+    bound_ref, entry_ref, gain_hbm, qe_hbm, qo_hbm, me_hbm, se_hbm, mo_hbm, so_hbm, out_hbm,
+    gain_ref, query_ref, mix_ref, scale_ref, out_ref, entry_scr, part_scr, gain_sem, query_sem, mix_sem, scale_sem, out_sem,
 ):
+    gain = pltpu.make_async_copy(gain_hbm, gain_ref, gain_sem)
     queries = [
         pltpu.make_async_copy(src, query_ref.at[i * G // 2 : (i + 1) * G // 2], query_sem.at[i])
         for i, src in enumerate((qe_hbm, qo_hbm))
@@ -491,31 +505,38 @@
         g = i % (G // 2) * 2 + i // (G // 2)
         cols = slice(g * GW, (g + 1) * GW)
         stores.append(pltpu.make_async_copy(out_ref.at[:, cols], out_hbm.at[:, cols], out_sem.at[i]))
-    for load in (*queries, *(c for pair in zip(mixes, scales) for c in pair)):
+    for load in (*queries, gain, *(c for pair in zip(mixes, scales) for c in pair)):
         load.start()
     bound = split2(jnp.maximum(bound_ref[...], FLOOR))
     for g in range(G):
         rows = slice(g * N, (g + 1) * N)
         entry_scr[rows, :] = root8(entry_ref[rows, :]) * dot(bound, expander(g))[:1]
-    for query in queries:
-        query.wait()
+    for load in (*queries, gain):
+        load.wait()
     for i in range(G):
         g = i % (G // 2) * 2 + i // (G // 2)
+        if i % 2 == 0:
+            for load in (*mixes[i : i + 2], *scales[i : i + 2]):
+                load.wait()
+        slot = i % 2
         own = dot_whole(query_ref[i], entry_scr[g * N : (g + 1) * N, :])
-        mixes[i].wait()
-        scales[i].wait()
+        squares = jnp.zeros((TOK, LANES), f32)
         for k in range(GW // LANES):
             cols = slice(k * LANES, (k + 1) * LANES)
             part = mix_ref[i, :, cols].astype(f32) + scale_ref[i, :, cols].astype(f32) * own[:, cols]
-            part_scr[:, cols] = part
-            square_scr[:, cols] = (part * part).astype(bf16)
-        mean = dot(square_scr[...], jnp.ones((GW, LANES), bf16)) * (1.0 / GW)
+            part_scr[slot, :, cols] = part
+            squares = squares + part * part
+        high = squares.astype(bf16)
+        low = (squares - high.astype(f32)).astype(bf16)
+        mean = dot(jnp.concatenate([high, low], axis=1), jnp.ones((2 * LANES, LANES), bf16)) * (1.0 / GW)
         mean = lax.rsqrt(mean + 1e-05)
         for k in range(GW // LANES):
             cols = slice(k * LANES, (k + 1) * LANES)
             at = slice(g * GW + k * LANES, g * GW + (k + 1) * LANES)
-            out_ref[:, at] = (part_scr[:, cols] * mean * gain_ref[:, at]).astype(bf16)
-        stores[i].start()
+            out_ref[:, at] = (part_scr[slot, :, cols] * mean * gain_ref[:, at]).astype(bf16)
+        if i % 2 == 1:
+            stores[i - 1].start()
+            stores[i].start()
     for store in stores:
         store.wait()
 
@@ -571,18 +592,19 @@
     dev = device.reshape(1).astype(jnp.int32)
 
     hbm = pl.BlockSpec(memory_space=pl.ANY)
+    vmem = pl.BlockSpec(memory_space=pltpu.VMEM)
     sems = pltpu.SemaphoreType.DMA
     packed = call(
         pack_kernel,
         struct(DEVS * 8, CHUNK),
         (1,),
-        [scalar, whole((32, LANES)), whole((TILE, H)), hbm, hbm, hbm],
+        [hbm] * 5,
         hbm,
-        scratch=[pltpu.VMEM((TILE, E), bf16), pltpu.VMEM((TILE, E), bf16), pltpu.VMEM((TILE, PW), bf16),
-                 pltpu.VMEM((DEVS * 8, CHUNK), bf16), sems((3,)), sems((5,))],
+        scratch=[pltpu.VMEM((32, LANES), jnp.int32), pltpu.VMEM((TILE, H), bf16), pltpu.VMEM((TILE, E), bf16), pltpu.VMEM((TILE, E), bf16), pltpu.VMEM((TILE, PW), bf16),
+                 pltpu.VMEM((DEVS * 8, CHUNK), bf16), sems((5,)), sems((5,))],
         est=cost(2 * 512 * 256 * CHUNK, 4_000_000),
         name="pack",
-    )(dev, far(tile_position.reshape(32, LANES)), far(tile_step), far(tile_values), far(tile_gate), far(tile_proj))
+    )(far(tile_position.reshape(32, LANES)), far(tile_step), far(tile_values), far(tile_gate), far(tile_proj))
     recv = kept(exchange(packed))
 
     position = tile_position.reshape(DEVS, TILE)
@@ -593,6 +615,7 @@
     ends = jnp.arange(TOK - KCONV + 1, TOK)[:, None]
     rim_slot = jnp.max(jnp.where(at == ends, jnp.arange(2 * DEVS)[None, :], -1), axis=1)
     at = far(at)
+    steps = far(text_step)
     bias = conv_bias[None, :]
 
     recv_spec = whole((DEVS * 8, CHUNK))
@@ -601,13 +624,13 @@
         rim_kernel,
         struct(EDGE, E + PW),
         (1,),
-        [scalar, recv_spec,
+        [scalar, vmem,
          pl.BlockSpec((EDGE, E), lambda i: (TOK // EDGE - 1, 0)),
-         pl.BlockSpec((EDGE, PW), lambda i: (TOK // EDGE - 1, 0))],
+         pl.BlockSpec((EDGE, PW), lambda i: (TOK // EDGE - 1, 0)), hbm, hbm],
         whole((EDGE, E + PW)),
         est=cost(2 * 16 * 48 * 5120, 3_000_000),
         name="rim",
-    )(rim_slot, recv, far(text_values), far(text_proj))
+    )(rim_slot, recv, far(text_values), far(text_proj), at, steps)
     rim = lax.ppermute(rim, "ctx", [(i, i + 1) for i in range(DEVS - 1)])
 
     conv, inputs, outputs, state, cum, size, total, head_v, head_p, tail = call(
@@ -619,27 +642,26 @@
             near(EDGE, E), near(EDGE, PW), near(EDGE, E, dtype=f32),
         ),
         (1,),
-        [hbm, hbm, hbm, at_spec, whole((TOK, H)), whole((KCONV, E + PW)), whole((1, E + PW)),
-         whole((1, H)), whole((1, H))],
-        [hbm, hbm, hbm, whole((G * N, GW)), whole((TOK, LANES)), whole((TOK, LANES)),
-         whole((8, LANES)), whole((EDGE, E)), whole((EDGE, PW)), whole((EDGE, E))],
-        scratch=[pltpu.VMEM((DEVS * 8, CHUNK), bf16), pltpu.VMEM((TOK, E), bf16), pltpu.VMEM((TOK, PW), bf16),
+        [hbm] * 9,
+        [hbm, hbm, hbm, vmem, whole((TOK, LANES)), whole((TOK, LANES)), vmem, vmem, vmem, vmem],
+        scratch=[pltpu.VMEM((1, 2 * DEVS), jnp.int32), pltpu.VMEM((TOK, H), bf16), pltpu.VMEM((KCONV, E + PW), f32),
+                 pltpu.VMEM((1, E + PW), f32), pltpu.VMEM((1, H), f32), pltpu.VMEM((1, H), f32),
+                 pltpu.VMEM((DEVS * 8, CHUNK), bf16), pltpu.VMEM((TOK, E), bf16), pltpu.VMEM((TOK, PW), bf16),
                  pltpu.VMEM((TOK, E), bf16), pltpu.VMEM((G // 2, TOK, LANES), bf16), pltpu.VMEM((G // 2, TOK, LANES), bf16),
                  pltpu.VMEM((TOK, LANES), bf16), pltpu.VMEM((TOK, LANES), f32),
                  pltpu.VMEM((GW // LANES, DEVS * 8, LANES), f32), pltpu.VMEM((TOK, LANES), bf16),
                  pltpu.VMEM((2, TOK, GW), f32), pltpu.VMEM((2, TOK, GW), f32), pltpu.VMEM((2, TOK, GW), bf16),
-                 sems((3,)), sems((G,)), sems(()), sems((G,)), sems((2,))],
+                 sems((6,)), sems((3,)), sems((G,)), sems(()), sems((G,)), sems((2,))],
         est=cost(2 * 256 * 512 * 5120, 10_000_000, 1_300_000),
         name="place",
-    )(recv, far(text_values), far(text_proj), at, far(text_step), far(conv_weight), far(bias),
+    )(recv, far(text_values), far(text_proj), at, steps, far(conv_weight), far(bias),
       far(step_bias[None, :]), far(decay_log[None, :]))
 
     send, edge, edge_p = call(
         edge_kernel,
         (struct(G * N, STATE_W), struct(EDGE, E), struct(EDGE, PW)),
         (1,),
-        [whole((EDGE, E + PW)), whole((EDGE, E)), whole((EDGE, PW)), whole((KCONV, E + PW)),
-         whole((1, E + PW)), whole((EDGE, E)), whole((8, LANES)), whole((G * N, GW))],
+        [vmem, vmem, vmem, whole((KCONV, E + PW)), whole((1, E + PW)), vmem, vmem, vmem],
         [whole((G * N, STATE_W)), whole((EDGE, E)), whole((EDGE, PW))],
         scratch=[pltpu.VMEM((G * N, GW), f32)],
         est=cost(2 * 64 * 16 * 4096, 2_000_000, 100_000),
@@ -656,14 +678,14 @@
         anywhere = pl.BlockSpec(memory_space=pl.ANY)
         return call(
             functools.partial(local_kernel, odd),
-            (struct(TOK, E // 2), struct(TOK, E // 2), struct(G // 2, TOK, N)),
+            (struct(TOK, E // 2), struct(TOK, E // 2), struct(G // 2, TOK, N), near(8, LANES, dtype=f32)),
             (G // 2,),
             [pl.BlockSpec((DEVS * 8, GW), lambda i: (0, G_AT // GW + odd)), at_spec, cols, cols,
              pl.BlockSpec((EDGE, GW), lambda i: (0, 2 * i + odd)), per_pair, per_pair,
              pl.BlockSpec((EDGE, LANES), lambda i: (0, i)), pl.BlockSpec((EDGE, LANES), lambda i: (0, G // 2 + i)),
              whole((TOK, LANES)), pl.BlockSpec((1, H // G, TOK), lambda i: (2 * i + odd, 0, 0)),
              whole((TOK, LANES)), whole((1, H))] + [anywhere] * len(more),
-            [own_cols, own_cols, pl.BlockSpec((1, TOK, N), lambda i: (i, 0, 0))],
+            [own_cols, own_cols, pl.BlockSpec((1, TOK, N), lambda i: (i, 0, 0)), whole((8, LANES))],
             scratch=[pltpu.VMEM((TOK, LANES), bf16), pltpu.VMEM((TOK, LANES), f32),
                      pltpu.VMEM((GW // LANES, DEVS * 8, LANES), f32), pltpu.VMEM((TOK, GW), f32), pltpu.VMEM((TOK, GW), f32), pltpu.VMEM((SPAN, GW), f32),
                      pltpu.VMEM((TOK, GW), f32), pltpu.VMEM((TOK, GW), f32)],
@@ -676,12 +698,12 @@
         scan_kernel,
         (struct(G * N, GW), near(8, LANES, dtype=f32)),
         (1,),
-        [scalar, whole((DEVS * 8, STATE_W)), pl.BlockSpec(memory_space=pl.ANY)],
-        [whole((G * N, GW)), whole((8, LANES))],
+        [scalar, vmem, vmem],
+        [whole((G * N, GW)), vmem],
         scratch=[pltpu.VMEM((G * N, GW), f32)],
         est=cost(2 * 512 * 512 * 128, 1_200_000),
         name="scan",
-    )(dev, states, even[2])
+    )(dev, states, kept(even[3]))
     entry = kept(exchange(entries))
     odds = rows_own(1, (bound,))
 
@@ -689,11 +711,11 @@
         final_kernel,
         struct(TOK, E),
         (1,),
-        [whole((8, LANES)), whole((G * N, GW)), whole((1, E))] + [hbm] * 6,
+        [vmem, vmem] + [hbm] * 7,
         hbm,
-        scratch=[pltpu.VMEM((G, TOK, N), bf16), pltpu.VMEM((G, TOK, GW), bf16), pltpu.VMEM((G, TOK, GW), bf16),
-                 pltpu.VMEM((TOK, E), bf16), pltpu.VMEM((G * N, GW), f32), pltpu.VMEM((TOK, GW), f32),
-                 pltpu.VMEM((TOK, GW), bf16), sems((2,)), sems((G,)), sems((G,)), sems((G,))],
+        scratch=[pltpu.VMEM((1, E), f32), pltpu.VMEM((G, TOK, N), bf16), pltpu.VMEM((G, TOK, GW), bf16), pltpu.VMEM((G, TOK, GW), bf16),
+                 pltpu.VMEM((TOK, E), bf16), pltpu.VMEM((G * N, GW), f32), pltpu.VMEM((2, TOK, GW), f32),
+                 sems(()), sems((2,)), sems((G,)), sems((G,)), sems((G,))],
         est=cost(2 * 256 * 64 * 4096, 11_000_000),
         name="final",
     )(kept(bound), entry, far(norm_gain[None, :]), *map(far, (even[2], odds[2], even[0], even[1], odds[0], odds[1])))

time: 122 us -> 116 us (0.951)
  Pallas kernels: 44.9 us -> 41.7 us
    pallas_call x1, Pallas kernels: 11.6 us -> 9.92 us  [shards(): call(place_kernel, (struct(TOK, E), struct(G // 2, TOK, LANES), struct(G...]
    pallas_call x3, Pallas kernels: 12.6 us -> 10.9 us  [the longest x1 6 us: shards(): call(final_kernel, struct(TOK, E), (1,), [vmem, vmem] + [hbm] * 7, hbm, s...]
  transfers between devices with their start and end apart: 4 -> 4, of which waited for: 3 -> 3; matrix products, arithmetic and copies ran while one was open for 9% -> 8% of each run, Pallas kernels for 22% -> 22%
where the time goes in v2:
time: 116 us
  Pallas kernels  41.7 us (36%)
  waiting for transfers between devices  34 us (29%)
  starting transfers between devices  30.2 us (26%)
  local copies, waits for them, and re-layouts  7.32 us (6%)
  other arithmetic  2.22 us (2%)
    all_to_all x3, waiting for transfers between devices, exchange(): return lax.all_to_all(rows, 'ctx', split_axis=0, concat_axis=0, tiled=True)  34 us
    all_to_all x3, starting transfers between devices, exchange(): return lax.all_to_all(rows, 'ctx', split_axis=0, concat_axis=0, tiled=True)  27.6 us
    pallas_call x2, Pallas kernels, rows_own(): call(functools.partial(local_kernel, odd), (struct(TOK, E // 2), struct(T...  15.5 us
    pallas_call x1, Pallas kernels, shards(): call(place_kernel, (struct(TOK, E), struct(G // 2, TOK, LANES), struct(G...  9.92 us
    pallas_call x1, Pallas kernels, shards(): call(final_kernel, struct(TOK, E), (1,), [vmem, vmem] + [hbm] * 7, hbm, s...  6 us
    pallas_call x1, Pallas kernels, shards(): call(edge_kernel, (struct(G * N, STATE_W), struct(EDGE, E), struct(EDGE,...  3.19 us
    pallas_call x1, Pallas kernels, shards(): call(pack_kernel, struct(DEVS * 8, CHUNK), (1,), [hbm] * 5, hbm, scratch=...  3.16 us
    ppermute x1, starting transfers between devices, shards(): rim = lax.ppermute(rim, 'ctx', [(i, i + 1) for i in range(DEVS - 1)])  2.61 us
  transfers between devices with their start and end apart: 4, of which 3 were waited for; matrix products, arithmetic and copies ran while one was open for 8% of the time, Pallas kernels for 22%

profile of v2, /device:TPU:0, one launch (start us, length us, event | category | flops | bytes accessed | tf_op | source)
XLA Modules:
  0.0 115.7 jit_solution(4780809898683580483)
XLA Ops:
  0.0 3.2 %pack.1 = bf16[512,2432]{1,0:T(8,128)(2,1)} custom-call(s32[32,128]{1,0:T(8,128)} %bitcast.25, bf16[64,64]{1,0:T(8,128)(2,1)} %step_hbm.2, bf16[64,4096]{1,0:T(8,128)(2,1)} %val_hbm.2, bf16[64,4096]{1,0:T(8,128)(2,1)} %gate_hbm.1, bf16[64,1024]{1,0:T(8,128)(2,1)} %proj_hbm.2), custom_call_target="tpu_custom_call" | custom-call | flops 637534208 | bytes 4000000 | tf_op jit(solution)/shard_map/pack/pallas_call | solution.py:597
  3.2 0.0 copy-start
  3.2 11.5 %all-to-all-start = ((bf16[64,8,2432]{2,1,0:T(8,128)(2,1)}), bf16[64,8,2432]{2,1,0:T(8,128)(2,1)S(1)}, u32[]{:S(2)}, u32[]{:S(2)}) async-start(bf16[64,8,2432]{2,1,0:T(8,128)(2,1)} %bitcast.22), calls=%async_computation | async-start | bytes 4980736 | tf_op jit(solution)/shard_map/all_to_all | solution.py:579
  14.7 0.0 copy-done
  14.7 1.8 %eq.27 = pred[64,32,2]{2,1,0:T(8,128)(4,1)} reshape(pred[4096]{0:T(1024)(128)(4,1)S(1)} %shift-right-arithmetic_compare_fusion) | data formatting | bytes 8192 | tf_op jit(solution)/shard_map/eq | solution.py:612
  16.6 1.0 and.18
  17.6 2.0 %select_reduce_fusion = s32[64,2]{1,0:T(8,128)} fusion(s32[64,32,2]{2,1,0:T(8,128)S(1)} %and.18, pred[64,32,2]{2,1,0:T(8,128)(4,1)} %eq.27, s32[32,2]{1,0:T(8,128)S(1)} %multiply_add_fusion, s32[64]{0:T(128)} %param.25), kind=kLoop, calls=%fused_computation | loop fusion | flops 16256 | bytes 21504 | tf_op jit(solution)/shard_map/reduce_max | solution.py:614
  19.6 1.4 %reshape.49.at_ref.at_hbm = s32[1,128]{1,0:T(1,128)} reshape(s32[64,2]{1,0:T(8,128)} %select_reduce_fusion) | data formatting | bytes 1024 | tf_op jit(solution)/shard_map/reshape | solution.py:614
  21.0 0.9 eq.28
  21.9 1.5 %copy.23.step_ref.step_hbm = bf16[256,64]{1,0:T(8,128)(2,1)} copy(bf16[256,64]{0,1:T(8,128)(2,1)} %param.19) | data formatting | bytes 65536 | tf_op args[3]
  23.4 0.2 select_reduce_fusion.1.slot_ref
  23.6 24.8 %all-to-all-done = bf16[64,8,2432]{2,1,0:T(8,128)(2,1)S(1)} async-done(((bf16[64,8,2432]{2,1,0:T(8,128)(2,1)}), bf16[64,8,2432]{2,1,0:T(8,128)(2,1)S(1)}, u32[]{:S(2)}, u32[]{:S(2)}) %all-to-all-start) | async-done | bytes 2490400 | tf_op jit(solution)/shard_map/all_to_all | solution.py:579
  48.4 1.8 %rim.1 = bf16[16,5120]{1,0:T(8,128)(2,1)} custom-call(s32[3]{0:T(128)S(1)} %select_reduce_fusion.1.slot_ref, bf16[512,2432]{1,0:T(8,128)(2,1)S(1)} %bitcast.16, bf16[256,4096]{1,0:T(8,128)(2,1)} %val_hbm.3, bf16[256,1024]{1,0:T(8,128)(2,1)} %proj_hbm.3, s32[1,128]{1,0:T(1,128)} %reshape.49.at_ref.at_hbm, bf16[256,64]{1,0:T(8,128)(2,1)} %copy.23.step_ref.step_hbm), custom_call_target="tpu_custom_call" | custom-call | flops 7864320 | bytes 3000000 | tf_op jit(solution)/shard_map/rim/pallas_call | solution.py:623
  50.2 2.6 %collective-permute-start = (bf16[16,5120]{1,0:T(8,128)(2,1)}, bf16[16,5120]{1,0:T(8,128)(2,1)S(1)}, u32[]{:S(2)}, u32[]{:S(2)}) collective-permute-start(bf16[16,5120]{1,0:T(8,128)(2,1)} %rim.1), channel_id=1, source_target_pairs={{0,1},{1,2},{2,3},{3,4},{4,5},{5,6},{6,7},{7,8},{8,9},{9,10},{10,1... | collective-permute-start | bytes 491528 | tf_op jit(solution)/shard_map/ppermute | solution.py:634
  52.8 9.9 %place.1 = (bf16[256,4096]{1,0:T(8,128)(2,1)}, bf16[4,256,128]{2,1,0:T(8,128)(2,1)}, bf16[4,256,128]{2,1,0:T(8,128)(2,1)}, f32[512,512]{1,0:T(8,128)S(1)}, f32[2...) custom-call(bf16[512,2432]{1,0:T(8,128)(2,1)S(1)} %bitcast.17, ...), custom_call_target="tpu_custom_call" | custom-call | flops 1342177280 | bytes 10000000 | tf_op jit(solution)/shard_map/place/pallas_call | solution.py:636
  62.7 0.0 copy-start.1
  62.7 0.0 collective-permute-done.rim_ref
  62.7 3.2 %edge.1 = (bf16[512,640]{1,0:T(8,128)(2,1)}, bf16[16,4096]{1,0:T(8,128)(2,1)}, bf16[16,1024]{1,0:T(8,128)(2,1)}) custom-call(bf16[16,5120]{1,0:T(8,128)(2,1)S(1)} %collective-permute-done.rim_ref, bf16[16,4096]{1,0:T(8,128)(2,1)S(1)} %get-tuple-element.27.hv_ref, bf16[16,1024]{1,0:T(8,128)(2,1)S(1)} %get-tuple-element.28.hp_ref, f32[4,5120]{1,0:T(4,128)} %w_ref.1, ...), custom_call_target="tpu_custom_call" | custom-call | flops 8388608 | bytes 2000000 | tf_op jit(solution)/shard_map/edge/pallas_call | solution.py:660
  65.9 10.9 %all-to-all-start.1 = ((bf16[64,8,640]{2,1,0:T(8,128)(2,1)}), bf16[64,8,640]{2,1,0:T(8,128)(2,1)S(1)}, u32[]{:S(2)}, u32[]{:S(2)}) async-start(bf16[64,8,640]{2,1,0:T(8,128)(2,1)} %bitcast.23), calls=%async_computation.1 | async-start | bytes 1310720 | tf_op jit(solution)/shard_map/all_to_all | solution.py:579
  76.8 0.0 copy-done.1
  76.8 0.7 copy.25
  77.5 7.8 %local0.1 = (bf16[256,2048]{1,0:T(8,128)(2,1)}, bf16[256,2048]{1,0:T(8,128)(2,1)}, bf16[4,256,64]{2,1,0:T(8,128)(2,1)}, f32[8,128]{1,0:T(8,128)S(1)}) custom-call(bf16[512,2432]{1,0:T(8,128)(2,1)S(1)} %bitcast.18, s32[1,128]{1,0:T(1,128)} %reshape.49.at_ref.at_hbm, bf16[256,4096]{1,0:T(8,128)(2,1)} %gate_ref.3, ...), custom_call_target="tpu_custom_call" | custom-call | flops 6000000000 | bytes 8000000 | tf_op jit(solution)/shard_map/local0/pallas_call | solution.py:679
  85.3 5.0 %all-to-all-done.1 = bf16[64,8,640]{2,1,0:T(8,128)(2,1)S(1)} async-done(((bf16[64,8,640]{2,1,0:T(8,128)(2,1)}), bf16[64,8,640]{2,1,0:T(8,128)(2,1)S(1)}, u32[]{:S(2)}, u32[]{:S(2)}) %all-to-all-start.1) | async-done | bytes 655392 | tf_op jit(solution)/shard_map/all_to_all | solution.py:579
  90.4 2.1 %scan.1 = (bf16[512,512]{1,0:T(8,128)(2,1)}, f32[8,128]{1,0:T(8,128)S(1)}) custom-call(s32[1]{0:T(128)} %bitcast.dev_ref, bf16[512,640]{1,0:T(8,128)(2,1)S(1)} %bitcast.20, f32[8,128]{1,0:T(8,128)S(1)} %get-tuple-element.40.after_ref), custom_call_target="tpu_custom_call" | custom-call | flops 67108864 | bytes 1200000 | tf_op jit(solution)/shard_map/scan/pallas_call | solution.py:697
  92.5 5.2 %all-to-all-start.2 = ((bf16[64,8,512]{2,1,0:T(8,128)(2,1)}), bf16[64,8,512]{2,1,0:T(8,128)(2,1)S(1)}, u32[]{:S(2)}, u32[]{:S(2)}) async-start(bf16[64,8,512]{2,1,0:T(8,128)(2,1)} %bitcast.24), calls=%async_computation.2 | async-start | bytes 1048576 | tf_op jit(solution)/shard_map/all_to_all | solution.py:579
  97.6 7.7 %local1.1 = (bf16[256,2048]{1,0:T(8,128)(2,1)}, bf16[256,2048]{1,0:T(8,128)(2,1)}, bf16[4,256,64]{2,1,0:T(8,128)(2,1)}, f32[8,128]{1,0:T(8,128)}) custom-call(bf16[512,2432]{1,0:T(8,128)(2,1)S(1)} %bitcast.19, s32[1,128]{1,0:T(1,128)} %reshape.49.at_ref.at_hbm, bf16[256,4096]{1,0:T(8,128)(2,1)} %gate_ref.3, bf16[256,4096]{1,0:T(8,128)(2,1)} %get-tuple-element.33.conv_ref, ...), custom_call_target="tpu_custom_call" | custom-call | flops 6000000000 | bytes 8000000 | tf_op jit(solution)/shard_map/local1/pallas_call | solution.py:679
  105.4 4.1 %all-to-all-done.2 = bf16[64,8,512]{2,1,0:T(8,128)(2,1)S(1)} async-done(((bf16[64,8,512]{2,1,0:T(8,128)(2,1)}), bf16[64,8,512]{2,1,0:T(8,128)(2,1)S(1)}, u32[]{:S(2)}, u32[]{:S(2)}) %all-to-all-start.2) | async-done | bytes 524320 | tf_op jit(solution)/shard_map/all_to_all | solution.py:579
  109.5 6.0 %final.1 = bf16[256,4096]{1,0:T(8,128)(2,1)} custom-call(f32[8,128]{1,0:T(8,128)S(1)} %get-tuple-element.41.rest_0_.bound_ref, bf16[512,512]{1,0:T(8,128)(2,1)S(1)} %bitcast.21, f32[1,4096]{1,0:T(1,128)} %bitcast.30, bf16[4,256,64]{2,1,0:T(8,128)(2,1)} %get-tuple-element.43.qe_hbm, bf16[4,256,64]{2,1,0:T(8,128)(2,1)} %get-tuple-element.44.qo_hbm, ...), custom_call_target="tpu_custom_call" | custom-call | flops 134217728 | bytes 11000000 | tf_op jit(solution)/shard_map/final/pallas_call | solution.py:710
  (5 shorter events, 0.0 us)
Async XLA Ops:
  3.2 11.5 %copy-start = (s32[4096]{0:T(1024)S(1)}, s32[4096]{0:T(1024)}, u32[]{:S(2)}) copy-start(s32[4096]{0:T(1024)} %param.24) | copy-start | bytes 49156
  3.2 45.2 %all-to-all-start = ((bf16[64,8,2432]{2,1,0:T(8,128)(2,1)}), bf16[64,8,2432]{2,1,0:T(8,128)(2,1)S(1)}, u32[]{:S(2)}, u32[]{:S(2)}) async-start(bf16[64,8,2432]{2,1,0:T(8,128)(2,1)} %bitcast.22), calls=%async_computation | async-start | bytes 4980736 | tf_op jit(solution)/shard_map/all_to_all | solution.py:579
  50.2 12.6 %collective-permute-start = (bf16[16,5120]{1,0:T(8,128)(2,1)}, bf16[16,5120]{1,0:T(8,128)(2,1)S(1)}, u32[]{:S(2)}, u32[]{:S(2)}) collective-permute-start(bf16[16,5120]{1,0:T(8,128)(2,1)} %rim.1), channel_id=1, source_target_pairs={{0,1},{1,2},{2,3},{3,4},{4,5},{5,6},{6,7},{7,8},{8,9},{9,10},{10,1... | collective-permute-start | bytes 491528 | tf_op jit(solution)/shard_map/ppermute | solution.py:634
  62.7 14.1 %copy-start.1 = (f32[256,128]{1,0:T(8,128)S(1)}, f32[256,128]{1,0:T(8,128)}, u32[]{:S(2)}) copy-start(f32[256,128]{1,0:T(8,128)} %get-tuple-element.38.cum_ref) | copy-start | bytes 393220
  65.9 24.5 %all-to-all-start.1 = ((bf16[64,8,640]{2,1,0:T(8,128)(2,1)}), bf16[64,8,640]{2,1,0:T(8,128)(2,1)S(1)}, u32[]{:S(2)}, u32[]{:S(2)}) async-start(bf16[64,8,640]{2,1,0:T(8,128)(2,1)} %bitcast.23), calls=%async_computation.1 | async-start | bytes 1310720 | tf_op jit(solution)/shard_map/all_to_all | solution.py:579
  92.5 17.0 %all-to-all-start.2 = ((bf16[64,8,512]{2,1,0:T(8,128)(2,1)}), bf16[64,8,512]{2,1,0:T(8,128)(2,1)S(1)}, u32[]{:S(2)}, u32[]{:S(2)}) async-start(bf16[64,8,512]{2,1,0:T(8,128)(2,1)} %bitcast.24), calls=%async_computation.2 | async-start | bytes 1048576 | tf_op jit(solution)/shard_map/all_to_all | solution.py:579

commit v3 on v2

--- a/solution.py
+++ b/solution.py
@@ -22,8 +22,9 @@
 EDGE = 16
 LANES = 128
 QUART = 4
-V_AT, G_AT, P_AT, S_AT = 0, 1024, 2048, 2304
-CHUNK = 2432
+V_AT, P_AT, S_AT = 0, 1024, 1280
+CHUNK = 1408
+G_CHUNK = 1024
 STATE_W = GW + LANES
 
 f32 = jnp.float32
@@ -83,44 +84,55 @@
     return jnp.where(head == col, 1.0, 0.0).astype(bf16)
 
 
-def pack_kernel(
-    pos_hbm, step_hbm, val_hbm, gate_hbm, proj_hbm, out_hbm,
-    pos_ref, step_ref, val_ref, gate_ref, proj_ref, out_ref, in_sem, out_sem,
-):
-    pairs = ((val_hbm, val_ref), (gate_hbm, gate_ref), (proj_hbm, proj_ref), (pos_hbm, pos_ref), (step_hbm, step_ref))
-    loads = [pltpu.make_async_copy(src, dst, in_sem.at[i]) for i, (src, dst) in enumerate(pairs)]
-    for load in (loads[3], loads[4], loads[0], loads[1], loads[2]):
-        load.start()
+def slot_keys(pos_ref):
     dev = lax.axis_index("ctx")
-    loads[3].wait()
-    loads[4].wait()
     row = pos_ref[pl.ds(dev // 2, 1), :]
     other = pltpu.roll(row, 64, 1)
     lane = iota((1, LANES), 1)
     own = jnp.where((lane >> 6) == lax.rem(dev, 2), row, other)
     key = (own >> 8) * 8 + (lane & 1) * QUART + (lane >> 6)
     keys = jnp.concatenate([key, key + 2], axis=1)
-    pick = jnp.where(iota((DEVS * 8, 2 * LANES), 0) == keys, 1.0, 0.0).astype(bf16)
+    return jnp.where(iota((DEVS * 8, 2 * LANES), 0) == keys, 1.0, 0.0).astype(bf16)
+
+
+def quarters(ref, width, low, count):
+    return jnp.concatenate([ref[:, b * width + low : b * width + low + count] for b in range(QUART)], axis=0)
+
+
+def pack_kernel(
+    pos_hbm, step_hbm, val_hbm, proj_hbm, out_hbm,
+    pos_ref, step_ref, val_ref, proj_ref, out_ref, in_sem, out_sem,
+):
+    pairs = ((pos_hbm, pos_ref), (step_hbm, step_ref), (proj_hbm, proj_ref), (val_hbm, val_ref))
+    loads = [pltpu.make_async_copy(src, dst, in_sem.at[i]) for i, (src, dst) in enumerate(pairs)]
+    for load in loads:
+        load.start()
+    loads[0].wait()
+    pick = slot_keys(pos_ref)
+    loads[1].wait()
     step = step_ref[...]
     out_ref[:, S_AT:] = dot(pick[:, :TILE], jnp.concatenate([step, step], axis=1)).astype(bf16)
+    loads[2].wait()
+    out_ref[:, P_AT:S_AT] = dot(pick, quarters(proj_ref, 256, 0, 256)).astype(bf16)
+    loads[3].wait()
     stores = []
-    for i, (ref, at, width, part) in enumerate(
-        ((val_ref, V_AT, 1024, 512), (gate_ref, G_AT, 1024, 512), (proj_ref, P_AT, 256, 256))
-    ):
-        loads[i].wait()
-        for low in range(0, width, part):
-            rows = [ref[:, b * width + low : b * width + low + part] for b in range(QUART)]
-            out_ref[:, at + low : at + low + part] = dot(pick, jnp.concatenate(rows, axis=0)).astype(bf16)
-            end = at + low + part if i < 2 else CHUNK
-            cols = slice(at + low, end)
-            store = pltpu.make_async_copy(out_ref.at[:, cols], out_hbm.at[:, cols], out_sem.at[len(stores)])
-            store.start()
-            stores.append(store)
+    for i, (low, high) in enumerate(((P_AT, CHUNK), (0, GW), (GW, 2 * GW))):
+        if i:
+            out_ref[:, low:high] = dot(pick, quarters(val_ref, 1024, low, GW)).astype(bf16)
+        store = pltpu.make_async_copy(out_ref.at[:, low:high], out_hbm.at[:, low:high], out_sem.at[i])
+        store.start()
+        stores.append(store)
     for store in stores:
         store.wait()
 
 
-def rim_kernel(slot_ref, recv_ref, val_ref, proj_ref, at_ref, step_ref, out_ref):
+def gate_kernel(pos_ref, gate_ref, at_ref, step_ref, slot_ref, out_ref):
+    pick = slot_keys(pos_ref)
+    for low in (0, GW):
+        out_ref[:, low : low + GW] = dot(pick, quarters(gate_ref, 1024, low, GW)).astype(bf16)
+
+
+def rim_kernel(slot_ref, recv_ref, val_ref, proj_ref, out_ref):
     count = KCONV - 1
     slots = [slot_ref[i] for i in range(count)]
     starts = [jnp.maximum(k, 0) * QUART for k in slots]
@@ -134,7 +146,7 @@
         taken = jnp.where(iota((EDGE, 1), 0) == EDGE - count + i, slots[i], taken)
     for b in range(QUART):
         place = jnp.where(col == at + b, 1.0, 0.0).astype(bf16)
-        tile = dot(place, rows[:, V_AT:G_AT])
+        tile = dot(place, rows[:, V_AT:P_AT])
         cols = slice(b * 1024, (b + 1) * 1024)
         out_ref[:, cols] = jnp.where(taken >= 0, tile, val_ref[:, cols].astype(f32)).astype(bf16)
         tile = dot(place, rows[:, P_AT:S_AT])
@@ -594,19 +606,19 @@
     hbm = pl.BlockSpec(memory_space=pl.ANY)
     vmem = pl.BlockSpec(memory_space=pltpu.VMEM)
     sems = pltpu.SemaphoreType.DMA
+    positions = tile_position.reshape(32, LANES)
     packed = call(
         pack_kernel,
         struct(DEVS * 8, CHUNK),
         (1,),
-        [hbm] * 5,
+        [hbm] * 4,
         hbm,
-        scratch=[pltpu.VMEM((32, LANES), jnp.int32), pltpu.VMEM((TILE, H), bf16), pltpu.VMEM((TILE, E), bf16), pltpu.VMEM((TILE, E), bf16), pltpu.VMEM((TILE, PW), bf16),
-                 pltpu.VMEM((DEVS * 8, CHUNK), bf16), sems((5,)), sems((5,))],
-        est=cost(2 * 512 * 256 * CHUNK, 4_000_000),
+        scratch=[pltpu.VMEM((32, LANES), jnp.int32), pltpu.VMEM((TILE, H), bf16), pltpu.VMEM((TILE, E), bf16),
+                 pltpu.VMEM((TILE, PW), bf16), pltpu.VMEM((DEVS * 8, CHUNK), bf16), sems((4,)), sems((3,))],
+        est=cost(2 * 512 * 256 * CHUNK, 3_000_000),
         name="pack",
-    )(far(tile_position.reshape(32, LANES)), far(tile_step), far(tile_values), far(tile_gate), far(tile_proj))
-    recv = kept(exchange(packed))
-
+    )(far(positions), far(tile_step), far(tile_values), far(tile_proj))
+    recv = exchange(packed)
     position = tile_position.reshape(DEVS, TILE)
     ids = jnp.arange(TILE, dtype=jnp.int32)
     landing = ((position >> 8) == device) & (ids[None, :] < tile_count[:, None])
@@ -616,6 +628,19 @@
     rim_slot = jnp.max(jnp.where(at == ends, jnp.arange(2 * DEVS)[None, :], -1), axis=1)
     at = far(at)
     steps = far(text_step)
+    gates = call(
+        gate_kernel,
+        struct(DEVS * 8, G_CHUNK),
+        (1,),
+        [whole((32, LANES)), whole((TILE, E)), hbm, hbm, hbm],
+        whole((DEVS * 8, G_CHUNK)),
+        est=cost(2 * 512 * 256 * G_CHUNK, 2_000_000),
+        name="gates",
+    )(far(positions), far(tile_gate), at, steps, rim_slot)
+    gates, recv = lax.optimization_barrier((gates, recv))
+    recv = kept(recv)
+    recv_gate = exchange(gates)
+
     bias = conv_bias[None, :]
 
     recv_spec = whole((DEVS * 8, CHUNK))
@@ -626,11 +651,11 @@
         (1,),
         [scalar, vmem,
          pl.BlockSpec((EDGE, E), lambda i: (TOK // EDGE - 1, 0)),
-         pl.BlockSpec((EDGE, PW), lambda i: (TOK // EDGE - 1, 0)), hbm, hbm],
+         pl.BlockSpec((EDGE, PW), lambda i: (TOK // EDGE - 1, 0))],
         whole((EDGE, E + PW)),
         est=cost(2 * 16 * 48 * 5120, 3_000_000),
         name="rim",
-    )(rim_slot, recv, far(text_values), far(text_proj), at, steps)
+    )(rim_slot, recv, far(text_values), far(text_proj))
     rim = lax.ppermute(rim, "ctx", [(i, i + 1) for i in range(DEVS - 1)])
 
     conv, inputs, outputs, state, cum, size, total, head_v, head_p, tail = call(
@@ -667,6 +692,7 @@
         est=cost(2 * 64 * 16 * 4096, 2_000_000, 100_000),
         name="edge",
     )(kept(rim), kept(head_v), kept(head_p), far(conv_weight), far(bias), kept(tail), kept(total), kept(state))
+    send, recv_gate = lax.optimization_barrier((send, recv_gate))
     states = kept(exchange(send))
 
     by_head = cum[:, :H].T.reshape(G, H // G, TOK)
@@ -680,7 +706,7 @@
             functools.partial(local_kernel, odd),
             (struct(TOK, E // 2), struct(TOK, E // 2), struct(G // 2, TOK, N), near(8, LANES, dtype=f32)),
             (G // 2,),
-            [pl.BlockSpec((DEVS * 8, GW), lambda i: (0, G_AT // GW + odd)), at_spec, cols, cols,
+            [pl.BlockSpec((DEVS * 8, GW), lambda i: (0, odd)), at_spec, cols, cols,
              pl.BlockSpec((EDGE, GW), lambda i: (0, 2 * i + odd)), per_pair, per_pair,
              pl.BlockSpec((EDGE, LANES), lambda i: (0, i)), pl.BlockSpec((EDGE, LANES), lambda i: (0, G // 2 + i)),
              whole((TOK, LANES)), pl.BlockSpec((1, H // G, TOK), lambda i: (2 * i + odd, 0, 0)),
@@ -691,7 +717,7 @@
                      pltpu.VMEM((TOK, GW), f32), pltpu.VMEM((TOK, GW), f32)],
             est=cost(6_000_000_000, 8_000_000, 2_000_000),
             name=f"local{odd}",
-        )(recv, at, far(text_gate), *map(far, (conv, edge, inputs, outputs, edge_p, edge_p, cum, by_head, size, skip_gain[None, :])), *more)
+        )(recv_gate, at, far(text_gate), *map(far, (conv, edge, inputs, outputs, edge_p, edge_p, cum, by_head, size, skip_gain[None, :])), *more)
 
     even = rows_own(0, ())
     entries, bound = call(

time: 116 us -> 110 us (0.948)
  waiting for transfers between devices: 34 us -> 25 us
  starting transfers between devices: 30.2 us -> 34.9 us
  local copies, waits for them, and re-layouts: 7.32 us -> 4.47 us
  Pallas kernels: 41.7 us -> 43.9 us
  other arithmetic: 2.22 us -> 0.66 us
    all_to_all x3 -> x4, waiting for transfers between devices: 34 us -> 25 us  [exchange(): return lax.all_to_all(rows, 'ctx', split_axis=0, concat_axis=0, tiled=True)]
    all_to_all x3 -> x4, starting transfers between devices: 27.6 us -> 31.5 us  [exchange(): return lax.all_to_all(rows, 'ctx', split_axis=0, concat_axis=0, tiled=True)]
    pallas_call x1 -> x2, Pallas kernels: 3.16 us -> 5.33 us  [the longest x1 2.8 us: shards(): call(pack_kernel, struct(DEVS * 8, CHUNK), (1,), [hbm] * 4, hbm, scratch=...]
    reduce_max x1, other arithmetic: 2.01 us -> 0.45 us  [shards(): at = jnp.max(local.reshape(DEVS, TILE // 2, 2), axis=1).reshape(1, 2 * DEVS)]
  transfers between devices with their start and end apart: 4 -> 5, of which waited for: 3 -> 3; matrix products, arithmetic and copies ran while one was open for 8% -> 5% of each run, Pallas kernels for 22% -> 30%
where the time goes in v3:
time: 110 us; the launch traced here: 109 us
  Pallas kernels  43.9 us (40%)
  starting transfers between devices  34.9 us (32%)
  waiting for transfers between devices  25 us (23%)
  local copies, waits for them, and re-layouts  4.47 us (4%)
    all_to_all x4, starting transfers between devices, exchange(): return lax.all_to_all(rows, 'ctx', split_axis=0, concat_axis=0, tiled=True)  31.5 us
    all_to_all x4, waiting for transfers between devices, exchange(): return lax.all_to_all(rows, 'ctx', split_axis=0, concat_axis=0, tiled=True)  25 us
    pallas_call x2, Pallas kernels, rows_own(): call(functools.partial(local_kernel, odd), (struct(TOK, E // 2), struct(T...  15.6 us
    pallas_call x1, Pallas kernels, shards(): call(place_kernel, (struct(TOK, E), struct(G // 2, TOK, LANES), struct(G...  9.93 us
    pallas_call x1, Pallas kernels, shards(): call(final_kernel, struct(TOK, E), (1,), [vmem, vmem] + [hbm] * 7, hbm, s...  6 us
    ppermute x1, starting transfers between devices, shards(): rim = lax.ppermute(rim, 'ctx', [(i, i + 1) for i in range(DEVS - 1)])  3.47 us
    pallas_call x1, Pallas kernels, shards(): call(edge_kernel, (struct(G * N, STATE_W), struct(EDGE, E), struct(EDGE,...  3.16 us
    pallas_call x1, Pallas kernels, shards(): call(pack_kernel, struct(DEVS * 8, CHUNK), (1,), [hbm] * 4, hbm, scratch=...  2.8 us
  transfers between devices with their start and end apart: 5, of which 3 were waited for; matrix products, arithmetic and copies ran while one was open for 5% of the time, Pallas kernels for 30%

profile of v3, /device:TPU:0, one launch (start us, length us, event | category | flops | bytes accessed | tf_op | source)
XLA Modules:
  0.0 109.3 jit_solution(17619543380904342156)
XLA Ops:
  0.0 0.0 copy-start
  0.0 2.8 %pack.1 = bf16[512,1408]{1,0:T(8,128)(2,1)} custom-call(s32[32,128]{1,0:T(8,128)} %bitcast.28, bf16[64,64]{1,0:T(8,128)(2,1)} %step_hbm.2, bf16[64,4096]{1,0:T(8,128)(2,1)} %val_hbm.2, bf16[64,1024]{1,0:T(8,128)(2,1)} %proj_hbm.2), custom_call_target="tpu_custom_call" | custom-call | flops 369098752 | bytes 3000000 | tf_op jit(solution)/shard_map/pack/pallas_call | solution.py:610
  2.8 0.0 copy-start.3
  2.8 11.5 %all-to-all-start = ((bf16[64,8,1408]{2,1,0:T(8,128)(2,1)}), bf16[64,8,1408]{2,1,0:T(8,128)(2,1)S(1)}, u32[]{:S(2)}, u32[]{:S(2)}) async-start(bf16[64,8,1408]{2,1,0:T(8,128)(2,1)} %bitcast.24), calls=%async_computation | async-start | bytes 2883584 | tf_op jit(solution)/shard_map/all_to_all | solution.py:591
  14.3 0.0 copy-start.2
  14.4 0.0 copy-done
  14.4 1.1 %eq.27 = pred[64,32,2]{2,1,0:T(8,128)(4,1)S(1)} reshape(pred[4096]{0:T(1024)(128)(4,1)S(1)} %shift-right-arithmetic_compare_fusion) | data formatting | bytes 8192 | tf_op jit(solution)/shard_map/eq | solution.py:624
  15.5 1.0 and.18
  16.6 0.0 copy-done.3
  16.6 0.4 select_reduce_fusion
  17.0 0.7 reshape.51.at_ref.at_hbm
  17.7 0.1 eq.28
  17.9 0.0 copy-done.2
  17.9 0.7 copy.23.step_ref.step_hbm
  18.6 0.2 select_reduce_fusion.1.slot_ref
  18.8 2.5 %gates.1 = bf16[512,1024]{1,0:T(8,128)(2,1)} custom-call(s32[32,128]{1,0:T(8,128)} %bitcast.29, bf16[64,4096]{1,0:T(8,128)(2,1)} %gate_ref.3, s32[1,128]{1,0:T(1,128)} %reshape.51.at_ref.at_hbm, bf16[256,64]{1,0:T(8,128)(2,1)} %copy.23.step_ref.step_hbm, s32[3]{0:T(128)S(1)} %select_reduce_fusion.1.slot_ref), custom_call_target="tpu_custom_call" | custom-call | flops 268435456 | bytes 2000000 | tf_op jit(solution)/shard_map/gates/pallas_call | solution.py:631
  21.3 15.8 %all-to-all-done = bf16[64,8,1408]{2,1,0:T(8,128)(2,1)S(1)} async-done(((bf16[64,8,1408]{2,1,0:T(8,128)(2,1)}), bf16[64,8,1408]{2,1,0:T(8,128)(2,1)S(1)}, u32[]{:S(2)}, u32[]{:S(2)}) %all-to-all-start) | async-done | bytes 1441824 | tf_op jit(solution)/shard_map/all_to_all | solution.py:591
  37.1 4.8 %all-to-all-start.1 = ((bf16[64,8,1024]{2,1,0:T(8,128)(2,1)}), bf16[64,8,1024]{2,1,0:T(8,128)(2,1)S(1)}, u32[]{:S(2)}, u32[]{:S(2)}) async-start(bf16[64,8,1024]{2,1,0:T(8,128)(2,1)} %bitcast.25), calls=%async_computation.1 | async-start | bytes 2097152 | tf_op jit(solution)/shard_map/all_to_all | solution.py:591
  41.9 1.8 %rim.1 = bf16[16,5120]{1,0:T(8,128)(2,1)} custom-call(s32[3]{0:T(128)S(1)} %select_reduce_fusion.1.slot_ref, bf16[512,1408]{1,0:T(8,128)(2,1)S(1)} %bitcast.18, bf16[256,4096]{1,0:T(8,128)(2,1)} %val_hbm.3, bf16[256,1024]{1,0:T(8,128)(2,1)} %proj_hbm.3), custom_call_target="tpu_custom_call" | custom-call | flops 7864320 | bytes 3000000 | tf_op jit(solution)/shard_map/rim/pallas_call | solution.py:648
  43.7 3.5 %collective-permute-start = (bf16[16,5120]{1,0:T(8,128)(2,1)}, bf16[16,5120]{1,0:T(8,128)(2,1)S(1)}, u32[]{:S(2)}, u32[]{:S(2)}) collective-permute-start(bf16[16,5120]{1,0:T(8,128)(2,1)} %rim.1), channel_id=1, source_target_pairs={{0,1},{1,2},{2,3},{3,4},{4,5},{5,6},{6,7},{7,8},{8,9},{9,10},{10,1... | collective-permute-start | bytes 491528 | tf_op jit(solution)/shard_map/ppermute | solution.py:659
  47.2 9.9 %place.1 = (bf16[256,4096]{1,0:T(8,128)(2,1)}, bf16[4,256,128]{2,1,0:T(8,128)(2,1)}, bf16[4,256,128]{2,1,0:T(8,128)(2,1)}, f32[512,512]{1,0:T(8,128)S(1)}, f32[2...) custom-call(bf16[512,1408]{1,0:T(8,128)(2,1)S(1)} %bitcast.19, ...), custom_call_target="tpu_custom_call" | custom-call | flops 1342177280 | bytes 10000000 | tf_op jit(solution)/shard_map/place/pallas_call | solution.py:661
  57.1 0.0 copy-start.1
  57.1 0.0 collective-permute-done.rim_ref
  57.2 3.2 %edge.1 = (bf16[512,640]{1,0:T(8,128)(2,1)}, bf16[16,4096]{1,0:T(8,128)(2,1)}, bf16[16,1024]{1,0:T(8,128)(2,1)}) custom-call(bf16[16,5120]{1,0:T(8,128)(2,1)S(1)} %collective-permute-done.rim_ref, bf16[16,4096]{1,0:T(8,128)(2,1)S(1)} %get-tuple-element.32.hv_ref, bf16[16,1024]{1,0:T(8,128)(2,1)S(1)} %get-tuple-element.33.hp_ref, f32[4,5120]{1,0:T(4,128)} %w_ref.1, ...), custom_call_target="tpu_custom_call" | custom-call | flops 8388608 | bytes 2000000 | tf_op jit(solution)/shard_map/edge/pallas_call | solution.py:685
  60.3 0.0 all-to-all-done.1
  60.3 10.1 %all-to-all-start.2 = ((bf16[64,8,640]{2,1,0:T(8,128)(2,1)}), bf16[64,8,640]{2,1,0:T(8,128)(2,1)S(1)}, u32[]{:S(2)}, u32[]{:S(2)}) async-start(bf16[64,8,640]{2,1,0:T(8,128)(2,1)} %bitcast.26), calls=%async_computation.2 | async-start | bytes 1310720 | tf_op jit(solution)/shard_map/all_to_all | solution.py:591
  70.4 0.0 copy-done.1
  70.5 0.7 copy.25
  71.2 7.8 %local0.1 = (bf16[256,2048]{1,0:T(8,128)(2,1)}, bf16[256,2048]{1,0:T(8,128)(2,1)}, bf16[4,256,64]{2,1,0:T(8,128)(2,1)}, f32[8,128]{1,0:T(8,128)S(1)}) custom-call(bf16[512,1024]{1,0:T(8,128)(2,1)S(1)} %bitcast.22, s32[1,128]{1,0:T(1,128)} %reshape.51.at_ref.at_hbm, bf16[256,4096]{1,0:T(8,128)(2,1)} %gate_ref.5, ...), custom_call_target="tpu_custom_call" | custom-call | flops 6000000000 | bytes 8000000 | tf_op jit(solution)/shard_map/local0/pallas_call | solution.py:705
  79.0 5.1 %all-to-all-done.2 = bf16[64,8,640]{2,1,0:T(8,128)(2,1)S(1)} async-done(((bf16[64,8,640]{2,1,0:T(8,128)(2,1)}), bf16[64,8,640]{2,1,0:T(8,128)(2,1)S(1)}, u32[]{:S(2)}, u32[]{:S(2)}) %all-to-all-start.2) | async-done | bytes 655392 | tf_op jit(solution)/shard_map/all_to_all | solution.py:591
  84.1 2.1 %scan.1 = (bf16[512,512]{1,0:T(8,128)(2,1)}, f32[8,128]{1,0:T(8,128)S(1)}) custom-call(s32[1]{0:T(128)} %bitcast.dev_ref, bf16[512,640]{1,0:T(8,128)(2,1)S(1)} %bitcast.20, f32[8,128]{1,0:T(8,128)S(1)} %get-tuple-element.48.after_ref), custom_call_target="tpu_custom_call" | custom-call | flops 67108864 | bytes 1200000 | tf_op jit(solution)/shard_map/scan/pallas_call | solution.py:723
  86.2 5.0 %all-to-all-start.3 = ((bf16[64,8,512]{2,1,0:T(8,128)(2,1)}), bf16[64,8,512]{2,1,0:T(8,128)(2,1)S(1)}, u32[]{:S(2)}, u32[]{:S(2)}) async-start(bf16[64,8,512]{2,1,0:T(8,128)(2,1)} %bitcast.27), calls=%async_computation.3 | async-start | bytes 1048576 | tf_op jit(solution)/shard_map/all_to_all | solution.py:591
  91.3 7.8 %local1.1 = (bf16[256,2048]{1,0:T(8,128)(2,1)}, bf16[256,2048]{1,0:T(8,128)(2,1)}, bf16[4,256,64]{2,1,0:T(8,128)(2,1)}, f32[8,128]{1,0:T(8,128)}) custom-call(bf16[512,1024]{1,0:T(8,128)(2,1)S(1)} %bitcast.23, s32[1,128]{1,0:T(1,128)} %reshape.51.at_ref.at_hbm, bf16[256,4096]{1,0:T(8,128)(2,1)} %gate_ref.5, bf16[256,4096]{1,0:T(8,128)(2,1)} %get-tuple-element.41.conv_ref, ...), custom_call_target="tpu_custom_call" | custom-call | flops 6000000000 | bytes 8000000 | tf_op jit(solution)/shard_map/local1/pallas_call | solution.py:705
  99.0 4.1 %all-to-all-done.3 = bf16[64,8,512]{2,1,0:T(8,128)(2,1)S(1)} async-done(((bf16[64,8,512]{2,1,0:T(8,128)(2,1)}), bf16[64,8,512]{2,1,0:T(8,128)(2,1)S(1)}, u32[]{:S(2)}, u32[]{:S(2)}) %all-to-all-start.3) | async-done | bytes 524320 | tf_op jit(solution)/shard_map/all_to_all | solution.py:591
  103.1 6.0 %final.1 = bf16[256,4096]{1,0:T(8,128)(2,1)} custom-call(f32[8,128]{1,0:T(8,128)S(1)} %get-tuple-element.49.rest_0_.bound_ref, bf16[512,512]{1,0:T(8,128)(2,1)S(1)} %bitcast.21, f32[1,4096]{1,0:T(1,128)} %bitcast.34, bf16[4,256,64]{2,1,0:T(8,128)(2,1)} %get-tuple-element.51.qe_hbm, bf16[4,256,64]{2,1,0:T(8,128)(2,1)} %get-tuple-element.52.qo_hbm, ...), custom_call_target="tpu_custom_call" | custom-call | flops 134217728 | bytes 11000000 | tf_op jit(solution)/shard_map/final/pallas_call | solution.py:736
  (5 shorter events, 0.0 us)
Async XLA Ops:
  0.0 14.4 %copy-start = (s32[4096]{0:T(1024)S(1)}, s32[4096]{0:T(1024)}, u32[]{:S(2)}) copy-start(s32[4096]{0:T(1024)} %param.24) | copy-start | bytes 49156
  2.8 13.7 %copy-start.3 = (s32[64]{0:T(128)S(1)}, s32[64]{0:T(128)}, u32[]{:S(2)}) copy-start(s32[64]{0:T(128)} %param.25) | copy-start | bytes 772
  2.8 34.3 %all-to-all-start = ((bf16[64,8,1408]{2,1,0:T(8,128)(2,1)}), bf16[64,8,1408]{2,1,0:T(8,128)(2,1)S(1)}, u32[]{:S(2)}, u32[]{:S(2)}) async-start(bf16[64,8,1408]{2,1,0:T(8,128)(2,1)} %bitcast.24), calls=%async_computation | async-start | bytes 2883584 | tf_op jit(solution)/shard_map/all_to_all | solution.py:591
  14.3 3.5 %copy-start.2 = (bf16[256,64]{0,1:T(8,128)(2,1)S(1)}, bf16[256,64]{0,1:T(8,128)(2,1)}, u32[]{:S(2)}) copy-start(bf16[256,64]{0,1:T(8,128)(2,1)} %param.19) | copy-start | bytes 98308
  37.1 23.2 %all-to-all-start.1 = ((bf16[64,8,1024]{2,1,0:T(8,128)(2,1)}), bf16[64,8,1024]{2,1,0:T(8,128)(2,1)S(1)}, u32[]{:S(2)}, u32[]{:S(2)}) async-start(bf16[64,8,1024]{2,1,0:T(8,128)(2,1)} %bitcast.25), calls=%async_computation.1 | async-start | bytes 2097152 | tf_op jit(solution)/shard_map/all_to_all | solution.py:591
  43.7 13.4 %collective-permute-start = (bf16[16,5120]{1,0:T(8,128)(2,1)}, bf16[16,5120]{1,0:T(8,128)(2,1)S(1)}, u32[]{:S(2)}, u32[]{:S(2)}) collective-permute-start(bf16[16,5120]{1,0:T(8,128)(2,1)} %rim.1), channel_id=1, source_target_pairs={{0,1},{1,2},{2,3},{3,4},{4,5},{5,6},{6,7},{7,8},{8,9},{9,10},{10,1... | collective-permute-start | bytes 491528 | tf_op jit(solution)/shard_map/ppermute | solution.py:659
  57.1 13.3 %copy-start.1 = (f32[256,128]{1,0:T(8,128)S(1)}, f32[256,128]{1,0:T(8,128)}, u32[]{:S(2)}) copy-start(f32[256,128]{1,0:T(8,128)} %get-tuple-element.46.cum_ref) | copy-start | bytes 393220
  60.3 23.8 %all-to-all-start.2 = ((bf16[64,8,640]{2,1,0:T(8,128)(2,1)}), bf16[64,8,640]{2,1,0:T(8,128)(2,1)S(1)}, u32[]{:S(2)}, u32[]{:S(2)}) async-start(bf16[64,8,640]{2,1,0:T(8,128)(2,1)} %bitcast.26), calls=%async_computation.2 | async-start | bytes 1310720 | tf_op jit(solution)/shard_map/all_to_all | solution.py:591
  86.2 16.9 %all-to-all-start.3 = ((bf16[64,8,512]{2,1,0:T(8,128)(2,1)}), bf16[64,8,512]{2,1,0:T(8,128)(2,1)S(1)}, u32[]{:S(2)}, u32[]{:S(2)}) async-start(bf16[64,8,512]{2,1,0:T(8,128)(2,1)} %bitcast.27), calls=%async_computation.3 | async-start | bytes 1048576 | tf_op jit(solution)/shard_map/all_to_all | solution.py:591

commit v4 on v3

--- a/solution.py
+++ b/solution.py
@@ -25,6 +25,7 @@
 V_AT, P_AT, S_AT = 0, 1024, 1280
 CHUNK = 1408
 G_CHUNK = 1024
+RIM_W = 1024
 STATE_W = GW + LANES
 
 f32 = jnp.float32
@@ -144,16 +145,25 @@
     for i, k in enumerate(starts):
         at = jnp.where(row == EDGE - count + i, 16 * i + (k & 15), at)
         taken = jnp.where(iota((EDGE, 1), 0) == EDGE - count + i, slots[i], taken)
+    blocks, proj = [], []
     for b in range(QUART):
         place = jnp.where(col == at + b, 1.0, 0.0).astype(bf16)
         tile = dot(place, rows[:, V_AT:P_AT])
-        cols = slice(b * 1024, (b + 1) * 1024)
-        out_ref[:, cols] = jnp.where(taken >= 0, tile, val_ref[:, cols].astype(f32)).astype(bf16)
+        text = val_ref[:, b * RIM_W : (b + 1) * RIM_W].astype(f32)
+        blocks.append(jnp.where(taken >= 0, tile, text))
         tile = dot(place, rows[:, P_AT:S_AT])
-        cols = slice(b * 256, (b + 1) * 256)
-        out_ref[:, E + b * 256 : E + (b + 1) * 256] = jnp.where(
-            taken >= 0, tile, proj_ref[:, cols].astype(f32)
-        ).astype(bf16)
+        text = proj_ref[:, b * 256 : (b + 1) * 256].astype(f32)
+        proj.append(jnp.where(taken >= 0, tile, text))
+    blocks.append(jnp.concatenate(proj, axis=1))
+    out = blocks[0]
+    row = iota((EDGE, RIM_W), 0)
+    for i, block in enumerate(blocks):
+        out = jnp.where((row >= i * count) & (row < (i + 1) * count), pltpu.roll(block, (i + 1) * count, 0), out)
+    out_ref[...] = out.astype(bf16)
+
+
+def rim_rows(rim, block):
+    return pltpu.roll(rim, EDGE - (block + 1) * (KCONV - 1), 0)[EDGE - 8 :]
 
 
 def placement(at_ref):
@@ -363,8 +373,12 @@
     send_ref, conv_ref, proj_ref,
     full_scr,
 ):
+    rim = rim_ref[...].astype(f32)
+    befores = [rim_rows(rim, i) for i in range((E + PW) // RIM_W)]
+
     def conv(x_ref, at, columns):
-        before = rim_ref[EDGE - 8 :, columns].astype(f32)
+        i, low = columns.start // RIM_W, columns.start % RIM_W
+        before = befores[i][:, low : low + columns.stop - columns.start]
         return conv_chunk(x_ref[:, at].astype(f32), before, w_ref[:, columns], b_ref[:, columns])
 
     p = [conv(hp_ref, slice(k * LANES, (k + 1) * LANES), slice(E + k * LANES, E + (k + 1) * LANES)) for k in range(PW // LANES)]
@@ -397,8 +411,8 @@
         send_ref[low : low + 16, GW:] = side
 
 
-def scan_kernel(dev_ref, recv_ref, after_ref, out_ref, bound_ref, side_scr):
-    dev = dev_ref[0]
+def scan_kernel(recv_ref, after_ref, out_hbm, bound_ref, side_scr, out_ref, out_sem):
+    dev = lax.axis_index("ctx")
     side_scr[...] = dot(recv_ref[:, GW:], expander(dev // 8))
 
     def code(state, bound):
@@ -423,8 +437,16 @@
         )
 
     zeros = (jnp.zeros((8, GW), f32), jnp.zeros((1, GW), f32), jnp.zeros((1, LANES), f32))
-    own = lax.fori_loop(0, DEVS // 2, two, zeros, unroll=8)[2]
-    bound_ref[...] = jnp.broadcast_to(own, bound_ref.shape)
+    carry, stores = zeros, []
+    for part in range(4):
+        carry = lax.fori_loop(part * DEVS // 8, (part + 1) * DEVS // 8, two, carry, unroll=8)
+        rows = slice(part * DEVS * 2, (part + 1) * DEVS * 2)
+        store = pltpu.make_async_copy(out_ref.at[rows, :], out_hbm.at[rows, :], out_sem.at[part])
+        store.start()
+        stores.append(store)
+    bound_ref[...] = jnp.broadcast_to(carry[2], bound_ref.shape)
+    for store in stores:
+        store.wait()
 
 
 def local_kernel(
@@ -601,7 +623,6 @@
 ):
     device = lax.axis_index("ctx")
     scalar = pl.BlockSpec(memory_space=pltpu.SMEM)
-    dev = device.reshape(1).astype(jnp.int32)
 
     hbm = pl.BlockSpec(memory_space=pl.ANY)
     vmem = pl.BlockSpec(memory_space=pltpu.VMEM)
@@ -647,12 +668,12 @@
     at_spec = whole((1, 2 * DEVS))
     rim = call(
         rim_kernel,
-        struct(EDGE, E + PW),
+        struct(EDGE, RIM_W),
         (1,),
         [scalar, vmem,
          pl.BlockSpec((EDGE, E), lambda i: (TOK // EDGE - 1, 0)),
          pl.BlockSpec((EDGE, PW), lambda i: (TOK // EDGE - 1, 0))],
-        whole((EDGE, E + PW)),
+        whole((EDGE, RIM_W)),
         est=cost(2 * 16 * 48 * 5120, 3_000_000),
         name="rim",
     )(rim_slot, recv, far(text_values), far(text_proj))
@@ -724,12 +745,12 @@
         scan_kernel,
         (struct(G * N, GW), near(8, LANES, dtype=f32)),
         (1,),
-        [scalar, vmem, vmem],
-        [whole((G * N, GW)), vmem],
-        scratch=[pltpu.VMEM((G * N, GW), f32)],
+        [vmem, vmem],
+        [hbm, vmem],
+        scratch=[pltpu.VMEM((G * N, GW), f32), pltpu.VMEM((G * N, GW), bf16), sems((4,))],
         est=cost(2 * 512 * 512 * 128, 1_200_000),
         name="scan",
-    )(dev, states, kept(even[3]))
+    )(states, kept(even[3]))
     entry = kept(exchange(entries))
     odds = rows_own(1, (bound,))
 

time: 110 us -> 109 us (level)
  waiting for transfers between devices: 25 us -> 23.8 us
    all_to_all x4, waiting for transfers between devices: 25 us -> 23.8 us  [exchange(): return lax.all_to_all(rows, 'ctx', split_axis=0, concat_axis=0, tiled=True)]
where the time goes in v4:
time: 109 us
  Pallas kernels  43.5 us (40%)
  starting transfers between devices  35.9 us (33%)
  waiting for transfers between devices  23.8 us (22%)
  local copies, waits for them, and re-layouts  4.47 us (4%)
    all_to_all x4, starting transfers between devices, exchange(): return lax.all_to_all(rows, 'ctx', split_axis=0, concat_axis=0, tiled=True)  32.5 us
    all_to_all x4, waiting for transfers between devices, exchange(): return lax.all_to_all(rows, 'ctx', split_axis=0, concat_axis=0, tiled=True)  23.8 us
    pallas_call x2, Pallas kernels, rows_own(): call(functools.partial(local_kernel, odd), (struct(TOK, E // 2), struct(T...  15.6 us
    pallas_call x1, Pallas kernels, shards(): call(place_kernel, (struct(TOK, E), struct(G // 2, TOK, LANES), struct(G...  9.93 us
    pallas_call x1, Pallas kernels, shards(): call(final_kernel, struct(TOK, E), (1,), [vmem, vmem] + [hbm] * 7, hbm, s...  5.99 us
    ppermute x1, starting transfers between devices, shards(): rim = lax.ppermute(rim, 'ctx', [(i, i + 1) for i in range(DEVS - 1)])  3.46 us
    pallas_call x1, Pallas kernels, shards(): call(edge_kernel, (struct(G * N, STATE_W), struct(EDGE, E), struct(EDGE,...  3.17 us
    pallas_call x1, Pallas kernels, shards(): call(pack_kernel, struct(DEVS * 8, CHUNK), (1,), [hbm] * 4, hbm, scratch=...  2.8 us
  transfers between devices with their start and end apart: 5, of which 3 were waited for; matrix products, arithmetic and copies ran while one was open for 5% of the time, Pallas kernels for 30%

profile of v4, /device:TPU:0, one launch (start us, length us, event | category | flops | bytes accessed | tf_op | source)
XLA Modules:
  0.0 108.8 jit_solution(12919340972490559)
XLA Ops:
  0.0 0.0 copy-start
  0.0 2.8 %pack.1 = bf16[512,1408]{1,0:T(8,128)(2,1)} custom-call(s32[32,128]{1,0:T(8,128)} %bitcast.27, bf16[64,64]{1,0:T(8,128)(2,1)} %step_hbm.2, bf16[64,4096]{1,0:T(8,128)(2,1)} %val_hbm.2, bf16[64,1024]{1,0:T(8,128)(2,1)} %proj_hbm.2), custom_call_target="tpu_custom_call" | custom-call | flops 369098752 | bytes 3000000 | tf_op jit(solution)/shard_map/pack/pallas_call | solution.py:631
  2.8 0.0 copy-start.3
  2.8 11.5 %all-to-all-start = ((bf16[64,8,1408]{2,1,0:T(8,128)(2,1)}), bf16[64,8,1408]{2,1,0:T(8,128)(2,1)S(1)}, u32[]{:S(2)}, u32[]{:S(2)}) async-start(bf16[64,8,1408]{2,1,0:T(8,128)(2,1)} %bitcast.23), calls=%async_computation | async-start | bytes 2883584 | tf_op jit(solution)/shard_map/all_to_all | solution.py:613
  14.3 0.0 copy-start.2
  14.3 0.0 copy-done
  14.4 1.1 %eq.27 = pred[64,32,2]{2,1,0:T(8,128)(4,1)S(1)} reshape(pred[4096]{0:T(1024)(128)(4,1)S(1)} %shift-right-arithmetic_compare_fusion) | data formatting | bytes 8192 | tf_op jit(solution)/shard_map/eq | solution.py:645
  15.5 1.0 and.18
  16.5 0.0 copy-done.3
  16.6 0.4 select_reduce_fusion
  17.0 0.7 reshape.47.at_ref.at_hbm
  17.7 0.1 eq.28
  17.9 0.0 copy-done.2
  17.9 0.7 copy.23.step_ref.step_hbm
  18.6 0.2 select_reduce_fusion.1.slot_ref
  18.8 2.5 %gates.1 = bf16[512,1024]{1,0:T(8,128)(2,1)} custom-call(s32[32,128]{1,0:T(8,128)} %bitcast.28, bf16[64,4096]{1,0:T(8,128)(2,1)} %gate_ref.3, s32[1,128]{1,0:T(1,128)} %reshape.47.at_ref.at_hbm, bf16[256,64]{1,0:T(8,128)(2,1)} %copy.23.step_ref.step_hbm, s32[3]{0:T(128)S(1)} %select_reduce_fusion.1.slot_ref), custom_call_target="tpu_custom_call" | custom-call | flops 268435456 | bytes 2000000 | tf_op jit(solution)/shard_map/gates/pallas_call | solution.py:652
  21.3 15.8 %all-to-all-done = bf16[64,8,1408]{2,1,0:T(8,128)(2,1)S(1)} async-done(((bf16[64,8,1408]{2,1,0:T(8,128)(2,1)}), bf16[64,8,1408]{2,1,0:T(8,128)(2,1)S(1)}, u32[]{:S(2)}, u32[]{:S(2)}) %all-to-all-start) | async-done | bytes 1441824 | tf_op jit(solution)/shard_map/all_to_all | solution.py:613
  37.1 4.8 %all-to-all-start.1 = ((bf16[64,8,1024]{2,1,0:T(8,128)(2,1)}), bf16[64,8,1024]{2,1,0:T(8,128)(2,1)S(1)}, u32[]{:S(2)}, u32[]{:S(2)}) async-start(bf16[64,8,1024]{2,1,0:T(8,128)(2,1)} %bitcast.24), calls=%async_computation.1 | async-start | bytes 2097152 | tf_op jit(solution)/shard_map/all_to_all | solution.py:613
  41.9 1.7 %rim.1 = bf16[16,1024]{1,0:T(8,128)(2,1)} custom-call(s32[3]{0:T(128)S(1)} %select_reduce_fusion.1.slot_ref, bf16[512,1408]{1,0:T(8,128)(2,1)S(1)} %bitcast.17, bf16[256,4096]{1,0:T(8,128)(2,1)} %val_hbm.3, bf16[256,1024]{1,0:T(8,128)(2,1)} %proj_hbm.3), custom_call_target="tpu_custom_call" | custom-call | flops 7864320 | bytes 3000000 | tf_op jit(solution)/shard_map/rim/pallas_call | solution.py:669
  43.7 3.5 %collective-permute-start = (bf16[16,1024]{1,0:T(8,128)(2,1)}, bf16[16,1024]{1,0:T(8,128)(2,1)S(1)}, u32[]{:S(2)}, u32[]{:S(2)}) collective-permute-start(bf16[16,1024]{1,0:T(8,128)(2,1)} %rim.1), channel_id=1, source_target_pairs={{0,1},{1,2},{2,3},{3,4},{4,5},{5,6},{6,7},{7,8},{8,9},{9,10},{10,1... | collective-permute-start | bytes 98312 | tf_op jit(solution)/shard_map/ppermute | solution.py:680
  47.1 9.9 %place.1 = (bf16[256,4096]{1,0:T(8,128)(2,1)}, bf16[4,256,128]{2,1,0:T(8,128)(2,1)}, bf16[4,256,128]{2,1,0:T(8,128)(2,1)}, f32[512,512]{1,0:T(8,128)S(1)}, f32[2...) custom-call(bf16[512,1408]{1,0:T(8,128)(2,1)S(1)} %bitcast.18, ...), custom_call_target="tpu_custom_call" | custom-call | flops 1342177280 | bytes 10000000 | tf_op jit(solution)/shard_map/place/pallas_call | solution.py:682
  57.1 0.0 copy-start.1
  57.1 0.0 collective-permute-done.rim_ref
  57.1 3.2 %edge.1 = (bf16[512,640]{1,0:T(8,128)(2,1)}, bf16[16,4096]{1,0:T(8,128)(2,1)}, bf16[16,1024]{1,0:T(8,128)(2,1)}) custom-call(bf16[16,1024]{1,0:T(8,128)(2,1)S(1)} %collective-permute-done.rim_ref, bf16[16,4096]{1,0:T(8,128)(2,1)S(1)} %get-tuple-element.32.hv_ref, bf16[16,1024]{1,0:T(8,128)(2,1)S(1)} %get-tuple-element.33.hp_ref, f32[4,5120]{1,0:T(4,128)} %w_ref.1, ...), custom_call_target="tpu_custom_call" | custom-call | flops 8388608 | bytes 2000000 | tf_op jit(solution)/shard_map/edge/pallas_call | solution.py:706
  60.3 0.0 all-to-all-done.1
  60.3 10.1 %all-to-all-start.2 = ((bf16[64,8,640]{2,1,0:T(8,128)(2,1)}), bf16[64,8,640]{2,1,0:T(8,128)(2,1)S(1)}, u32[]{:S(2)}, u32[]{:S(2)}) async-start(bf16[64,8,640]{2,1,0:T(8,128)(2,1)} %bitcast.25), calls=%async_computation.2 | async-start | bytes 1310720 | tf_op jit(solution)/shard_map/all_to_all | solution.py:613
  70.4 0.0 copy-done.1
  70.4 0.7 copy.25
  71.1 7.8 %local0.1 = (bf16[256,2048]{1,0:T(8,128)(2,1)}, bf16[256,2048]{1,0:T(8,128)(2,1)}, bf16[4,256,64]{2,1,0:T(8,128)(2,1)}, f32[8,128]{1,0:T(8,128)S(1)}) custom-call(bf16[512,1024]{1,0:T(8,128)(2,1)S(1)} %bitcast.21, s32[1,128]{1,0:T(1,128)} %reshape.47.at_ref.at_hbm, bf16[256,4096]{1,0:T(8,128)(2,1)} %gate_ref.5, ...), custom_call_target="tpu_custom_call" | custom-call | flops 6000000000 | bytes 8000000 | tf_op jit(solution)/shard_map/local0/pallas_call | solution.py:726
  79.0 4.1 %all-to-all-done.2 = bf16[64,8,640]{2,1,0:T(8,128)(2,1)S(1)} async-done(((bf16[64,8,640]{2,1,0:T(8,128)(2,1)}), bf16[64,8,640]{2,1,0:T(8,128)(2,1)S(1)}, u32[]{:S(2)}, u32[]{:S(2)}) %all-to-all-start.2) | async-done | bytes 655392 | tf_op jit(solution)/shard_map/all_to_all | solution.py:613
  83.1 1.8 %scan.1 = (bf16[512,512]{1,0:T(8,128)(2,1)}, f32[8,128]{1,0:T(8,128)S(1)}) custom-call(bf16[512,640]{1,0:T(8,128)(2,1)S(1)} %bitcast.19, f32[8,128]{1,0:T(8,128)S(1)} %get-tuple-element.48.after_ref), custom_call_target="tpu_custom_call" | custom-call | flops 67108864 | bytes 1200000 | tf_op jit(solution)/shard_map/scan/pallas_call | solution.py:744
  84.9 6.1 %all-to-all-start.3 = ((bf16[64,8,512]{2,1,0:T(8,128)(2,1)}), bf16[64,8,512]{2,1,0:T(8,128)(2,1)S(1)}, u32[]{:S(2)}, u32[]{:S(2)}) async-start(bf16[64,8,512]{2,1,0:T(8,128)(2,1)} %bitcast.26), calls=%async_computation.3 | async-start | bytes 1048576 | tf_op jit(solution)/shard_map/all_to_all | solution.py:613
  91.0 7.8 %local1.1 = (bf16[256,2048]{1,0:T(8,128)(2,1)}, bf16[256,2048]{1,0:T(8,128)(2,1)}, bf16[4,256,64]{2,1,0:T(8,128)(2,1)}, f32[8,128]{1,0:T(8,128)}) custom-call(bf16[512,1024]{1,0:T(8,128)(2,1)S(1)} %bitcast.22, s32[1,128]{1,0:T(1,128)} %reshape.47.at_ref.at_hbm, bf16[256,4096]{1,0:T(8,128)(2,1)} %gate_ref.5, bf16[256,4096]{1,0:T(8,128)(2,1)} %get-tuple-element.41.conv_ref, ...), custom_call_target="tpu_custom_call" | custom-call | flops 6000000000 | bytes 8000000 | tf_op jit(solution)/shard_map/local1/pallas_call | solution.py:726
  98.7 3.9 %all-to-all-done.3 = bf16[64,8,512]{2,1,0:T(8,128)(2,1)S(1)} async-done(((bf16[64,8,512]{2,1,0:T(8,128)(2,1)}), bf16[64,8,512]{2,1,0:T(8,128)(2,1)S(1)}, u32[]{:S(2)}, u32[]{:S(2)}) %all-to-all-start.3) | async-done | bytes 524320 | tf_op jit(solution)/shard_map/all_to_all | solution.py:613
  102.7 6.0 %final.1 = bf16[256,4096]{1,0:T(8,128)(2,1)} custom-call(f32[8,128]{1,0:T(8,128)S(1)} %get-tuple-element.49.rest_0_.bound_ref, bf16[512,512]{1,0:T(8,128)(2,1)S(1)} %bitcast.20, f32[1,4096]{1,0:T(1,128)} %bitcast.33, bf16[4,256,64]{2,1,0:T(8,128)(2,1)} %get-tuple-element.51.qe_hbm, bf16[4,256,64]{2,1,0:T(8,128)(2,1)} %get-tuple-element.52.qo_hbm, ...), custom_call_target="tpu_custom_call" | custom-call | flops 134217728 | bytes 11000000 | tf_op jit(solution)/shard_map/final/pallas_call | solution.py:757
  (5 shorter events, 0.0 us)
Async XLA Ops:
  0.0 14.4 %copy-start = (s32[4096]{0:T(1024)S(1)}, s32[4096]{0:T(1024)}, u32[]{:S(2)}) copy-start(s32[4096]{0:T(1024)} %param.24) | copy-start | bytes 49156
  2.8 13.7 %copy-start.3 = (s32[64]{0:T(128)S(1)}, s32[64]{0:T(128)}, u32[]{:S(2)}) copy-start(s32[64]{0:T(128)} %param.25) | copy-start | bytes 772
  2.8 34.3 %all-to-all-start = ((bf16[64,8,1408]{2,1,0:T(8,128)(2,1)}), bf16[64,8,1408]{2,1,0:T(8,128)(2,1)S(1)}, u32[]{:S(2)}, u32[]{:S(2)}) async-start(bf16[64,8,1408]{2,1,0:T(8,128)(2,1)} %bitcast.23), calls=%async_computation | async-start | bytes 2883584 | tf_op jit(solution)/shard_map/all_to_all | solution.py:613
  14.3 3.5 %copy-start.2 = (bf16[256,64]{0,1:T(8,128)(2,1)S(1)}, bf16[256,64]{0,1:T(8,128)(2,1)}, u32[]{:S(2)}) copy-start(bf16[256,64]{0,1:T(8,128)(2,1)} %param.19) | copy-start | bytes 98308
  37.1 23.1 %all-to-all-start.1 = ((bf16[64,8,1024]{2,1,0:T(8,128)(2,1)}), bf16[64,8,1024]{2,1,0:T(8,128)(2,1)S(1)}, u32[]{:S(2)}, u32[]{:S(2)}) async-start(bf16[64,8,1024]{2,1,0:T(8,128)(2,1)} %bitcast.24), calls=%async_computation.1 | async-start | bytes 2097152 | tf_op jit(solution)/shard_map/all_to_all | solution.py:613
  43.7 13.4 %collective-permute-start = (bf16[16,1024]{1,0:T(8,128)(2,1)}, bf16[16,1024]{1,0:T(8,128)(2,1)S(1)}, u32[]{:S(2)}, u32[]{:S(2)}) collective-permute-start(bf16[16,1024]{1,0:T(8,128)(2,1)} %rim.1), channel_id=1, source_target_pairs={{0,1},{1,2},{2,3},{3,4},{4,5},{5,6},{6,7},{7,8},{8,9},{9,10},{10,1... | collective-permute-start | bytes 98312 | tf_op jit(solution)/shard_map/ppermute | solution.py:680
  57.1 13.3 %copy-start.1 = (f32[256,128]{1,0:T(8,128)S(1)}, f32[256,128]{1,0:T(8,128)}, u32[]{:S(2)}) copy-start(f32[256,128]{1,0:T(8,128)} %get-tuple-element.46.cum_ref) | copy-start | bytes 393220
  60.3 22.8 %all-to-all-start.2 = ((bf16[64,8,640]{2,1,0:T(8,128)(2,1)}), bf16[64,8,640]{2,1,0:T(8,128)(2,1)S(1)}, u32[]{:S(2)}, u32[]{:S(2)}) async-start(bf16[64,8,640]{2,1,0:T(8,128)(2,1)} %bitcast.25), calls=%async_computation.2 | async-start | bytes 1310720 | tf_op jit(solution)/shard_map/all_to_all | solution.py:613
  84.9 17.8 %all-to-all-start.3 = ((bf16[64,8,512]{2,1,0:T(8,128)(2,1)}), bf16[64,8,512]{2,1,0:T(8,128)(2,1)S(1)}, u32[]{:S(2)}, u32[]{:S(2)}) async-start(bf16[64,8,512]{2,1,0:T(8,128)(2,1)} %bitcast.26), calls=%async_computation.3 | async-start | bytes 1048576 | tf_op jit(solution)/shard_map/all_to_all | solution.py:613

commit v5 on v4

--- a/solution.py
+++ b/solution.py
@@ -217,7 +217,7 @@
 
 def place_kernel(
     recv_hbm, val_hbm, proj_hbm, at_hbm, step_hbm, w_hbm, b_hbm, sbias_hbm, dlog_hbm,
-    conv_hbm, in_hbm, out_hbm, state_ref, cum_ref, size_ref, total_ref, hv_ref, hp_ref, we_ref,
+    conv_hbm, in_hbm, out_hbm, state_ref, cum_ref, size_ref, total_ref, hv_ref, hp_ref, we_ref, wk_ref, bk_ref,
     at_ref, step_ref, w_ref, b_ref, sbias_ref, dlog_ref,
     recv_ref, val_ref, proj_ref, conv_ref, in_ref, out_ref, place_scr, taken_scr, wide_scr, tail_scr,
     tile_scr, weight_scr, part_scr, small_sem, recv_sem, val_sem, proj_sem, conv_sem, bc_sem,
@@ -261,6 +261,8 @@
         taken_scr[...] = dot(place_scr[...], jnp.ones((LANES, LANES), bf16))
         for load_small in small[1:]:
             load_small.wait()
+        wk_ref[...] = w_ref[...]
+        bk_ref[...] = b_ref[...]
         pieces[0].wait()
         spread_out(recv_ref[:, P_AT:], wide_scr)
         load_proj.wait()
@@ -679,17 +681,18 @@
     )(rim_slot, recv, far(text_values), far(text_proj))
     rim = lax.ppermute(rim, "ctx", [(i, i + 1) for i in range(DEVS - 1)])
 
-    conv, inputs, outputs, state, cum, size, total, head_v, head_p, tail = call(
+    conv, inputs, outputs, state, cum, size, total, head_v, head_p, tail, taps, shift = call(
         place_kernel,
         (
             struct(TOK, E), struct(G // 2, TOK, LANES), struct(G // 2, TOK, LANES), near(G * N, GW, dtype=f32),
             struct(TOK, LANES, dtype=f32), struct(TOK, LANES, dtype=f32),
             near(8, LANES, dtype=f32),
             near(EDGE, E), near(EDGE, PW), near(EDGE, E, dtype=f32),
+            near(KCONV, E + PW, dtype=f32), near(1, E + PW, dtype=f32),
         ),
         (1,),
         [hbm] * 9,
-        [hbm, hbm, hbm, vmem, whole((TOK, LANES)), whole((TOK, LANES)), vmem, vmem, vmem, vmem],
+        [hbm, hbm, hbm, vmem, whole((TOK, LANES)), whole((TOK, LANES)), vmem, vmem, vmem, vmem, vmem, vmem],
         scratch=[pltpu.VMEM((1, 2 * DEVS), jnp.int32), pltpu.VMEM((TOK, H), bf16), pltpu.VMEM((KCONV, E + PW), f32),
                  pltpu.VMEM((1, E + PW), f32), pltpu.VMEM((1, H), f32), pltpu.VMEM((1, H), f32),
                  pltpu.VMEM((DEVS * 8, CHUNK), bf16), pltpu.VMEM((TOK, E), bf16), pltpu.VMEM((TOK, PW), bf16),
@@ -707,12 +710,12 @@
         edge_kernel,
         (struct(G * N, STATE_W), struct(EDGE, E), struct(EDGE, PW)),
         (1,),
-        [vmem, vmem, vmem, whole((KCONV, E + PW)), whole((1, E + PW)), vmem, vmem, vmem],
+        [vmem] * 8,
         [whole((G * N, STATE_W)), whole((EDGE, E)), whole((EDGE, PW))],
         scratch=[pltpu.VMEM((G * N, GW), f32)],
         est=cost(2 * 64 * 16 * 4096, 2_000_000, 100_000),
         name="edge",
-    )(kept(rim), kept(head_v), kept(head_p), far(conv_weight), far(bias), kept(tail), kept(total), kept(state))
+    )(kept(rim), kept(head_v), kept(head_p), kept(taps), kept(shift), kept(tail), kept(total), kept(state))
     send, recv_gate = lax.optimization_barrier((send, recv_gate))
     states = kept(exchange(send))
 

time: 109 us -> 108 us (level)
  transfers between devices with their start and end apart: 5 -> 5, of which waited for: 3 -> 4; matrix products, arithmetic and copies ran while one was open for 5% -> 5% of each run, Pallas kernels for 30% -> 30%
where the time goes in v5:
time: 108 us
  Pallas kernels  42.6 us (39%)
  starting transfers between devices  35.7 us (33%)
  waiting for transfers between devices  24.1 us (22%)
  local copies, waits for them, and re-layouts  4.47 us (4%)
    all_to_all x4, starting transfers between devices, exchange(): return lax.all_to_all(rows, 'ctx', split_axis=0, concat_axis=0, tiled=True)  32.2 us
    all_to_all x4, waiting for transfers between devices, exchange(): return lax.all_to_all(rows, 'ctx', split_axis=0, concat_axis=0, tiled=True)  24.1 us
    pallas_call x2, Pallas kernels, rows_own(): call(functools.partial(local_kernel, odd), (struct(TOK, E // 2), struct(T...  15.6 us
    pallas_call x1, Pallas kernels, shards(): call(place_kernel, (struct(TOK, E), struct(G // 2, TOK, LANES), struct(G...  9.91 us
    pallas_call x1, Pallas kernels, shards(): call(final_kernel, struct(TOK, E), (1,), [vmem, vmem] + [hbm] * 7, hbm, s...  5.99 us
    ppermute x1, starting transfers between devices, shards(): rim = lax.ppermute(rim, 'ctx', [(i, i + 1) for i in range(DEVS - 1)])  3.46 us
    pallas_call x1, Pallas kernels, shards(): call(pack_kernel, struct(DEVS * 8, CHUNK), (1,), [hbm] * 4, hbm, scratch=...  2.8 us
    pallas_call x1, Pallas kernels, shards(): call(gate_kernel, struct(DEVS * 8, G_CHUNK), (1,), [whole((32, LANES)), w...  2.53 us
  transfers between devices with their start and end apart: 5, of which 4 were waited for; matrix products, arithmetic and copies ran while one was open for 5% of the time, Pallas kernels for 30%

profile of v5, /device:TPU:0, one launch (start us, length us, event | category | flops | bytes accessed | tf_op | source)
XLA Modules:
  0.0 107.9 jit_solution(14434788341113382677)
XLA Ops:
  0.0 0.0 copy-start
  0.0 2.8 %pack.1 = bf16[512,1408]{1,0:T(8,128)(2,1)} custom-call(s32[32,128]{1,0:T(8,128)} %bitcast.27, bf16[64,64]{1,0:T(8,128)(2,1)} %step_hbm.2, bf16[64,4096]{1,0:T(8,128)(2,1)} %val_hbm.2, bf16[64,1024]{1,0:T(8,128)(2,1)} %proj_hbm.2), custom_call_target="tpu_custom_call" | custom-call | flops 369098752 | bytes 3000000 | tf_op jit(solution)/shard_map/pack/pallas_call | solution.py:633
  2.8 0.0 copy-start.3
  2.8 11.5 %all-to-all-start = ((bf16[64,8,1408]{2,1,0:T(8,128)(2,1)}), bf16[64,8,1408]{2,1,0:T(8,128)(2,1)S(1)}, u32[]{:S(2)}, u32[]{:S(2)}) async-start(bf16[64,8,1408]{2,1,0:T(8,128)(2,1)} %bitcast.23), calls=%async_computation | async-start | bytes 2883584 | tf_op jit(solution)/shard_map/all_to_all | solution.py:615
  14.3 0.0 copy-start.2
  14.3 0.0 copy-done
  14.4 1.1 %eq.27 = pred[64,32,2]{2,1,0:T(8,128)(4,1)S(1)} reshape(pred[4096]{0:T(1024)(128)(4,1)S(1)} %shift-right-arithmetic_compare_fusion) | data formatting | bytes 8192 | tf_op jit(solution)/shard_map/eq | solution.py:647
  15.5 1.0 and.18
  16.5 0.0 copy-done.3
  16.6 0.4 select_reduce_fusion
  17.0 0.7 reshape.47.at_ref.at_hbm
  17.7 0.1 eq.28
  17.9 0.0 copy-done.2
  17.9 0.7 copy.23.step_ref.step_hbm
  18.6 0.2 select_reduce_fusion.1.slot_ref
  18.8 2.5 %gates.1 = bf16[512,1024]{1,0:T(8,128)(2,1)} custom-call(s32[32,128]{1,0:T(8,128)} %bitcast.28, bf16[64,4096]{1,0:T(8,128)(2,1)} %gate_ref.3, s32[1,128]{1,0:T(1,128)} %reshape.47.at_ref.at_hbm, bf16[256,64]{1,0:T(8,128)(2,1)} %copy.23.step_ref.step_hbm, s32[3]{0:T(128)S(1)} %select_reduce_fusion.1.slot_ref), custom_call_target="tpu_custom_call" | custom-call | flops 268435456 | bytes 2000000 | tf_op jit(solution)/shard_map/gates/pallas_call | solution.py:654
  21.3 15.8 %all-to-all-done = bf16[64,8,1408]{2,1,0:T(8,128)(2,1)S(1)} async-done(((bf16[64,8,1408]{2,1,0:T(8,128)(2,1)}), bf16[64,8,1408]{2,1,0:T(8,128)(2,1)S(1)}, u32[]{:S(2)}, u32[]{:S(2)}) %all-to-all-start) | async-done | bytes 1441824 | tf_op jit(solution)/shard_map/all_to_all | solution.py:615
  37.1 4.8 %all-to-all-start.1 = ((bf16[64,8,1024]{2,1,0:T(8,128)(2,1)}), bf16[64,8,1024]{2,1,0:T(8,128)(2,1)S(1)}, u32[]{:S(2)}, u32[]{:S(2)}) async-start(bf16[64,8,1024]{2,1,0:T(8,128)(2,1)} %bitcast.24), calls=%async_computation.1 | async-start | bytes 2097152 | tf_op jit(solution)/shard_map/all_to_all | solution.py:615
  41.9 1.7 %rim.1 = bf16[16,1024]{1,0:T(8,128)(2,1)} custom-call(s32[3]{0:T(128)S(1)} %select_reduce_fusion.1.slot_ref, bf16[512,1408]{1,0:T(8,128)(2,1)S(1)} %bitcast.17, bf16[256,4096]{1,0:T(8,128)(2,1)} %val_hbm.3, bf16[256,1024]{1,0:T(8,128)(2,1)} %proj_hbm.3), custom_call_target="tpu_custom_call" | custom-call | flops 7864320 | bytes 3000000 | tf_op jit(solution)/shard_map/rim/pallas_call | solution.py:671
  43.7 3.5 %collective-permute-start = (bf16[16,1024]{1,0:T(8,128)(2,1)}, bf16[16,1024]{1,0:T(8,128)(2,1)S(1)}, u32[]{:S(2)}, u32[]{:S(2)}) collective-permute-start(bf16[16,1024]{1,0:T(8,128)(2,1)} %rim.1), channel_id=1, source_target_pairs={{0,1},{1,2},{2,3},{3,4},{4,5},{5,6},{6,7},{7,8},{8,9},{9,10},{10,1... | collective-permute-start | bytes 98312 | tf_op jit(solution)/shard_map/ppermute | solution.py:682
  47.1 9.9 %place.1 = (bf16[256,4096]{1,0:T(8,128)(2,1)}, bf16[4,256,128]{2,1,0:T(8,128)(2,1)}, bf16[4,256,128]{2,1,0:T(8,128)(2,1)}, f32[512,512]{1,0:T(8,128)S(1)}, f32[2...) custom-call(bf16[512,1408]{1,0:T(8,128)(2,1)S(1)} %bitcast.18, ...), custom_call_target="tpu_custom_call" | custom-call | flops 1342177280 | bytes 10000000 | tf_op jit(solution)/shard_map/place/pallas_call | solution.py:684
  57.1 0.0 copy-start.1
  57.1 0.0 collective-permute-done.rim_ref
  57.1 2.2 %edge.1 = (bf16[512,640]{1,0:T(8,128)(2,1)}, bf16[16,4096]{1,0:T(8,128)(2,1)}, bf16[16,1024]{1,0:T(8,128)(2,1)}) custom-call(bf16[16,1024]{1,0:T(8,128)(2,1)S(1)} %collective-permute-done.rim_ref, bf16[16,4096]{1,0:T(8,128)(2,1)S(1)} %get-tuple-element.34.hv_ref, bf16[16,1024]{1,0:T(8,128)(2,1)S(1)} %get-tuple-element.35.hp_ref, ...), custom_call_target="tpu_custom_call" | custom-call | flops 8388608 | bytes 2000000 | tf_op jit(solution)/shard_map/edge/pallas_call | solution.py:709
  59.3 0.3 all-to-all-done.1
  59.6 9.8 %all-to-all-start.2 = ((bf16[64,8,640]{2,1,0:T(8,128)(2,1)}), bf16[64,8,640]{2,1,0:T(8,128)(2,1)S(1)}, u32[]{:S(2)}, u32[]{:S(2)}) async-start(bf16[64,8,640]{2,1,0:T(8,128)(2,1)} %bitcast.25), calls=%async_computation.2 | async-start | bytes 1310720 | tf_op jit(solution)/shard_map/all_to_all | solution.py:615
  69.5 0.0 copy-done.1
  69.5 0.7 copy.25
  70.2 7.8 %local0.1 = (bf16[256,2048]{1,0:T(8,128)(2,1)}, bf16[256,2048]{1,0:T(8,128)(2,1)}, bf16[4,256,64]{2,1,0:T(8,128)(2,1)}, f32[8,128]{1,0:T(8,128)S(1)}) custom-call(bf16[512,1024]{1,0:T(8,128)(2,1)S(1)} %bitcast.21, s32[1,128]{1,0:T(1,128)} %reshape.47.at_ref.at_hbm, bf16[256,4096]{1,0:T(8,128)(2,1)} %gate_ref.5, ...), custom_call_target="tpu_custom_call" | custom-call | flops 6000000000 | bytes 8000000 | tf_op jit(solution)/shard_map/local0/pallas_call | solution.py:729
  78.0 4.1 %all-to-all-done.2 = bf16[64,8,640]{2,1,0:T(8,128)(2,1)S(1)} async-done(((bf16[64,8,640]{2,1,0:T(8,128)(2,1)}), bf16[64,8,640]{2,1,0:T(8,128)(2,1)S(1)}, u32[]{:S(2)}, u32[]{:S(2)}) %all-to-all-start.2) | async-done | bytes 655392 | tf_op jit(solution)/shard_map/all_to_all | solution.py:615
  82.1 1.8 %scan.1 = (bf16[512,512]{1,0:T(8,128)(2,1)}, f32[8,128]{1,0:T(8,128)S(1)}) custom-call(bf16[512,640]{1,0:T(8,128)(2,1)S(1)} %bitcast.19, f32[8,128]{1,0:T(8,128)S(1)} %get-tuple-element.52.after_ref), custom_call_target="tpu_custom_call" | custom-call | flops 67108864 | bytes 1200000 | tf_op jit(solution)/shard_map/scan/pallas_call | solution.py:747
  83.9 6.1 %all-to-all-start.3 = ((bf16[64,8,512]{2,1,0:T(8,128)(2,1)}), bf16[64,8,512]{2,1,0:T(8,128)(2,1)S(1)}, u32[]{:S(2)}, u32[]{:S(2)}) async-start(bf16[64,8,512]{2,1,0:T(8,128)(2,1)} %bitcast.26), calls=%async_computation.3 | async-start | bytes 1048576 | tf_op jit(solution)/shard_map/all_to_all | solution.py:615
  90.0 7.8 %local1.1 = (bf16[256,2048]{1,0:T(8,128)(2,1)}, bf16[256,2048]{1,0:T(8,128)(2,1)}, bf16[4,256,64]{2,1,0:T(8,128)(2,1)}, f32[8,128]{1,0:T(8,128)}) custom-call(bf16[512,1024]{1,0:T(8,128)(2,1)S(1)} %bitcast.22, s32[1,128]{1,0:T(1,128)} %reshape.47.at_ref.at_hbm, bf16[256,4096]{1,0:T(8,128)(2,1)} %gate_ref.5, bf16[256,4096]{1,0:T(8,128)(2,1)} %get-tuple-element.45.conv_ref, ...), custom_call_target="tpu_custom_call" | custom-call | flops 6000000000 | bytes 8000000 | tf_op jit(solution)/shard_map/local1/pallas_call | solution.py:729
  97.8 3.9 %all-to-all-done.3 = bf16[64,8,512]{2,1,0:T(8,128)(2,1)S(1)} async-done(((bf16[64,8,512]{2,1,0:T(8,128)(2,1)}), bf16[64,8,512]{2,1,0:T(8,128)(2,1)S(1)}, u32[]{:S(2)}, u32[]{:S(2)}) %all-to-all-start.3) | async-done | bytes 524320 | tf_op jit(solution)/shard_map/all_to_all | solution.py:615
  101.7 6.0 %final.1 = bf16[256,4096]{1,0:T(8,128)(2,1)} custom-call(f32[8,128]{1,0:T(8,128)S(1)} %get-tuple-element.53.rest_0_.bound_ref, bf16[512,512]{1,0:T(8,128)(2,1)S(1)} %bitcast.20, f32[1,4096]{1,0:T(1,128)} %bitcast.31, bf16[4,256,64]{2,1,0:T(8,128)(2,1)} %get-tuple-element.55.qe_hbm, bf16[4,256,64]{2,1,0:T(8,128)(2,1)} %get-tuple-element.56.qo_hbm, ...), custom_call_target="tpu_custom_call" | custom-call | flops 134217728 | bytes 11000000 | tf_op jit(solution)/shard_map/final/pallas_call | solution.py:760
  (5 shorter events, 0.0 us)
Async XLA Ops:
  0.0 14.4 %copy-start = (s32[4096]{0:T(1024)S(1)}, s32[4096]{0:T(1024)}, u32[]{:S(2)}) copy-start(s32[4096]{0:T(1024)} %param.24) | copy-start | bytes 49156
  2.8 13.7 %copy-start.3 = (s32[64]{0:T(128)S(1)}, s32[64]{0:T(128)}, u32[]{:S(2)}) copy-start(s32[64]{0:T(128)} %param.25) | copy-start | bytes 772
  2.8 34.3 %all-to-all-start = ((bf16[64,8,1408]{2,1,0:T(8,128)(2,1)}), bf16[64,8,1408]{2,1,0:T(8,128)(2,1)S(1)}, u32[]{:S(2)}, u32[]{:S(2)}) async-start(bf16[64,8,1408]{2,1,0:T(8,128)(2,1)} %bitcast.23), calls=%async_computation | async-start | bytes 2883584 | tf_op jit(solution)/shard_map/all_to_all | solution.py:615
  14.3 3.5 %copy-start.2 = (bf16[256,64]{0,1:T(8,128)(2,1)S(1)}, bf16[256,64]{0,1:T(8,128)(2,1)}, u32[]{:S(2)}) copy-start(bf16[256,64]{0,1:T(8,128)(2,1)} %param.19) | copy-start | bytes 98308
  37.1 22.5 %all-to-all-start.1 = ((bf16[64,8,1024]{2,1,0:T(8,128)(2,1)}), bf16[64,8,1024]{2,1,0:T(8,128)(2,1)S(1)}, u32[]{:S(2)}, u32[]{:S(2)}) async-start(bf16[64,8,1024]{2,1,0:T(8,128)(2,1)} %bitcast.24), calls=%async_computation.1 | async-start | bytes 2097152 | tf_op jit(solution)/shard_map/all_to_all | solution.py:615
  43.7 13.4 %collective-permute-start = (bf16[16,1024]{1,0:T(8,128)(2,1)}, bf16[16,1024]{1,0:T(8,128)(2,1)S(1)}, u32[]{:S(2)}, u32[]{:S(2)}) collective-permute-start(bf16[16,1024]{1,0:T(8,128)(2,1)} %rim.1), channel_id=1, source_target_pairs={{0,1},{1,2},{2,3},{3,4},{4,5},{5,6},{6,7},{7,8},{8,9},{9,10},{10,1... | collective-permute-start | bytes 98312 | tf_op jit(solution)/shard_map/ppermute | solution.py:682
  57.1 12.4 %copy-start.1 = (f32[256,128]{1,0:T(8,128)S(1)}, f32[256,128]{1,0:T(8,128)}, u32[]{:S(2)}) copy-start(f32[256,128]{1,0:T(8,128)} %get-tuple-element.50.cum_ref) | copy-start | bytes 393220
  59.6 22.5 %all-to-all-start.2 = ((bf16[64,8,640]{2,1,0:T(8,128)(2,1)}), bf16[64,8,640]{2,1,0:T(8,128)(2,1)S(1)}, u32[]{:S(2)}, u32[]{:S(2)}) async-start(bf16[64,8,640]{2,1,0:T(8,128)(2,1)} %bitcast.25), calls=%async_computation.2 | async-start | bytes 1310720 | tf_op jit(solution)/shard_map/all_to_all | solution.py:615
  83.9 17.8 %all-to-all-start.3 = ((bf16[64,8,512]{2,1,0:T(8,128)(2,1)}), bf16[64,8,512]{2,1,0:T(8,128)(2,1)S(1)}, u32[]{:S(2)}, u32[]{:S(2)}) async-start(bf16[64,8,512]{2,1,0:T(8,128)(2,1)} %bitcast.26), calls=%async_computation.3 | async-start | bytes 1048576 | tf_op jit(solution)/shard_map/all_to_all | solution.py:615

commit v6 on v5

--- a/solution.py
+++ b/solution.py
@@ -220,7 +220,7 @@
     conv_hbm, in_hbm, out_hbm, state_ref, cum_ref, size_ref, total_ref, hv_ref, hp_ref, we_ref, wk_ref, bk_ref,
     at_ref, step_ref, w_ref, b_ref, sbias_ref, dlog_ref,
     recv_ref, val_ref, proj_ref, conv_ref, in_ref, out_ref, place_scr, taken_scr, wide_scr, tail_scr,
-    tile_scr, weight_scr, part_scr, small_sem, recv_sem, val_sem, proj_sem, conv_sem, bc_sem,
+    tile_scr, weight_scr, part_scr, turned_scr, small_sem, recv_sem, val_sem, proj_sem, conv_sem, bc_sem,
 ):
     def load(i):
         cols = group_cols(order(i))
@@ -287,6 +287,9 @@
                 )
         for copy in store_bc:
             copy.start()
+        for pair in range(G // 2):
+            turned = jnp.transpose(in_ref[pair].astype(f32))
+            turned_scr[pair] = jnp.where(iota((LANES, TOK), 1) >= EDGE, turned, 0.0).astype(bf16)
         steps = wide_scr[2, pl.ds(0, 2 * DEVS, stride=QUART), :].astype(bf16)
         tile = dot(place_scr[...], steps)
         step = step_ref[...].astype(f32)
@@ -343,8 +346,8 @@
             for slot in range(2):
                 pair = 2 * two + slot
                 rows = pl.ds(pl.multiple_of((2 * pair + odd) * N, N), N)
-                b_g = in_ref[pair, EDGE:, odd * N : (odd + 1) * N]
-                state_ref[rows, :] = dot_rows(b_g, part_scr[slot, EDGE:, :])
+                b_g = turned_scr[pair, odd * N : (odd + 1) * N, :]
+                state_ref[rows, :] = dot(b_g, part_scr[slot])
             for slot in range(2):
                 store(odd * (G // 2) + 2 * two + slot).start()
 
@@ -700,7 +703,7 @@
                  pltpu.VMEM((TOK, LANES), bf16), pltpu.VMEM((TOK, LANES), f32),
                  pltpu.VMEM((GW // LANES, DEVS * 8, LANES), f32), pltpu.VMEM((TOK, LANES), bf16),
                  pltpu.VMEM((2, TOK, GW), f32), pltpu.VMEM((2, TOK, GW), f32), pltpu.VMEM((2, TOK, GW), bf16),
-                 sems((6,)), sems((3,)), sems((G,)), sems(()), sems((G,)), sems((2,))],
+                 pltpu.VMEM((G // 2, LANES, TOK), bf16), sems((6,)), sems((3,)), sems((G,)), sems(()), sems((G,)), sems((2,))],
         est=cost(2 * 256 * 512 * 5120, 10_000_000, 1_300_000),
         name="place",
     )(recv, far(text_values), far(text_proj), at, steps, far(conv_weight), far(bias),

time: 108 us -> 109 us (level)
  no operation moved by 1% of the time
where the time goes in v6:
time: 109 us; the launch traced here: 108 us
  Pallas kernels  42.6 us (39%)
  starting transfers between devices  35.7 us (33%)
  waiting for transfers between devices  24.1 us (22%)
  local copies, waits for them, and re-layouts  4.47 us (4%)
    all_to_all x4, starting transfers between devices, exchange(): return lax.all_to_all(rows, 'ctx', split_axis=0, concat_axis=0, tiled=True)  32.2 us
    all_to_all x4, waiting for transfers between devices, exchange(): return lax.all_to_all(rows, 'ctx', split_axis=0, concat_axis=0, tiled=True)  24.1 us
    pallas_call x2, Pallas kernels, rows_own(): call(functools.partial(local_kernel, odd), (struct(TOK, E // 2), struct(T...  15.6 us
    pallas_call x1, Pallas kernels, shards(): call(place_kernel, (struct(TOK, E), struct(G // 2, TOK, LANES), struct(G...  9.94 us
    pallas_call x1, Pallas kernels, shards(): call(final_kernel, struct(TOK, E), (1,), [vmem, vmem] + [hbm] * 7, hbm, s...  5.99 us
    ppermute x1, starting transfers between devices, shards(): rim = lax.ppermute(rim, 'ctx', [(i, i + 1) for i in range(DEVS - 1)])  3.46 us
    pallas_call x1, Pallas kernels, shards(): call(pack_kernel, struct(DEVS * 8, CHUNK), (1,), [hbm] * 4, hbm, scratch=...  2.8 us
    pallas_call x1, Pallas kernels, shards(): call(gate_kernel, struct(DEVS * 8, G_CHUNK), (1,), [whole((32, LANES)), w...  2.53 us
  transfers between devices with their start and end apart: 5, of which 4 were waited for; matrix products, arithmetic and copies ran while one was open for 5% of the time, Pallas kernels for 30%

profile of v6, /device:TPU:0, one launch (start us, length us, event | category | flops | bytes accessed | tf_op | source)
XLA Modules:
  0.0 107.9 jit_solution(17826281129153096708)
XLA Ops:
  0.0 0.0 copy-start
  0.0 2.8 %pack.1 = bf16[512,1408]{1,0:T(8,128)(2,1)} custom-call(s32[32,128]{1,0:T(8,128)} %bitcast.27, bf16[64,64]{1,0:T(8,128)(2,1)} %step_hbm.2, bf16[64,4096]{1,0:T(8,128)(2,1)} %val_hbm.2, bf16[64,1024]{1,0:T(8,128)(2,1)} %proj_hbm.2), custom_call_target="tpu_custom_call" | custom-call | flops 369098752 | bytes 3000000 | tf_op jit(solution)/shard_map/pack/pallas_call | solution.py:636
  2.8 0.0 copy-start.3
  2.8 11.5 %all-to-all-start = ((bf16[64,8,1408]{2,1,0:T(8,128)(2,1)}), bf16[64,8,1408]{2,1,0:T(8,128)(2,1)S(1)}, u32[]{:S(2)}, u32[]{:S(2)}) async-start(bf16[64,8,1408]{2,1,0:T(8,128)(2,1)} %bitcast.23), calls=%async_computation | async-start | bytes 2883584 | tf_op jit(solution)/shard_map/all_to_all | solution.py:618
  14.3 0.0 copy-start.2
  14.3 0.0 copy-done
  14.4 1.1 %eq.27 = pred[64,32,2]{2,1,0:T(8,128)(4,1)S(1)} reshape(pred[4096]{0:T(1024)(128)(4,1)S(1)} %shift-right-arithmetic_compare_fusion) | data formatting | bytes 8192 | tf_op jit(solution)/shard_map/eq | solution.py:650
  15.5 1.0 and.18
  16.5 0.0 copy-done.3
  16.6 0.4 select_reduce_fusion
  17.0 0.7 reshape.47.at_ref.at_hbm
  17.7 0.1 eq.28
  17.9 0.0 copy-done.2
  17.9 0.7 copy.23.step_ref.step_hbm
  18.6 0.2 select_reduce_fusion.1.slot_ref
  18.8 2.5 %gates.1 = bf16[512,1024]{1,0:T(8,128)(2,1)} custom-call(s32[32,128]{1,0:T(8,128)} %bitcast.28, bf16[64,4096]{1,0:T(8,128)(2,1)} %gate_ref.3, s32[1,128]{1,0:T(1,128)} %reshape.47.at_ref.at_hbm, bf16[256,64]{1,0:T(8,128)(2,1)} %copy.23.step_ref.step_hbm, s32[3]{0:T(128)S(1)} %select_reduce_fusion.1.slot_ref), custom_call_target="tpu_custom_call" | custom-call | flops 268435456 | bytes 2000000 | tf_op jit(solution)/shard_map/gates/pallas_call | solution.py:657
  21.3 15.8 %all-to-all-done = bf16[64,8,1408]{2,1,0:T(8,128)(2,1)S(1)} async-done(((bf16[64,8,1408]{2,1,0:T(8,128)(2,1)}), bf16[64,8,1408]{2,1,0:T(8,128)(2,1)S(1)}, u32[]{:S(2)}, u32[]{:S(2)}) %all-to-all-start) | async-done | bytes 1441824 | tf_op jit(solution)/shard_map/all_to_all | solution.py:618
  37.1 4.8 %all-to-all-start.1 = ((bf16[64,8,1024]{2,1,0:T(8,128)(2,1)}), bf16[64,8,1024]{2,1,0:T(8,128)(2,1)S(1)}, u32[]{:S(2)}, u32[]{:S(2)}) async-start(bf16[64,8,1024]{2,1,0:T(8,128)(2,1)} %bitcast.24), calls=%async_computation.1 | async-start | bytes 2097152 | tf_op jit(solution)/shard_map/all_to_all | solution.py:618
  41.9 1.7 %rim.1 = bf16[16,1024]{1,0:T(8,128)(2,1)} custom-call(s32[3]{0:T(128)S(1)} %select_reduce_fusion.1.slot_ref, bf16[512,1408]{1,0:T(8,128)(2,1)S(1)} %bitcast.17, bf16[256,4096]{1,0:T(8,128)(2,1)} %val_hbm.3, bf16[256,1024]{1,0:T(8,128)(2,1)} %proj_hbm.3), custom_call_target="tpu_custom_call" | custom-call | flops 7864320 | bytes 3000000 | tf_op jit(solution)/shard_map/rim/pallas_call | solution.py:674
  43.7 3.5 %collective-permute-start = (bf16[16,1024]{1,0:T(8,128)(2,1)}, bf16[16,1024]{1,0:T(8,128)(2,1)S(1)}, u32[]{:S(2)}, u32[]{:S(2)}) collective-permute-start(bf16[16,1024]{1,0:T(8,128)(2,1)} %rim.1), channel_id=1, source_target_pairs={{0,1},{1,2},{2,3},{3,4},{4,5},{5,6},{6,7},{7,8},{8,9},{9,10},{10,1... | collective-permute-start | bytes 98312 | tf_op jit(solution)/shard_map/ppermute | solution.py:685
  47.1 9.9 %place.1 = (bf16[256,4096]{1,0:T(8,128)(2,1)}, bf16[4,256,128]{2,1,0:T(8,128)(2,1)}, bf16[4,256,128]{2,1,0:T(8,128)(2,1)}, f32[512,512]{1,0:T(8,128)S(1)}, f32[2...) custom-call(bf16[512,1408]{1,0:T(8,128)(2,1)S(1)} %bitcast.18, ...), custom_call_target="tpu_custom_call" | custom-call | flops 1342177280 | bytes 10000000 | tf_op jit(solution)/shard_map/place/pallas_call | solution.py:687
  57.1 0.0 copy-start.1
  57.1 0.0 collective-permute-done.rim_ref
  57.1 2.2 %edge.1 = (bf16[512,640]{1,0:T(8,128)(2,1)}, bf16[16,4096]{1,0:T(8,128)(2,1)}, bf16[16,1024]{1,0:T(8,128)(2,1)}) custom-call(bf16[16,1024]{1,0:T(8,128)(2,1)S(1)} %collective-permute-done.rim_ref, bf16[16,4096]{1,0:T(8,128)(2,1)S(1)} %get-tuple-element.34.hv_ref, bf16[16,1024]{1,0:T(8,128)(2,1)S(1)} %get-tuple-element.35.hp_ref, ...), custom_call_target="tpu_custom_call" | custom-call | flops 8388608 | bytes 2000000 | tf_op jit(solution)/shard_map/edge/pallas_call | solution.py:712
  59.3 0.3 all-to-all-done.1
  59.6 9.9 %all-to-all-start.2 = ((bf16[64,8,640]{2,1,0:T(8,128)(2,1)}), bf16[64,8,640]{2,1,0:T(8,128)(2,1)S(1)}, u32[]{:S(2)}, u32[]{:S(2)}) async-start(bf16[64,8,640]{2,1,0:T(8,128)(2,1)} %bitcast.25), calls=%async_computation.2 | async-start | bytes 1310720 | tf_op jit(solution)/shard_map/all_to_all | solution.py:618
  69.5 0.0 copy-done.1
  69.5 0.7 copy.25
  70.2 7.8 %local0.1 = (bf16[256,2048]{1,0:T(8,128)(2,1)}, bf16[256,2048]{1,0:T(8,128)(2,1)}, bf16[4,256,64]{2,1,0:T(8,128)(2,1)}, f32[8,128]{1,0:T(8,128)S(1)}) custom-call(bf16[512,1024]{1,0:T(8,128)(2,1)S(1)} %bitcast.21, s32[1,128]{1,0:T(1,128)} %reshape.47.at_ref.at_hbm, bf16[256,4096]{1,0:T(8,128)(2,1)} %gate_ref.5, ...), custom_call_target="tpu_custom_call" | custom-call | flops 6000000000 | bytes 8000000 | tf_op jit(solution)/shard_map/local0/pallas_call | solution.py:732
  78.0 4.1 %all-to-all-done.2 = bf16[64,8,640]{2,1,0:T(8,128)(2,1)S(1)} async-done(((bf16[64,8,640]{2,1,0:T(8,128)(2,1)}), bf16[64,8,640]{2,1,0:T(8,128)(2,1)S(1)}, u32[]{:S(2)}, u32[]{:S(2)}) %all-to-all-start.2) | async-done | bytes 655392 | tf_op jit(solution)/shard_map/all_to_all | solution.py:618
  82.1 1.8 %scan.1 = (bf16[512,512]{1,0:T(8,128)(2,1)}, f32[8,128]{1,0:T(8,128)S(1)}) custom-call(bf16[512,640]{1,0:T(8,128)(2,1)S(1)} %bitcast.19, f32[8,128]{1,0:T(8,128)S(1)} %get-tuple-element.52.after_ref), custom_call_target="tpu_custom_call" | custom-call | flops 67108864 | bytes 1200000 | tf_op jit(solution)/shard_map/scan/pallas_call | solution.py:750
  84.0 6.1 %all-to-all-start.3 = ((bf16[64,8,512]{2,1,0:T(8,128)(2,1)}), bf16[64,8,512]{2,1,0:T(8,128)(2,1)S(1)}, u32[]{:S(2)}, u32[]{:S(2)}) async-start(bf16[64,8,512]{2,1,0:T(8,128)(2,1)} %bitcast.26), calls=%async_computation.3 | async-start | bytes 1048576 | tf_op jit(solution)/shard_map/all_to_all | solution.py:618
  90.0 7.8 %local1.1 = (bf16[256,2048]{1,0:T(8,128)(2,1)}, bf16[256,2048]{1,0:T(8,128)(2,1)}, bf16[4,256,64]{2,1,0:T(8,128)(2,1)}, f32[8,128]{1,0:T(8,128)}) custom-call(bf16[512,1024]{1,0:T(8,128)(2,1)S(1)} %bitcast.22, s32[1,128]{1,0:T(1,128)} %reshape.47.at_ref.at_hbm, bf16[256,4096]{1,0:T(8,128)(2,1)} %gate_ref.5, bf16[256,4096]{1,0:T(8,128)(2,1)} %get-tuple-element.45.conv_ref, ...), custom_call_target="tpu_custom_call" | custom-call | flops 6000000000 | bytes 8000000 | tf_op jit(solution)/shard_map/local1/pallas_call | solution.py:732
  97.8 3.9 %all-to-all-done.3 = bf16[64,8,512]{2,1,0:T(8,128)(2,1)S(1)} async-done(((bf16[64,8,512]{2,1,0:T(8,128)(2,1)}), bf16[64,8,512]{2,1,0:T(8,128)(2,1)S(1)}, u32[]{:S(2)}, u32[]{:S(2)}) %all-to-all-start.3) | async-done | bytes 524320 | tf_op jit(solution)/shard_map/all_to_all | solution.py:618
  101.7 6.0 %final.1 = bf16[256,4096]{1,0:T(8,128)(2,1)} custom-call(f32[8,128]{1,0:T(8,128)S(1)} %get-tuple-element.53.rest_0_.bound_ref, bf16[512,512]{1,0:T(8,128)(2,1)S(1)} %bitcast.20, f32[1,4096]{1,0:T(1,128)} %bitcast.31, bf16[4,256,64]{2,1,0:T(8,128)(2,1)} %get-tuple-element.55.qe_hbm, bf16[4,256,64]{2,1,0:T(8,128)(2,1)} %get-tuple-element.56.qo_hbm, ...), custom_call_target="tpu_custom_call" | custom-call | flops 134217728 | bytes 11000000 | tf_op jit(solution)/shard_map/final/pallas_call | solution.py:763
  (5 shorter events, 0.0 us)
Async XLA Ops:
  0.0 14.4 %copy-start = (s32[4096]{0:T(1024)S(1)}, s32[4096]{0:T(1024)}, u32[]{:S(2)}) copy-start(s32[4096]{0:T(1024)} %param.24) | copy-start | bytes 49156
  2.8 13.7 %copy-start.3 = (s32[64]{0:T(128)S(1)}, s32[64]{0:T(128)}, u32[]{:S(2)}) copy-start(s32[64]{0:T(128)} %param.25) | copy-start | bytes 772
  2.8 34.3 %all-to-all-start = ((bf16[64,8,1408]{2,1,0:T(8,128)(2,1)}), bf16[64,8,1408]{2,1,0:T(8,128)(2,1)S(1)}, u32[]{:S(2)}, u32[]{:S(2)}) async-start(bf16[64,8,1408]{2,1,0:T(8,128)(2,1)} %bitcast.23), calls=%async_computation | async-start | bytes 2883584 | tf_op jit(solution)/shard_map/all_to_all | solution.py:618
  14.3 3.5 %copy-start.2 = (bf16[256,64]{0,1:T(8,128)(2,1)S(1)}, bf16[256,64]{0,1:T(8,128)(2,1)}, u32[]{:S(2)}) copy-start(bf16[256,64]{0,1:T(8,128)(2,1)} %param.19) | copy-start | bytes 98308
  37.1 22.5 %all-to-all-start.1 = ((bf16[64,8,1024]{2,1,0:T(8,128)(2,1)}), bf16[64,8,1024]{2,1,0:T(8,128)(2,1)S(1)}, u32[]{:S(2)}, u32[]{:S(2)}) async-start(bf16[64,8,1024]{2,1,0:T(8,128)(2,1)} %bitcast.24), calls=%async_computation.1 | async-start | bytes 2097152 | tf_op jit(solution)/shard_map/all_to_all | solution.py:618
  43.7 13.4 %collective-permute-start = (bf16[16,1024]{1,0:T(8,128)(2,1)}, bf16[16,1024]{1,0:T(8,128)(2,1)S(1)}, u32[]{:S(2)}, u32[]{:S(2)}) collective-permute-start(bf16[16,1024]{1,0:T(8,128)(2,1)} %rim.1), channel_id=1, source_target_pairs={{0,1},{1,2},{2,3},{3,4},{4,5},{5,6},{6,7},{7,8},{8,9},{9,10},{10,1... | collective-permute-start | bytes 98312 | tf_op jit(solution)/shard_map/ppermute | solution.py:685
  57.1 12.4 %copy-start.1 = (f32[256,128]{1,0:T(8,128)S(1)}, f32[256,128]{1,0:T(8,128)}, u32[]{:S(2)}) copy-start(f32[256,128]{1,0:T(8,128)} %get-tuple-element.50.cum_ref) | copy-start | bytes 393220
  59.6 22.5 %all-to-all-start.2 = ((bf16[64,8,640]{2,1,0:T(8,128)(2,1)}), bf16[64,8,640]{2,1,0:T(8,128)(2,1)S(1)}, u32[]{:S(2)}, u32[]{:S(2)}) async-start(bf16[64,8,640]{2,1,0:T(8,128)(2,1)} %bitcast.25), calls=%async_computation.2 | async-start | bytes 1310720 | tf_op jit(solution)/shard_map/all_to_all | solution.py:618
  84.0 17.8 %all-to-all-start.3 = ((bf16[64,8,512]{2,1,0:T(8,128)(2,1)}), bf16[64,8,512]{2,1,0:T(8,128)(2,1)S(1)}, u32[]{:S(2)}, u32[]{:S(2)}) async-start(bf16[64,8,512]{2,1,0:T(8,128)(2,1)} %bitcast.26), calls=%async_computation.3 | async-start | bytes 1048576 | tf_op jit(solution)/shard_map/all_to_all | solution.py:618
